TPU v7x, 32 devices: a whole 2x2x4 slice. The times are simulated.
32 devices in a mesh: tile: 8 (over z, x), dp: 4 (over y, core).
Axes of the slice: x: 2, y: 2, z: 4, core: 2. Of those that a mesh axis runs over, the one named last changes fastest.
Arguments:
- inputs: bfloat16 [4, 8, 32, 32, 128], P('dp', 'tile'), may hold values from -6 to 6
- weight_one: bfloat16 [9, 128, 128], replicated, may hold values from -0.1875 to 0.1875
- weight_two: bfloat16 [9, 128, 128], replicated, may hold values from -0.1875 to 0.1875
- cotangent: bfloat16 [4, 8, 32, 32, 128], P('dp', 'tile'), may hold values from -6 to 6
- edge_code: int32 [8, 4], replicated, may hold values from 0 to 7
- corner_code: int32 [8, 4], replicated, may hold values from 0 to 3
Outputs:
- output: bfloat16 [4, 8, 32, 32, 128], P('dp', 'tile')
- d_input: bfloat16 [4, 8, 32, 32, 128], P('dp', 'tile')
- grad_one: float32 [9, 128, 128], replicated
- grad_two: float32 [9, 128, 128], replicated
Inputs may be any that keep to these rules, and one draw needn't show every extreme that they name: edge_code[t, k]: which border of the neighbour across side k fills that margin side (code mod 4), reversed for codes 4 to 7. corner_code[t, q]: which corner pixel of diagonal neighbour q fills margin corner q.
All inputs are finite; a program needn't handle non-finite values.
Results may differ from a plain program's by a relative error of at most 0.0036.
Values may be sent and summed in bfloat16 or wider, within the bound.
No kernel may reach another device: no remote copies, remote signals or barrier semaphores. Data moves between devices by JAX's collectives and lax.ppermute only.
A program may use at most 64 MiB of HBM per device.

v0:
```python
from functools import partial
import math

import jax
import jax.numpy as jnp
from jax import lax
from jax.sharding import PartitionSpec as P

RW = 4


def from_behind(x, axis, by):
    count = lax.axis_size(axis)
    return lax.ppermute(x, axis, [(i, (i + by) % count) for i in range(count)])


def side_offsets():
    return (-RW, 1, RW, -1)


def corner_offsets():
    return (-RW - 1, -RW + 1, RW + 1, RW - 1)


def pad_halo(source, edge_code, corner_code):
    tiles = lax.axis_size("tile")
    mine = lax.axis_index("tile")
    extent = source.shape[1]
    borders = jnp.stack(
        [source[:, 0], source[:, :, extent - 1], source[:, extent - 1], source[:, :, 0]], axis=0
    )
    corners = jnp.stack(
        [
            source[:, 0, 0],
            source[:, 0, extent - 1],
            source[:, extent - 1, extent - 1],
            source[:, extent - 1, 0],
        ],
        axis=0,
    )
    strips = []
    for edge_index, offset in enumerate(side_offsets()):
        target = (mine - offset) % tiles
        code = edge_code[target, edge_index]
        chosen = lax.dynamic_index_in_dim(borders, code % 4, 0, keepdims=False)
        chosen = jnp.where(code >= 4, chosen[:, ::-1], chosen)
        strips.append(from_behind(chosen, "tile", -offset))
    picks = []
    for corner_index, offset in enumerate(corner_offsets()):
        target = (mine - offset) % tiles
        code = corner_code[target, corner_index]
        chosen = lax.dynamic_index_in_dim(corners, code, 0, keepdims=False)
        picks.append(from_behind(chosen, "tile", -offset))
    top_row = jnp.concatenate([picks[0][:, None], strips[0], picks[1][:, None]], axis=1)
    bottom_row = jnp.concatenate([picks[3][:, None], strips[2], picks[2][:, None]], axis=1)
    middle = jnp.concatenate([strips[3][:, :, None], source, strips[1][:, :, None]], axis=2)
    return jnp.concatenate([top_row[:, None], middle, bottom_row[:, None]], axis=1)


def convolve(padded, weights):
    extent = padded.shape[1] - 2
    members = padded.shape[0]
    channels = padded.shape[-1]
    total = jnp.zeros((members * extent * extent, weights.shape[2]), jnp.float32)
    for row_tap in range(3):
        for col_tap in range(3):
            piece = padded[:, row_tap : row_tap + extent, col_tap : col_tap + extent, :].reshape(
                -1, channels
            )
            total = total + jnp.dot(
                piece, weights[3 * row_tap + col_tap], preferred_element_type=jnp.float32
            )
    return total.reshape(members, extent, extent, weights.shape[2])


def conv_back(grad, weights):
    gpadded = jnp.pad(grad, ((0, 0), (2, 2), (2, 2), (0, 0)))
    flipped = jnp.transpose(weights[::-1], (0, 2, 1))
    return convolve(gpadded, flipped)


def weight_grad(padded, grad):
    channels = grad.shape[-1]
    extent = grad.shape[1]
    flat_grad = grad.reshape(-1, channels)
    terms = []
    for row_tap in range(3):
        for col_tap in range(3):
            piece = padded[:, row_tap : row_tap + extent, col_tap : col_tap + extent, :].reshape(
                -1, padded.shape[-1]
            )
            terms.append(
                lax.dot_general(
                    piece, flat_grad, (((0,), (0,)), ((), ())), preferred_element_type=jnp.float32
                )
            )
    return jnp.stack(terms, axis=0)


def return_halo(dpadded, edge_code, corner_code):
    tiles = lax.axis_size("tile")
    mine = lax.axis_index("tile")
    extent = dpadded.shape[1] - 2
    interior = dpadded[:, 1 : extent + 1, 1 : extent + 1]
    rims = [
        dpadded[:, 0, 1 : extent + 1],
        dpadded[:, 1 : extent + 1, extent + 1],
        dpadded[:, extent + 1, 1 : extent + 1],
        dpadded[:, 1 : extent + 1, 0],
    ]
    selector = jnp.arange(4, dtype=jnp.int32)
    accum = jnp.zeros((4,) + rims[0].shape, jnp.float32)
    for edge_index, offset in enumerate(side_offsets()):
        arrived = from_behind(rims[edge_index], "tile", offset)
        code = edge_code[(mine - offset) % tiles, edge_index]
        arrived = jnp.where(code >= 4, arrived[:, ::-1], arrived)
        onehot = (selector == code % 4).astype(jnp.float32)
        accum = accum + onehot[:, None, None, None] * arrived[None]
    places = ((0, 0), (0, extent + 1), (extent + 1, extent + 1), (extent + 1, 0))
    caccum = jnp.zeros((4, dpadded.shape[0], dpadded.shape[-1]), jnp.float32)
    for corner_index, offset in enumerate(corner_offsets()):
        values = dpadded[:, places[corner_index][0], places[corner_index][1]]
        arrived = from_behind(values, "tile", offset)
        code = corner_code[(mine - offset) % tiles, corner_index]
        onehot = (selector == code).astype(jnp.float32)
        caccum = caccum + onehot[:, None, None] * arrived[None]
    result = interior.at[:, 0].add(accum[0])
    result = result.at[:, :, extent - 1].add(accum[1])
    result = result.at[:, extent - 1].add(accum[2])
    result = result.at[:, :, 0].add(accum[3])
    result = result.at[:, 0, 0].add(caccum[0])
    result = result.at[:, 0, extent - 1].add(caccum[1])
    result = result.at[:, extent - 1, extent - 1].add(caccum[2])
    result = result.at[:, extent - 1, 0].add(caccum[3])
    return result


def gelu_slope(values):
    return jax.vjp(partial(jax.nn.gelu, approximate=True), values)[1](jnp.ones_like(values))[0]


def per_device(inputs, weight_one, weight_two, cotangent, edge_code, corner_code):
    source = inputs[:, 0]
    grad_out = cotangent[:, 0]
    counted = (
        inputs.shape[0]
        * lax.axis_size("dp")
        * lax.axis_size("tile")
        * inputs.shape[2]
        * inputs.shape[3]
    )
    factor = 1.0 / math.sqrt(counted)
    x_margin = pad_halo(source, edge_code, corner_code)
    pre_one = convolve(x_margin, weight_one)
    hidden = jax.nn.gelu(pre_one, approximate=True).astype(jnp.bfloat16)
    h_margin = pad_halo(hidden, edge_code, corner_code)
    pre_two = convolve(h_margin, weight_two)
    output = (source.astype(jnp.float32) + pre_two).astype(jnp.bfloat16)
    dh_margin = conv_back(grad_out, weight_two)
    local_two = weight_grad(h_margin, grad_out)
    d_hidden = return_halo(dh_margin, edge_code, corner_code)
    d_pre = (d_hidden * gelu_slope(pre_one)).astype(jnp.bfloat16)
    dx_margin = conv_back(d_pre, weight_one)
    local_one = weight_grad(x_margin, d_pre)
    d_input = (
        grad_out.astype(jnp.float32) + return_halo(dx_margin, edge_code, corner_code)
    ).astype(jnp.bfloat16)
    summed_one, summed_two = lax.psum((local_one, local_two), ("tile", "dp"))
    return (output[:, None], d_input[:, None], summed_one * factor, summed_two * factor)


def solution(mesh):
    in_specs = (
        P("dp", "tile", None, None, None),
        P(),
        P(),
        P("dp", "tile", None, None, None),
        P(),
        P(),
    )
    out_specs = (P("dp", "tile", None, None, None), P("dp", "tile", None, None, None), P(), P())
    return jax.shard_map(
        per_device, mesh=mesh, in_specs=in_specs, out_specs=out_specs, check_vma=False
    )
```

profile of v0, /device:TPU:0, one launch (start us, length us, event | category | flops | bytes accessed | tf_op | source)
XLA Modules:
  0.0 295.7 jit_solution(17937688795575977605)
XLA Ops:
  17.0 5.0 %collective-permute-start.5 = (bf16[1,128]{1,0:T(2,128)(2,1)S(1)}, bf16[1,128]{1,0:T(2,128)(2,1)S(1)}, u32[]{:S(2)}, u32[]{:S(2)}) collective-permute-start(bf16[1,128]{1,0:T(2,128)(2,1)S(1)} %get-tuple-element.307), channel_id=1, source_target_pairs={{0,20},{4,24},{8,28},{12,0},{16,4},{20,8},{24,12},{28,16},{1,21},{... | collective-permute-start | bytes 776 | tf_op jit(solution)/shard_map/ppermute | solution.py:14
  31.6 3.8 %collective-permute-start.22 = (f32[1,128]{1,0:T(1,128)S(1)}, f32[1,128]{1,0:T(1,128)S(1)}, u32[]{:S(2)}, u32[]{:S(2)}) collective-permute-start(f32[1,128]{1,0:T(1,128)S(1)} %get-tuple-element.228), channel_id=1, source_target_pairs={{0,20},{4,24},{8,28},{12,0},{16,4},{20,8},{24,12},{28,16},{1,21},{... | collective-permute-start | bytes 1544 | tf_op jit(solution)/shard_map/ppermute | solution.py:14
  35.6 2.7 collective-permute-start.23
  49.4 1.3 compare_convert_fusion
  53.2 1.2 compare_convert_fusion.2
  54.7 4.5 %collective-permute-start.2 = (bf16[1,128]{1,0:T(2,128)(2,1)S(1)}, bf16[1,128]{1,0:T(2,128)(2,1)S(1)}, u32[]{:S(2)}, u32[]{:S(2)}) collective-permute-start(bf16[1,128]{1,0:T(2,128)(2,1)S(1)} %get-tuple-element.309), channel_id=1, source_target_pairs={{0,12},{4,16},{8,20},{12,24},{16,28},{20,0},{24,4},{28,8},{1,13},{... | collective-permute-start | bytes 776 | tf_op jit(solution)/shard_map/ppermute | solution.py:14
  59.2 4.7 %collective-permute-start.4 = (bf16[1,32,128]{2,1,0:T(8,128)(2,1)S(1)}, bf16[1,32,128]{2,1,0:T(8,128)(2,1)S(1)}, u32[]{:S(2)}, u32[]{:S(2)}) collective-permute-start(bf16[1,32,128]{2,1,0:T(8,128)(2,1)S(1)} %broadcast_select_fusion.3), channel_id=1, source_target_pairs={{0,28},{4,0},{8,4},{12,8},{16,12},{20,16},{24,20},{28,24},{1,29},{... | collective-permute-start | bytes 24584 | tf_op jit(solution)/shard_map/ppermute | solution.py:14
  64.1 1.5 collective-permute-done.3
  66.1 2.8 collective-permute-start.6
  70.0 3.5 %collective-permute-start.19 = (f32[1,32,128]{2,1,0:T(8,128)S(1)}, f32[1,32,128]{2,1,0:T(8,128)S(1)}, u32[]{:S(2)}, u32[]{:S(2)}) collective-permute-start(f32[1,32,128]{2,1,0:T(8,128)S(1)} %bitcast.560), channel_id=1, source_target_pairs={{0,28},{4,0},{8,4},{12,8},{16,12},{20,16},{24,20},{28,24},{1,29},{... | collective-permute-start | bytes 49160 | tf_op jit(solution)/shard_map/ppermute | solution.py:14
  73.7 2.9 collective-permute-start.18
  80.6 2.0 broadcast_select_fusion.8
  82.6 1.3 scatter-add.61
  85.5 1.4 pad_slice_fusion
  86.9 1.8 reshape.1500
  88.7 1.8 reshape.1493
  90.5 1.8 reshape.1494
  92.3 1.8 reshape.1495
  94.0 1.8 reshape.1496
  97.0 1.1 fusion.51
  112.2 2.9 collective-permute-start.28
  116.1 2.4 collective-permute-start.30
  119.5 3.8 %collective-permute-start.15 = (bf16[1,128]{1,0:T(2,128)(2,1)S(1)}, bf16[1,128]{1,0:T(2,128)(2,1)S(1)}, u32[]{:S(2)}, u32[]{:S(2)}) collective-permute-start(bf16[1,128]{1,0:T(2,128)(2,1)S(1)} %get-tuple-element.304), channel_id=1, source_target_pairs={{0,12},{4,16},{8,20},{12,24},{16,28},{20,0},{24,4},{28,8},{1,13},{... | collective-permute-start | bytes 776 | tf_op jit(solution)/shard_map/ppermute | solution.py:14
  123.3 4.7 %collective-permute-start.10 = (bf16[1,128]{1,0:T(2,128)(2,1)S(1)}, bf16[1,128]{1,0:T(2,128)(2,1)S(1)}, u32[]{:S(2)}, u32[]{:S(2)}) collective-permute-start(bf16[1,128]{1,0:T(2,128)(2,1)S(1)} %get-tuple-element.305), channel_id=1, source_target_pairs={{0,12},{4,16},{8,20},{12,24},{16,28},{20,0},{24,4},{28,8},{1,13},{... | collective-permute-start | bytes 776 | tf_op jit(solution)/shard_map/ppermute | solution.py:14
  128.0 4.7 %collective-permute-start.12 = (bf16[1,32,128]{2,1,0:T(8,128)(2,1)S(1)}, bf16[1,32,128]{2,1,0:T(8,128)(2,1)S(1)}, u32[]{:S(2)}, u32[]{:S(2)}) collective-permute-start(bf16[1,32,128]{2,1,0:T(8,128)(2,1)S(1)} %broadcast_select_fusion.2), channel_id=1, source_target_pairs={{0,28},{4,0},{8,4},{12,8},{16,12},{20,16},{24,20},{28,24},{1,29},{... | collective-permute-start | bytes 24584 | tf_op jit(solution)/shard_map/ppermute | solution.py:14
  134.7 3.0 %collective-permute-start.14 = (bf16[1,32,128]{2,1,0:T(8,128)(2,1)S(1)}, bf16[1,32,128]{2,1,0:T(8,128)(2,1)S(1)}, u32[]{:S(2)}, u32[]{:S(2)}) collective-permute-start(bf16[1,32,128]{2,1,0:T(8,128)(2,1)S(1)} %broadcast_select_fusion), channel_id=1, source_target_pairs={{0,16},{4,20},{8,24},{12,28},{16,0},{20,4},{24,8},{28,12},{1,17},{... | collective-permute-start | bytes 24584 | tf_op jit(solution)/shard_map/ppermute | solution.py:14
  138.8 3.5 %collective-permute-start.27 = (f32[1,32,128]{2,1,0:T(8,128)S(1)}, f32[1,32,128]{2,1,0:T(8,128)S(1)}, u32[]{:S(2)}, u32[]{:S(2)}) collective-permute-start(f32[1,32,128]{2,1,0:T(8,128)S(1)} %bitcast.558), channel_id=1, source_target_pairs={{0,28},{4,0},{8,4},{12,8},{16,12},{20,16},{24,20},{28,24},{1,29},{... | collective-permute-start | bytes 49160 | tf_op jit(solution)/shard_map/ppermute | solution.py:14
  142.4 2.9 collective-permute-start.26
  154.3 2.0 broadcast_select_fusion.9
  156.3 1.3 scatter-add.75
  158.7 127.3 %all-reduce.5.cloned.1.call-done = (f32[9,128,128]{2,1,0:T(8,128)}, f32[9,128,128]{2,1,0:T(8,128)}) async-done(((f32[9,128,128]{2,1,0:T(8,128)}, f32[9,128,128]{2,1,0:T(8,128)}), (f32[9,128,128]{2,1,0:T(8,128)}, f32[9,128,128]{2,1,0:T(8,128)})) %all-reduce.5.cloned.1.call-update) | async-done | bytes 1179664 | tf_op jit(solution)/shard_map/psum | solution.py:168
  286.0 2.0 broadcast_multiply_fusion.1
  (323 shorter events, 52.6 us)
Async XLA Ops:
  7.2 278.8 %all-reduce.5.cloned.1.call-start = ((), (), s32[]{:S(2)}) async-start(), calls=%async_computation | async-start | bytes 2359296 | tf_op jit(solution)/shard_map/psum | solution.py:168
  17.0 56.6 %collective-permute-start.5 = (bf16[1,128]{1,0:T(2,128)(2,1)S(1)}, bf16[1,128]{1,0:T(2,128)(2,1)S(1)}, u32[]{:S(2)}, u32[]{:S(2)}) collective-permute-start(bf16[1,128]{1,0:T(2,128)(2,1)S(1)} %get-tuple-element.307), channel_id=1, source_target_pairs={{0,20},{4,24},{8,28},{12,0},{16,4},{20,8},{24,12},{28,16},{1,21},{... | collective-permute-start | bytes 776 | tf_op jit(solution)/shard_map/ppermute | solution.py:14
  31.6 23.0 %collective-permute-start.20 = (f32[1,128]{1,0:T(1,128)S(1)}, f32[1,128]{1,0:T(1,128)S(1)}, u32[]{:S(2)}, u32[]{:S(2)}) collective-permute-start(f32[1,128]{1,0:T(1,128)S(1)} %get-tuple-element.227), channel_id=1, source_target_pairs={{0,12},{4,16},{8,20},{12,24},{16,28},{20,0},{24,4},{28,8},{1,13},{... | collective-permute-start | bytes 1544 | tf_op jit(solution)/shard_map/ppermute | solution.py:14
  31.6 23.0 %collective-permute-start.22 = (f32[1,128]{1,0:T(1,128)S(1)}, f32[1,128]{1,0:T(1,128)S(1)}, u32[]{:S(2)}, u32[]{:S(2)}) collective-permute-start(f32[1,128]{1,0:T(1,128)S(1)} %get-tuple-element.228), channel_id=1, source_target_pairs={{0,20},{4,24},{8,28},{12,0},{16,4},{20,8},{24,12},{28,16},{1,21},{... | collective-permute-start | bytes 1544 | tf_op jit(solution)/shard_map/ppermute | solution.py:14
  35.5 23.8 %collective-permute-start.21 = (f32[1,128]{1,0:T(1,128)S(1)}, f32[1,128]{1,0:T(1,128)S(1)}, u32[]{:S(2)}, u32[]{:S(2)}) collective-permute-start(f32[1,128]{1,0:T(1,128)S(1)} %get-tuple-element.229), channel_id=1, source_target_pairs={{0,20},{4,24},{8,28},{12,0},{16,4},{20,8},{24,12},{28,16},{1,21},{... | collective-permute-start | bytes 1544 | tf_op jit(solution)/shard_map/ppermute | solution.py:14
  35.6 23.6 %collective-permute-start.23 = (f32[1,128]{1,0:T(1,128)S(1)}, f32[1,128]{1,0:T(1,128)S(1)}, u32[]{:S(2)}, u32[]{:S(2)}) collective-permute-start(f32[1,128]{1,0:T(1,128)S(1)} %get-tuple-element.230), channel_id=1, source_target_pairs={{0,12},{4,16},{8,20},{12,24},{16,28},{20,0},{24,4},{28,8},{1,13},{... | collective-permute-start | bytes 1544 | tf_op jit(solution)/shard_map/ppermute | solution.py:14
  54.6 19.1 %collective-permute-start.7 = (bf16[1,128]{1,0:T(2,128)(2,1)S(1)}, bf16[1,128]{1,0:T(2,128)(2,1)S(1)}, u32[]{:S(2)}, u32[]{:S(2)}) collective-permute-start(bf16[1,128]{1,0:T(2,128)(2,1)S(1)} %get-tuple-element.308), channel_id=1, source_target_pairs={{0,12},{4,16},{8,20},{12,24},{16,28},{20,0},{24,4},{28,8},{1,13},{... | collective-permute-start | bytes 776 | tf_op jit(solution)/shard_map/ppermute | solution.py:14
  54.7 11.4 %collective-permute-start.2 = (bf16[1,128]{1,0:T(2,128)(2,1)S(1)}, bf16[1,128]{1,0:T(2,128)(2,1)S(1)}, u32[]{:S(2)}, u32[]{:S(2)}) collective-permute-start(bf16[1,128]{1,0:T(2,128)(2,1)S(1)} %get-tuple-element.309), channel_id=1, source_target_pairs={{0,12},{4,16},{8,20},{12,24},{16,28},{20,0},{24,4},{28,8},{1,13},{... | collective-permute-start | bytes 776 | tf_op jit(solution)/shard_map/ppermute | solution.py:14
  59.2 6.3 %collective-permute-start.3 = (bf16[1,32,128]{2,1,0:T(8,128)(2,1)S(1)}, bf16[1,32,128]{2,1,0:T(8,128)(2,1)S(1)}, u32[]{:S(2)}, u32[]{:S(2)}) collective-permute-start(bf16[1,32,128]{2,1,0:T(8,128)(2,1)S(1)} %broadcast_select_fusion.5), channel_id=1, source_target_pairs={{0,4},{4,8},{8,12},{12,16},{16,20},{20,24},{24,28},{28,0},{1,5},{5... | collective-permute-start | bytes 24584 | tf_op jit(solution)/shard_map/ppermute | solution.py:14
  59.2 6.4 %collective-permute-start.4 = (bf16[1,32,128]{2,1,0:T(8,128)(2,1)S(1)}, bf16[1,32,128]{2,1,0:T(8,128)(2,1)S(1)}, u32[]{:S(2)}, u32[]{:S(2)}) collective-permute-start(bf16[1,32,128]{2,1,0:T(8,128)(2,1)S(1)} %broadcast_select_fusion.3), channel_id=1, source_target_pairs={{0,28},{4,0},{8,4},{12,8},{16,12},{20,16},{24,20},{28,24},{1,29},{... | collective-permute-start | bytes 24584 | tf_op jit(solution)/shard_map/ppermute | solution.py:14
  65.6 4.4 %collective-permute-start = (bf16[1,128]{1,0:T(2,128)(2,1)S(1)}, bf16[1,128]{1,0:T(2,128)(2,1)S(1)}, u32[]{:S(2)}, u32[]{:S(2)}) collective-permute-start(bf16[1,128]{1,0:T(2,128)(2,1)S(1)} %get-tuple-element.310), channel_id=1, source_target_pairs={{0,20},{4,24},{8,28},{12,0},{16,4},{20,8},{24,12},{28,16},{1,21},{... | collective-permute-start | bytes 776 | tf_op jit(solution)/shard_map/ppermute | solution.py:14
  65.6 7.9 %collective-permute-start.1 = (bf16[1,32,128]{2,1,0:T(8,128)(2,1)S(1)}, bf16[1,32,128]{2,1,0:T(8,128)(2,1)S(1)}, u32[]{:S(2)}, u32[]{:S(2)}) collective-permute-start(bf16[1,32,128]{2,1,0:T(8,128)(2,1)S(1)} %broadcast_select_fusion.7), channel_id=1, source_target_pairs={{0,16},{4,20},{8,24},{12,28},{16,0},{20,4},{24,8},{28,12},{1,17},{... | collective-permute-start | bytes 24584 | tf_op jit(solution)/shard_map/ppermute | solution.py:14
  66.1 10.4 %collective-permute-start.6 = (bf16[1,32,128]{2,1,0:T(8,128)(2,1)S(1)}, bf16[1,32,128]{2,1,0:T(8,128)(2,1)S(1)}, u32[]{:S(2)}, u32[]{:S(2)}) collective-permute-start(bf16[1,32,128]{2,1,0:T(8,128)(2,1)S(1)} %broadcast_select_fusion.1), channel_id=1, source_target_pairs={{0,16},{4,20},{8,24},{12,28},{16,0},{20,4},{24,8},{28,12},{1,17},{... | collective-permute-start | bytes 24584 | tf_op jit(solution)/shard_map/ppermute | solution.py:14
  70.0 9.1 %collective-permute-start.19 = (f32[1,32,128]{2,1,0:T(8,128)S(1)}, f32[1,32,128]{2,1,0:T(8,128)S(1)}, u32[]{:S(2)}, u32[]{:S(2)}) collective-permute-start(f32[1,32,128]{2,1,0:T(8,128)S(1)} %bitcast.560), channel_id=1, source_target_pairs={{0,28},{4,0},{8,4},{12,8},{16,12},{20,16},{24,20},{28,24},{1,29},{... | collective-permute-start | bytes 49160 | tf_op jit(solution)/shard_map/ppermute | solution.py:14
  73.6 6.4 %collective-permute-start.17 = (f32[1,32,128]{2,1,0:T(8,128)S(1)}, f32[1,32,128]{2,1,0:T(8,128)S(1)}, u32[]{:S(2)}, u32[]{:S(2)}) collective-permute-start(f32[1,32,128]{2,1,0:T(8,128)S(1)} %bitcast.559), channel_id=1, source_target_pairs={{0,4},{4,8},{8,12},{12,16},{16,20},{20,24},{24,28},{28,0},{1,5},{5... | collective-permute-start | bytes 49160 | tf_op jit(solution)/shard_map/ppermute | solution.py:14
  73.6 6.4 %collective-permute-start.16 = (f32[1,32,128]{2,1,0:T(8,128)S(1)}, f32[1,32,128]{2,1,0:T(8,128)S(1)}, u32[]{:S(2)}, u32[]{:S(2)}) collective-permute-start(f32[1,32,128]{2,1,0:T(8,128)S(1)} %get-tuple-element.231), channel_id=1, source_target_pairs={{0,16},{4,20},{8,24},{12,28},{16,0},{20,4},{24,8},{28,12},{1,17},{... | collective-permute-start | bytes 49160 | tf_op jit(solution)/shard_map/ppermute | solution.py:14
  73.7 6.4 %collective-permute-start.18 = (f32[1,32,128]{2,1,0:T(8,128)S(1)}, f32[1,32,128]{2,1,0:T(8,128)S(1)}, u32[]{:S(2)}, u32[]{:S(2)}) collective-permute-start(f32[1,32,128]{2,1,0:T(8,128)S(1)} %get-tuple-element.232), channel_id=1, source_target_pairs={{0,16},{4,20},{8,24},{12,28},{16,0},{20,4},{24,8},{28,12},{1,17},{... | collective-permute-start | bytes 49160 | tf_op jit(solution)/shard_map/ppermute | solution.py:14
  104.1 38.2 %collective-permute-start.13 = (bf16[1,128]{1,0:T(2,128)(2,1)S(1)}, bf16[1,128]{1,0:T(2,128)(2,1)S(1)}, u32[]{:S(2)}, u32[]{:S(2)}) collective-permute-start(bf16[1,128]{1,0:T(2,128)(2,1)S(1)} %get-tuple-element.303), channel_id=1, source_target_pairs={{0,20},{4,24},{8,28},{12,0},{16,4},{20,8},{24,12},{28,16},{1,21},{... | collective-permute-start | bytes 776 | tf_op jit(solution)/shard_map/ppermute | solution.py:14
  112.2 7.2 %collective-permute-start.28 = (f32[1,128]{1,0:T(1,128)S(1)}, f32[1,128]{1,0:T(1,128)S(1)}, u32[]{:S(2)}, u32[]{:S(2)}) collective-permute-start(f32[1,128]{1,0:T(1,128)S(1)} %get-tuple-element.218), channel_id=1, source_target_pairs={{0,12},{4,16},{8,20},{12,24},{16,28},{20,0},{24,4},{28,8},{1,13},{... | collective-permute-start | bytes 1544 | tf_op jit(solution)/shard_map/ppermute | solution.py:14
  115.2 8.1 %collective-permute-start.29 = (f32[1,128]{1,0:T(1,128)S(1)}, f32[1,128]{1,0:T(1,128)S(1)}, u32[]{:S(2)}, u32[]{:S(2)}) collective-permute-start(f32[1,128]{1,0:T(1,128)S(1)} %get-tuple-element.219), channel_id=1, source_target_pairs={{0,20},{4,24},{8,28},{12,0},{16,4},{20,8},{24,12},{28,16},{1,21},{... | collective-permute-start | bytes 1544 | tf_op jit(solution)/shard_map/ppermute | solution.py:14
  116.1 11.9 %collective-permute-start.30 = (f32[1,128]{1,0:T(1,128)S(1)}, f32[1,128]{1,0:T(1,128)S(1)}, u32[]{:S(2)}, u32[]{:S(2)}) collective-permute-start(f32[1,128]{1,0:T(1,128)S(1)} %get-tuple-element.220), channel_id=1, source_target_pairs={{0,20},{4,24},{8,28},{12,0},{16,4},{20,8},{24,12},{28,16},{1,21},{... | collective-permute-start | bytes 1544 | tf_op jit(solution)/shard_map/ppermute | solution.py:14
  118.4 9.5 %collective-permute-start.31 = (f32[1,128]{1,0:T(1,128)S(1)}, f32[1,128]{1,0:T(1,128)S(1)}, u32[]{:S(2)}, u32[]{:S(2)}) collective-permute-start(f32[1,128]{1,0:T(1,128)S(1)} %get-tuple-element.221), channel_id=1, source_target_pairs={{0,12},{4,16},{8,20},{12,24},{16,28},{20,0},{24,4},{28,8},{1,13},{... | collective-permute-start | bytes 1544 | tf_op jit(solution)/shard_map/ppermute | solution.py:14
  119.5 22.9 %collective-permute-start.15 = (bf16[1,128]{1,0:T(2,128)(2,1)S(1)}, bf16[1,128]{1,0:T(2,128)(2,1)S(1)}, u32[]{:S(2)}, u32[]{:S(2)}) collective-permute-start(bf16[1,128]{1,0:T(2,128)(2,1)S(1)} %get-tuple-element.304), channel_id=1, source_target_pairs={{0,12},{4,16},{8,20},{12,24},{16,28},{20,0},{24,4},{28,8},{1,13},{... | collective-permute-start | bytes 776 | tf_op jit(solution)/shard_map/ppermute | solution.py:14
  123.3 11.4 %collective-permute-start.10 = (bf16[1,128]{1,0:T(2,128)(2,1)S(1)}, bf16[1,128]{1,0:T(2,128)(2,1)S(1)}, u32[]{:S(2)}, u32[]{:S(2)}) collective-permute-start(bf16[1,128]{1,0:T(2,128)(2,1)S(1)} %get-tuple-element.305), channel_id=1, source_target_pairs={{0,12},{4,16},{8,20},{12,24},{16,28},{20,0},{24,4},{28,8},{1,13},{... | collective-permute-start | bytes 776 | tf_op jit(solution)/shard_map/ppermute | solution.py:14
  128.0 6.3 %collective-permute-start.11 = (bf16[1,32,128]{2,1,0:T(8,128)(2,1)S(1)}, bf16[1,32,128]{2,1,0:T(8,128)(2,1)S(1)}, u32[]{:S(2)}, u32[]{:S(2)}) collective-permute-start(bf16[1,32,128]{2,1,0:T(8,128)(2,1)S(1)} %broadcast_select_fusion.4), channel_id=1, source_target_pairs={{0,4},{4,8},{8,12},{12,16},{16,20},{20,24},{24,28},{28,0},{1,5},{5... | collective-permute-start | bytes 24584 | tf_op jit(solution)/shard_map/ppermute | solution.py:14
  128.0 6.4 %collective-permute-start.12 = (bf16[1,32,128]{2,1,0:T(8,128)(2,1)S(1)}, bf16[1,32,128]{2,1,0:T(8,128)(2,1)S(1)}, u32[]{:S(2)}, u32[]{:S(2)}) collective-permute-start(bf16[1,32,128]{2,1,0:T(8,128)(2,1)S(1)} %broadcast_select_fusion.2), channel_id=1, source_target_pairs={{0,28},{4,0},{8,4},{12,8},{16,12},{20,16},{24,20},{28,24},{1,29},{... | collective-permute-start | bytes 24584 | tf_op jit(solution)/shard_map/ppermute | solution.py:14
  134.4 7.9 %collective-permute-start.9 = (bf16[1,32,128]{2,1,0:T(8,128)(2,1)S(1)}, bf16[1,32,128]{2,1,0:T(8,128)(2,1)S(1)}, u32[]{:S(2)}, u32[]{:S(2)}) collective-permute-start(bf16[1,32,128]{2,1,0:T(8,128)(2,1)S(1)} %broadcast_select_fusion.6), channel_id=1, source_target_pairs={{0,16},{4,20},{8,24},{12,28},{16,0},{20,4},{24,8},{28,12},{1,17},{... | collective-permute-start | bytes 24584 | tf_op jit(solution)/shard_map/ppermute | solution.py:14
  134.7 10.6 %collective-permute-start.14 = (bf16[1,32,128]{2,1,0:T(8,128)(2,1)S(1)}, bf16[1,32,128]{2,1,0:T(8,128)(2,1)S(1)}, u32[]{:S(2)}, u32[]{:S(2)}) collective-permute-start(bf16[1,32,128]{2,1,0:T(8,128)(2,1)S(1)} %broadcast_select_fusion), channel_id=1, source_target_pairs={{0,16},{4,20},{8,24},{12,28},{16,0},{20,4},{24,8},{28,12},{1,17},{... | collective-permute-start | bytes 24584 | tf_op jit(solution)/shard_map/ppermute | solution.py:14
  138.8 14.3 %collective-permute-start.27 = (f32[1,32,128]{2,1,0:T(8,128)S(1)}, f32[1,32,128]{2,1,0:T(8,128)S(1)}, u32[]{:S(2)}, u32[]{:S(2)}) collective-permute-start(f32[1,32,128]{2,1,0:T(8,128)S(1)} %bitcast.558), channel_id=1, source_target_pairs={{0,28},{4,0},{8,4},{12,8},{16,12},{20,16},{24,20},{28,24},{1,29},{... | collective-permute-start | bytes 49160 | tf_op jit(solution)/shard_map/ppermute | solution.py:14
  142.3 10.8 %collective-permute-start.25 = (f32[1,32,128]{2,1,0:T(8,128)S(1)}, f32[1,32,128]{2,1,0:T(8,128)S(1)}, u32[]{:S(2)}, u32[]{:S(2)}) collective-permute-start(f32[1,32,128]{2,1,0:T(8,128)S(1)} %bitcast.557), channel_id=1, source_target_pairs={{0,4},{4,8},{8,12},{12,16},{16,20},{20,24},{24,28},{28,0},{1,5},{5... | collective-permute-start | bytes 49160 | tf_op jit(solution)/shard_map/ppermute | solution.py:14
  142.3 10.8 %collective-permute-start.24 = (f32[1,32,128]{2,1,0:T(8,128)S(1)}, f32[1,32,128]{2,1,0:T(8,128)S(1)}, u32[]{:S(2)}, u32[]{:S(2)}) collective-permute-start(f32[1,32,128]{2,1,0:T(8,128)S(1)} %get-tuple-element.222), channel_id=1, source_target_pairs={{0,16},{4,20},{8,24},{12,28},{16,0},{20,4},{24,8},{28,12},{1,17},{... | collective-permute-start | bytes 49160 | tf_op jit(solution)/shard_map/ppermute | solution.py:14
  142.4 10.8 %collective-permute-start.26 = (f32[1,32,128]{2,1,0:T(8,128)S(1)}, f32[1,32,128]{2,1,0:T(8,128)S(1)}, u32[]{:S(2)}, u32[]{:S(2)}) collective-permute-start(f32[1,32,128]{2,1,0:T(8,128)S(1)} %get-tuple-element.224), channel_id=1, source_target_pairs={{0,16},{4,20},{8,24},{12,28},{16,0},{20,4},{24,8},{28,12},{1,17},{... | collective-permute-start | bytes 49160 | tf_op jit(solution)/shard_map/ppermute | solution.py:14
  (40 other events, 274.9 us)
Sparse Core Ops, SparseCore 0:
  153.2 132.7 all-reduce.4
where the time goes:
time: 297 us; the launch traced here: 296 us
  waiting for transfers between devices  133 us (45%)
  starting transfers between devices  61 us (21%)
  between operations  33.7 us (11%)
  local copies, waits for them, and re-layouts  33.5 us (11%)
  matrix products  21.6 us (7%)
  other arithmetic  12.9 us (4%)
    psum x1, waiting for transfers between devices, per_device(): summed_one, summed_two = lax.psum((local_one, local_two), ('tile', 'dp'))  127 us
    ppermute x32, starting transfers between devices, from_behind(): return lax.ppermute(x, axis, [(i, (i + by) % count) for i in range(count)])  61 us
    reshape x18, local copies, waits for them, and re-layouts, convolve(): padded[:, row_tap:row_tap + extent, col_tap:col_tap + extent, :]  11.5 us
    dot_general x36, matrix products, convolve(): jnp.dot(piece, weights[3 * row_tap + col_tap], preferred_element_type=jnp...  11 us
    unnamed x83, local copies, waits for them, and re-layouts  10.8 us
    dot_general x18, matrix products, weight_grad(): lax.dot_general(piece, flat_grad, (((0,), (0,)), ((), ())), preferred_ele...  10.6 us
  transfers between devices with their start and end apart: 33, of which 6 were waited for; matrix products, arithmetic and copies ran while one was open for 12% of the time, Pallas kernels for 0%

commit v1 on v0

v1 whole, which is shorter than its diff:
```python
import math

import jax
import jax.numpy as jnp
from jax import lax
from jax.experimental import pallas as pl
from jax.experimental.pallas import tpu as pltpu
from jax.sharding import PartitionSpec as P

RW = 4
SIDES = (-RW, 1, RW, -1)
CORNERS = (-RW - 1, -RW + 1, RW + 1, RW - 1)
F32 = jnp.float32
BF16 = jnp.bfloat16
AXES = ("tile", "dp")
LIMIT = 48 * 1024 * 1024

BLOCKS = ((0, (0, 1)), (2, (3, 2)), (1, ()), (3, ()))


def block_rows(extent):
    return (extent + 16, extent + 16, extent, extent)


def block_starts(extent):
    rows = block_rows(extent)
    return (0, rows[0], rows[0] + rows[1], rows[0] + rows[1] + rows[2])


def block_taps(position):
    return ((0, 1, 2), (6, 7, 8), (2, 5, 8), (0, 3, 6))[position]


def routes(tiles):
    found = {}
    for kind, offsets in (("a", SIDES), ("b", SIDES), ("ac", CORNERS), ("bc", CORNERS)):
        for which, offset in enumerate(offsets):
            distance = (-offset if kind[0] == "a" else offset) % tiles
            found.setdefault(distance, []).append((kind, which))
    plan = []
    for distance, parts in found.items():
        sides = [p for p in parts if len(p[0]) == 1]
        corners = [p for p in parts if len(p[0]) == 2]
        plan.append((distance, sides, corners))
    return plan


def route_rows(route, extent):
    return extent * len(route[1]) + (16 if route[2] else 0)


def iota(shape, axis):
    return lax.broadcasted_iota(jnp.int32, shape, axis)


def dot(a, b):
    return lax.dot_general(a, b, (((1,), (0,)), ((), ())), preferred_element_type=F32)


def dot_t(a, b):
    return lax.dot_general(a, b, (((0,), (0,)), ((), ())), preferred_element_type=F32)


def corner_pixel(code, extent):
    last = extent - 1
    return jnp.where(code == 0, 0, jnp.where(code == 1, last, jnp.where(code == 2, extent * extent - 1, extent * last)))


def side_line(code, extent):
    last = extent - 1
    border = code % 4
    base = jnp.where(border == 1, last, jnp.where(border == 2, extent * last, 0))
    step = jnp.where(border % 2 == 0, 1, extent)
    return jnp.where(code >= 4, base + last * step, base), jnp.where(code >= 4, -step, step)


def seam_lines(edge_ref, corner_ref, extent):
    tiles = edge_ref.shape[0]
    mine = lax.axis_index("tile")
    lines = [side_line(edge_ref[(mine - o + tiles + RW * tiles) % tiles, k], extent) for k, o in enumerate(SIDES)]
    pixels = [corner_pixel(corner_ref[(mine - o + tiles + RW * tiles) % tiles, q], extent) for q, o in enumerate(CORNERS)]
    return lines, pixels


def fixed_lines(extent):
    last = extent - 1
    lines = [(0, 1), (last, extent), (extent * last, 1), (0, extent)]
    return lines, [0, last, extent * extent - 1, extent * last]


def pick_rows(indices, count):
    return (iota((indices.shape[0], count), 1) == indices).astype(F32).astype(BF16)


def line_rows(line, extent, count):
    return pick_rows(line[0] + line[1] * iota((extent, 1), 0), count)


def spot_rows(spots, count):
    rows = iota((16, 1), 0)
    index = jnp.full((16, 1), -1, jnp.int32)
    for row, pixel in spots:
        index = jnp.where(rows == row, pixel, index)
    return pick_rows(index, count)


def gather_block(image, position, lines, pixels, extent):
    side, corners = BLOCKS[position]
    count = image.shape[0]
    rows = line_rows(lines[side], extent, count)
    if corners:
        rows = jnp.concatenate([rows, spot_rows([(i, pixels[q]) for i, q in enumerate(corners)], count)], axis=0)
    return dot(rows, image).astype(BF16)


def gather_blocks(image, lines, pixels, extent):
    return [gather_block(image, i, lines, pixels, extent) for i in range(4)]


def write_routes(a_blocks, b_blocks, plan, out_refs, extent):
    side_at = {side: i for i, (side, _) in enumerate(BLOCKS)}
    corner_at = {q: (i, extent + j) for i, (_, corners) in enumerate(BLOCKS) for j, q in enumerate(corners)}
    for route, out in zip(plan, out_refs):
        at = 0
        for kind, side in route[1]:
            blocks = a_blocks if kind == "a" else b_blocks
            out[at : at + extent, :] = blocks[side_at[side]][:extent]
            at += extent
        if route[2]:
            rows = iota((16, 1), 0)
            tile = jnp.zeros((16, out.shape[1]), F32)
            for i, (kind, q) in enumerate(route[2]):
                block, row = corner_at[q]
                source = (a_blocks if kind == "ac" else b_blocks)[block][extent : extent + 16].astype(F32)
                tile = jnp.where(rows == i, source[row - extent : row - extent + 1], tile)
            out[at : at + 16, :] = tile.astype(BF16)


def read_routes(plan, in_refs, extent):
    sides, corners = {}, {}
    for route, ref in zip(plan, in_refs):
        at = 0
        for key in route[1]:
            sides[key] = ref[at : at + extent, :]
            at += extent
        if route[2]:
            tile = ref[at : at + 16, :].astype(F32)
            for i, key in enumerate(route[2]):
                corners[key] = tile[i : i + 1]
    result = []
    rows = iota((16, 1), 0)
    for kind in ("a", "b"):
        blocks = []
        for side, ends in BLOCKS:
            block = sides[(kind, side)]
            if ends:
                tile = jnp.zeros((16, block.shape[1]), F32)
                for i, q in enumerate(ends):
                    tile = jnp.where(rows == i, corners[(kind + "c", q)], tile)
                block = jnp.concatenate([block, tile.astype(BF16)], axis=0)
            blocks.append(block)
        result.append(blocks)
    return result


def shifted(image, by, extent):
    if by == 0:
        return image
    column = iota((image.shape[0], 1), 0) % extent
    rolled = pltpu.roll(image, (-by) % image.shape[0], 0)
    return jnp.where(column == (extent - 1 if by == 1 else 0), 0.0, rolled)


def write_columns(q_ref, image, forward, extent):
    count, channels = image.shape
    zero = jnp.zeros((extent, q_ref.shape[1]), BF16)
    q_ref[0:extent, :] = zero
    q_ref[extent + count : 2 * extent + count, :] = zero
    wide = image.astype(F32)
    for b in range(3):
        by = b - 1 if forward else 1 - b
        q_ref[extent : extent + count, b * channels : (b + 1) * channels] = shifted(wide, by, extent).astype(BF16)


def window_product(q_ref, weight, forward, extent, chunk=256):
    count = q_ref.shape[0] - 2 * extent
    pieces = []
    for start in range(0, count, chunk):
        rows = [q_ref[(a if forward else 2 - a) * extent + start : (a if forward else 2 - a) * extent + start + chunk, :] for a in range(3)]
        pieces.append(dot(jnp.concatenate(rows, axis=1), weight))
    return jnp.concatenate(pieces, axis=0)


def tap_weight(weight, taps, channels):
    return jnp.concatenate([weight[t * channels : (t + 1) * channels, :] for t in taps], axis=0)


def halves(values):
    high = values.astype(BF16)
    return high, (values - high.astype(F32)).astype(BF16)


def margin_forward(strips, weight, extent):
    channels = strips[0].shape[1]
    count = extent * extent
    adds = []
    for position, (side, ends) in enumerate(BLOCKS):
        middle = strips[position][:extent].astype(F32)
        row = iota((extent, 1), 0)
        before, after = 0.0, 0.0
        if ends:
            tile = strips[position][extent : extent + 16].astype(F32)
            before, after = tile[0:1], tile[1:2]
        left = jnp.where(row == 0, before, pltpu.roll(middle, 1, 0))
        right = jnp.where(row == extent - 1, after, pltpu.roll(middle, extent - 1, 0))
        columns = jnp.concatenate([left, middle, right], axis=1).astype(BF16)
        adds.append(dot(columns, tap_weight(weight, block_taps(position), channels)))
    spread = jnp.concatenate(list(halves(adds[2])) + list(halves(adds[3])), axis=0)
    lane = iota((1, 4 * extent), 1)
    target = (lane % extent) * extent + jnp.where(lane < 2 * extent, extent - 1, 0)
    image = dot((iota((count, 1), 0) == target).astype(F32).astype(BF16), spread)
    top = image[:extent] + adds[0]
    bottom = image[count - extent :] + adds[1]
    return jnp.concatenate([top, image[extent : count - extent], bottom], axis=0)


def strip_columns(strips, extent):
    result = []
    for position, (side, ends) in enumerate(BLOCKS):
        middle = strips[position][:extent].astype(F32)
        row = iota((extent, 1), 0)
        after = jnp.where(row == extent - 1, 0.0, pltpu.roll(middle, extent - 1, 0))
        before = jnp.where(row == 0, 0.0, pltpu.roll(middle, 1, 0))
        columns = jnp.concatenate([after, middle, before], axis=1)
        if ends:
            tile = strips[position][extent : extent + 16].astype(F32)
            row = iota((16, 1), 0)
            low = jnp.where(row == 0, tile, 0.0)
            high = jnp.where(row == 1, tile, 0.0)
            columns = jnp.concatenate([columns, jnp.concatenate([low, jnp.zeros_like(tile), high], axis=1)], axis=0)
        result.append(columns.astype(BF16))
    return result


def margin_backward(columns, weight_t, lines, pixels, extent):
    channels = weight_t.shape[1]
    count = extent * extent
    adds = [dot(columns[i], tap_weight(weight_t, block_taps(i), channels)) for i in range(4)]
    stacked = jnp.concatenate(adds, axis=0)
    total = stacked.shape[0]
    lane = iota((1, total), 1)
    index = jnp.full((1, total), -1, jnp.int32)
    for start, (side, ends) in zip(block_starts(extent), BLOCKS):
        base, step = lines[side]
        index = jnp.where((lane >= start) & (lane < start + extent), base + step * (lane - start), index)
        for i, q in enumerate(ends):
            index = jnp.where(lane == start + extent + i, pixels[q], index)
    scatter = (iota((count, 1), 0) == index).astype(F32).astype(BF16)
    high, low = halves(stacked)
    return dot(scatter, high) + dot(scatter, low)


def weight_sum(out_ref, image_t, q_ref, strips, columns, extent):
    channels = image_t.shape[0]
    count = image_t.shape[1]
    wide = [dot_t(strips[i], columns[i]) for i in range(4)]
    for a in range(3):
        rows = q_ref[(2 - a) * extent : (2 - a) * extent + count, :]
        product = dot(image_t, rows)
        for b in range(3):
            tap = 3 * a + b
            value = product[:, b * channels : (b + 1) * channels]
            for position in range(4):
                taps = block_taps(position)
                if tap in taps:
                    at = taps.index(tap)
                    value = value + wide[position][:, at * channels : (at + 1) * channels]
            out_ref[tap * channels : (tap + 1) * channels, :] = value


def transpose_taps(out_ref, weight_ref):
    channels = out_ref.shape[1]
    for tap in range(9):
        block = weight_ref[tap * channels : (tap + 1) * channels, :]
        out_ref[tap * channels : (tap + 1) * channels, :] = jnp.transpose(block.astype(F32)).astype(BF16)


def gelu_parts(u):
    scale = math.sqrt(2.0 / math.pi)
    square = u * u
    t = jnp.tanh(scale * (u + 0.044715 * (square * u)))
    value = 0.5 * u * (1.0 + t)
    slope = 0.5 * (1.0 + t) + (0.5 * u) * (1.0 - t * t) * (scale * (1.0 + 3.0 * 0.044715 * square))
    return value, slope


def call(kernel, name, outs, ins, operands, scratch=(), flops=0):
    specs = [pl.BlockSpec(memory_space=pltpu.SMEM if i == "s" else pltpu.VMEM) for i in ins]
    moved = sum(math.prod(o.shape) * o.dtype.itemsize for o in list(outs) + list(operands))
    return pl.pallas_call(
        kernel,
        name=name,
        out_shape=outs,
        in_specs=specs,
        out_specs=[pl.BlockSpec(memory_space=pltpu.VMEM) for _ in outs],
        scratch_shapes=list(scratch),
        cost_estimate=pl.CostEstimate(flops=flops, bytes_accessed=moved, transcendentals=0),
        compiler_params=pltpu.CompilerParams(vmem_limit_bytes=LIMIT),
    )(*operands)


def sds(shape, dtype):
    return jax.ShapeDtypeStruct(shape, dtype)


def exchange(payloads, plan, tiles):
    return [
        lax.ppermute(p, "tile", [(i, (i + route[0]) % tiles) for i in range(tiles)]) for p, route in zip(payloads, plan)
    ]


def swap(value, mask, total):
    return lax.ppermute(value, AXES, [(i, i ^ mask) for i in range(total)])


def reduce_gradients(keep, send, total):
    rows, channels = keep.shape
    wire = BF16 if total <= 32 else F32
    me = lax.axis_index(AXES)
    own = keep + swap(send, 1, total).astype(F32)
    plane = (me >> 1) & 3
    parts = own.reshape(4, rows // 4, channels)
    sent = parts.astype(wire)
    arrived = [
        swap(lax.dynamic_index_in_dim(sent, plane ^ m, 0, keepdims=False), m << 1, total).astype(F32) for m in (3, 1, 2)
    ]
    part = lax.dynamic_index_in_dim(parts, plane, 0, keepdims=False)
    part = part + arrived[0] + arrived[1] + arrived[2]
    bit = 8
    while bit < total:
        mine = part.astype(wire)
        if 2 * bit < total:
            far, middle, near = [swap(mine, m * bit, total).astype(F32) for m in (3, 2, 1)]
            part = (mine.astype(F32) + near) + (middle + far)
            bit *= 4
        else:
            part = mine.astype(F32) + swap(mine, bit, total).astype(F32)
            bit *= 2
    mine = part.astype(wire)
    ring = jnp.stack([mine] + [swap(mine, m << 1, total) for m in (1, 2, 3)])
    whole = jnp.concatenate([lax.dynamic_index_in_dim(ring, plane ^ j, 0) for j in range(4)], axis=0)
    other = swap(whole, 1, total)
    first = (me & 1) == 0
    return jnp.where(first, whole, other), jnp.where(first, other, whole)


def per_device(inputs, weight_one, weight_two, cotangent, edge_code, corner_code):
    tiles, members = lax.axis_size("tile"), lax.axis_size("dp")
    extent, channels = inputs.shape[2], inputs.shape[4]
    count = extent * extent
    factor = 1.0 / math.sqrt(inputs.shape[0] * members * tiles * count)
    source = inputs.reshape(count, channels)
    grad_out = cotangent.reshape(count, channels)
    w_one = weight_one.reshape(9 * channels, channels)
    w_two = weight_two.reshape(9 * channels, channels)
    plan = routes(tiles)
    routed = [sds((route_rows(r, extent), channels), BF16) for r in plan]
    n_routes = len(plan)
    image_b, image_f = sds((count, channels), BF16), sds((count, channels), F32)
    columns_b = sds((count + 2 * extent, 3 * channels), BF16)
    taps_b, taps_f = sds((9 * channels, channels), BF16), sds((9 * channels, channels), F32)
    turned_b = sds((channels, count), BF16)
    conv = 2 * count * 9 * channels * channels

    def first_strips(edge_ref, corner_ref, x_ref, g_ref, *outs):
        lines, pixels = seam_lines(edge_ref, corner_ref, extent)
        a = gather_blocks(x_ref[...], lines, pixels, extent)
        b = gather_blocks(g_ref[...], *fixed_lines(extent), extent)
        write_routes(a, b, plan, outs, extent)

    first = call(first_strips, "first_strips", routed, "ssvv", (edge_code, corner_code, source, grad_out))
    first_arrived = exchange(first, plan, tiles)

    def inner(x_ref, g_ref, w1_ref, w2_ref, pre_ref, dh_ref, xt_ref, qg_ref, w1t_ref, w2t_ref, qx_ref):
        transpose_taps(w1t_ref, w1_ref)
        transpose_taps(w2t_ref, w2_ref)
        write_columns(qx_ref, x_ref[...], True, extent)
        pre_ref[...] = window_product(qx_ref, w1_ref[...], True, extent)
        write_columns(qg_ref, g_ref[...], False, extent)
        dh_ref[...] = window_product(qg_ref, w2t_ref[...], False, extent)
        xt_ref[...] = jnp.transpose(x_ref[...].astype(F32)).astype(BF16)

    pre, dh, xt, qg, w1t, w2t = call(
        inner,
        "inner_products",
        [image_f, image_f, turned_b, columns_b, taps_b, taps_b],
        "vvvv",
        (source, grad_out, w_one, w_two),
        scratch=[pltpu.VMEM(columns_b.shape, BF16)],
        flops=2 * conv,
    )

    def middle(edge_ref, corner_ref, pre_ref, dh_ref, xt_ref, qg_ref, w1_ref, w2t_ref, *refs):
        arrived = refs[:n_routes]
        keep_ref, send_ref, hid_ref, dpre_ref = refs[n_routes : n_routes + 4]
        outs = refs[n_routes + 4 : 2 * n_routes + 4]
        qd_ref, sum_ref = refs[2 * n_routes + 4 :]
        lines, pixels = seam_lines(edge_ref, corner_ref, extent)
        x_strips, g_strips = read_routes(plan, arrived, extent)
        columns = strip_columns(g_strips, extent)
        value, slope = gelu_parts(pre_ref[...] + margin_forward(x_strips, w1_ref[...], extent))
        hidden = value.astype(BF16)
        hid_ref[...] = hidden
        d_hidden = dh_ref[...] + margin_backward(columns, w2t_ref[...], lines, pixels, extent)
        d_pre = (d_hidden * slope).astype(BF16)
        dpre_ref[...] = d_pre
        a = gather_blocks(hidden, lines, pixels, extent)
        b = gather_blocks(d_pre, *fixed_lines(extent), extent)
        write_routes(a, b, plan, outs, extent)
        write_columns(qd_ref, d_pre, False, extent)
        weight_sum(sum_ref.at[0], xt_ref[...], qd_ref, x_strips, strip_columns(b, extent), extent)
        weight_sum(sum_ref.at[1], jnp.transpose(value).astype(BF16), qg_ref, a, columns, extent)
        core = lax.axis_index("dp") % 2
        keep_ref[...] = sum_ref[core]
        send_ref[...] = sum_ref[1 - core].astype(BF16)

    results = call(
        middle,
        "gradients",
        [taps_f, taps_b, image_b, image_b] + routed,
        "ss" + "v" * (6 + n_routes),
        (edge_code, corner_code, pre, dh, xt, qg, w_one, w2t, *first_arrived),
        scratch=[pltpu.VMEM(columns_b.shape, BF16), pltpu.VMEM((2,) + taps_f.shape, F32)],
        flops=2 * conv,
    )
    keep, send, hidden, d_pre = results[:4]
    second_arrived = exchange(results[4:], plan, tiles)

    def last(edge_ref, corner_ref, x_ref, g_ref, hid_ref, dpre_ref, w2_ref, w1t_ref, *refs):
        arrived = refs[:n_routes]
        out_ref, dx_ref, q_ref = refs[n_routes:]
        lines, pixels = seam_lines(edge_ref, corner_ref, extent)
        h_strips, d_strips = read_routes(plan, arrived, extent)
        write_columns(q_ref, hid_ref[...], True, extent)
        total = window_product(q_ref, w2_ref[...], True, extent) + margin_forward(h_strips, w2_ref[...], extent)
        out_ref[...] = (x_ref[...].astype(F32) + total).astype(BF16)
        write_columns(q_ref, dpre_ref[...], False, extent)
        total = window_product(q_ref, w1t_ref[...], False, extent)
        total = total + margin_backward(strip_columns(d_strips, extent), w1t_ref[...], lines, pixels, extent)
        dx_ref[...] = (g_ref[...].astype(F32) + total).astype(BF16)

    output, d_input = call(
        last,
        "outputs",
        [image_b, image_b],
        "ss" + "v" * (6 + n_routes),
        (edge_code, corner_code, source, grad_out, hidden, d_pre, w_two, w1t, *second_arrived),
        scratch=[pltpu.VMEM(columns_b.shape, BF16)],
        flops=2 * conv,
    )
    one, two = reduce_gradients(keep, send, tiles * members)
    shape = (9, channels, channels)
    return (
        output.reshape(inputs.shape),
        d_input.reshape(inputs.shape),
        (one.astype(F32) * factor).reshape(shape),
        (two.astype(F32) * factor).reshape(shape),
    )


def solution(mesh):
    split = P("dp", "tile", None, None, None)
    return jax.shard_map(
        per_device,
        mesh=mesh,
        in_specs=(split, P(), P(), split, P(), P()),
        out_specs=(split, split, P(), P()),
        check_vma=False,
    )
```

time: 297 us -> 68.9 us (0.23)
  waiting for transfers between devices: 133 us -> 22 us
  between operations: 33.7 us -> 0.83 us
  starting transfers between devices: 61 us -> 30.4 us
  local copies, waits for them, and re-layouts: 33.5 us -> 4.5 us
  matrix products: 21.6 us -> 0 us
  other arithmetic: 12.9 us -> 1.4 us
  Pallas kernels: 0 us -> 9.47 us
    psum x1 -> x0, waiting for transfers between devices: 127 us -> none  [per_device(): summed_one, summed_two = lax.psum((local_one, local_two), ('tile', 'dp'))]
    ppermute x32 -> x21, starting transfers between devices: 61 us -> 30.4 us  [the longest x10 17.8 us: exchange(): lax.ppermute(p, 'tile', [(i, (i + route[0]) % tiles) for i in range(tiles)])]
    dot_general x54 -> x0, matrix products: 21.6 us -> none  [the longest x36 11 us: convolve(): jnp.dot(piece, weights[3 * row_tap + col_tap], preferred_element_type=jnp...]
    ppermute x32 -> x21, waiting for transfers between devices: 5.57 us -> 22 us  [the longest x11 14.4 us: swap(): return lax.ppermute(value, AXES, [(i, i ^ mask) for i in range(total)])]
    reshape x20 -> x0, local copies, waits for them, and re-layouts: 11.6 us -> none  [the longest x18 11.5 us: convolve(): padded[:, row_tap:row_tap + extent, col_tap:col_tap + extent, :]]
    pallas_call x0 -> x4, Pallas kernels: none -> 9.47 us  [call(): pl.pallas_call(kernel, name=name, out_shape=outs, in_specs=specs, out_spe...]
    unnamed x83 -> x16, local copies, waits for them, and re-layouts: 10.8 us -> 4.44 us
    another operation x8 -> x1, other arithmetic: 4.8 us -> 0.04 us  [reduce_gradients(): ring = jnp.stack([mine] + [swap(mine, m << 1, total) for m in (1, 2, 3)])]
  transfers between devices with their start and end apart: 33 -> 21, of which waited for: 6 -> 12; matrix products, arithmetic and copies ran while one was open for 12% -> 0% of each run, Pallas kernels for 0% -> 7%
where the time goes in v1:
time: 68.9 us; the launch traced here: 68.6 us
  starting transfers between devices  30.4 us (44%)
  waiting for transfers between devices  22 us (32%)
  Pallas kernels  9.47 us (14%)
  local copies, waits for them, and re-layouts  4.5 us (7%)
  other arithmetic  1.4 us (2%)
  between operations  0.83 us (1%)
    ppermute x10, starting transfers between devices, exchange(): lax.ppermute(p, 'tile', [(i, (i + route[0]) % tiles) for i in range(tiles)])  17.8 us
    ppermute x11, waiting for transfers between devices, swap(): return lax.ppermute(value, AXES, [(i, i ^ mask) for i in range(total)])  14.4 us
    ppermute x11, starting transfers between devices, swap(): return lax.ppermute(value, AXES, [(i, i ^ mask) for i in range(total)])  12.6 us
    pallas_call x4, Pallas kernels, call(): pl.pallas_call(kernel, name=name, out_shape=outs, in_specs=specs, out_spe...  9.47 us
    ppermute x10, waiting for transfers between devices, exchange(): lax.ppermute(p, 'tile', [(i, (i + route[0]) % tiles) for i in range(tiles)])  7.59 us
    unnamed x16, local copies, waits for them, and re-layouts  4.44 us
  transfers between devices with their start and end apart: 21, of which 12 were waited for; matrix products, arithmetic and copies ran while one was open for 0% of the time, Pallas kernels for 7%

profile of v1, /device:TPU:0, one launch (start us, length us, event | category | flops | bytes accessed | tf_op | source)
XLA Modules:
  0.0 68.6 jit_solution(3747456124670766916)
XLA Ops:
  0.6 0.8 %copy.14.edge_ref = s32[8,4]{1,0:T(8,128)S(1)} copy(s32[8,4]{0,1:T(4,128)} %param.10) | data formatting | bytes 256 | tf_op args[4]
  2.2 0.9 %copy-done.1 = bf16[1,1,32,32,128]{4,3,2,1,0:T(8,128)(2,1)S(1)} copy-done((bf16[1,1,32,32,128]{4,3,2,1,0:T(8,128)(2,1)S(1)}, bf16[1,1,32,32,128]{4,3,2,1,0:T(8,128)(2,1)}, u32[]{:S(2)}) %copy-start.1) | copy-done | bytes 262168
  3.1 0.9 %copy-done.3 = bf16[1,1,32,32,128]{4,3,2,1,0:T(8,128)(2,1)S(1)} copy-done((bf16[1,1,32,32,128]{4,3,2,1,0:T(8,128)(2,1)S(1)}, bf16[1,1,32,32,128]{4,3,2,1,0:T(8,128)(2,1)}, u32[]{:S(2)}) %copy-start.3) | copy-done | bytes 262168
  4.1 1.1 %first_strips.1 = (bf16[128,128]{1,0:T(8,128)(2,1)S(1)}, bf16[64,128]{1,0:T(8,128)(2,1)S(1)}, bf16[64,128]{1,0:T(8,128)(2,1)S(1)}, bf16[16,128]{1,0:T(8,128)(2,1)S(1)}, bf16[16,128]{1,0:T(8,128)(2,1)S(1)}) custom-call(s32[8,4]{1,0:T(8,128)S(1)} %copy.14.edge_ref, s32[8,4]{1,0:T(8,128)S(1)} %copy.15.corner_ref, bf16[1024,128]{1,0:T(8,128)(2,1)S(1)} %bitcast.29, ...), custom_call_target="tpu_custom_call" | custom-call | bytes 598272 | tf_op jit(solution)/shard_map/first_strips/pallas_call | solution.py:300
  5.2 4.1 %collective-permute-start = (bf16[128,128]{1,0:T(8,128)(2,1)S(1)}, bf16[128,128]{1,0:T(8,128)(2,1)S(1)}, u32[]{:S(2)}, u32[]{:S(2)}) collective-permute-start(bf16[128,128]{1,0:T(8,128)(2,1)S(1)} %get-tuple-element.31), channel_id=1, source_target_pairs={{0,16},{4,20},{8,24},{12,28},{16,0},{20,4},{24,8},{28,12},{1,17},{... | collective-permute-start | bytes 98312 | tf_op jit(solution)/shard_map/ppermute | solution.py:318
  9.3 2.3 %collective-permute-start.1 = (bf16[64,128]{1,0:T(8,128)(2,1)S(1)}, bf16[64,128]{1,0:T(8,128)(2,1)S(1)}, u32[]{:S(2)}, u32[]{:S(2)}) collective-permute-start(bf16[64,128]{1,0:T(8,128)(2,1)S(1)} %get-tuple-element.32), channel_id=1, source_target_pairs={{0,28},{4,0},{8,4},{12,8},{16,12},{20,16},{24,20},{28,24},{1,29},{... | collective-permute-start | bytes 49160 | tf_op jit(solution)/shard_map/ppermute | solution.py:318
  11.6 1.9 %collective-permute-start.3 = (bf16[16,128]{1,0:T(8,128)(2,1)S(1)}, bf16[16,128]{1,0:T(8,128)(2,1)S(1)}, u32[]{:S(2)}, u32[]{:S(2)}) collective-permute-start(bf16[16,128]{1,0:T(8,128)(2,1)S(1)} %get-tuple-element.34), channel_id=1, source_target_pairs={{0,20},{4,24},{8,28},{12,0},{16,4},{20,8},{24,12},{28,16},{1,21},{... | collective-permute-start | bytes 12296 | tf_op jit(solution)/shard_map/ppermute | solution.py:318
  13.5 1.2 %collective-permute-start.4 = (bf16[16,128]{1,0:T(8,128)(2,1)S(1)}, bf16[16,128]{1,0:T(8,128)(2,1)S(1)}, u32[]{:S(2)}, u32[]{:S(2)}) collective-permute-start(bf16[16,128]{1,0:T(8,128)(2,1)S(1)} %get-tuple-element.35), channel_id=1, source_target_pairs={{0,12},{4,16},{8,20},{12,24},{16,28},{20,0},{24,4},{28,8},{1,13},{... | collective-permute-start | bytes 12296 | tf_op jit(solution)/shard_map/ppermute | solution.py:318
  14.7 1.0 %copy-done.5 = bf16[9,128,128]{2,1,0:T(8,128)(2,1)S(1)} copy-done((bf16[9,128,128]{2,1,0:T(8,128)(2,1)S(1)}, bf16[9,128,128]{2,1,0:T(8,128)(2,1)}, u32[]{:S(2)}) %copy-start.5) | copy-done | bytes 294936
  15.7 1.4 %inner_products.1 = (f32[1024,128]{1,0:T(8,128)S(1)}, f32[1024,128]{1,0:T(8,128)S(1)}, bf16[128,1024]{1,0:T(8,128)(2,1)S(1)}, bf16[1088,384]{1,0:T(8,128)(2,1)S(...) custom-call(bf16[1024,128]{1,0:T(8,128)(2,1)S(1)} %bitcast.30, bf16[1024,128]{1,0:T(8,128)(2,1)S(1)} %bitcast.33, ...), custom_call_target="tpu_custom_call" | custom-call | flops 603979776 | bytes 3850240 | tf_op jit(solution)/shard_map/inner_products/pallas_call | solution.py:300
  17.1 1.7 %collective-permute-done.4.refs_4_ = bf16[16,128]{1,0:T(8,128)(2,1)S(1)} collective-permute-done((bf16[16,128]{1,0:T(8,128)(2,1)S(1)}, bf16[16,128]{1,0:T(8,128)(2,1)S(1)}, u32[]{:S(2)}, u32[]{:S(2)}) %collective-permute-start.4) | collective-permute-done | bytes 4128 | tf_op jit(solution)/shard_map/ppermute | solution.py:318
  18.9 3.4 %gradients.1 = (f32[1152,128]{1,0:T(8,128)S(1)}, bf16[1152,128]{1,0:T(8,128)(2,1)S(1)}, bf16[1024,128]{1,0:T(8,128)(2,1)S(1)}, bf16[1024,128]{1,0:T(8,128)(2,1)S...) custom-call(s32[8,4]{1,0:T(8,128)S(1)} %copy.14.edge_ref, ...), custom_call_target="tpu_custom_call" | custom-call | flops 603979776 | bytes 4292864 | tf_op jit(solution)/shard_map/gradients/pallas_call | solution.py:300
  22.4 1.5 %collective-permute-done.10 = bf16[1152,128]{1,0:T(8,128)(2,1)S(1)} collective-permute-done((bf16[1152,128]{1,0:T(8,128)(2,1)S(1)}, bf16[1152,128]{1,0:T(8,128)(2,1)S(1)}, u32[]{:S(2)}, u32[]{:S(2)}) %collective-permute-start.10) | collective-permute-done | bytes 294944 | tf_op jit(solution)/shard_map/ppermute | solution.py:323
  24.1 2.6 %collective-permute-start.11 = (bf16[288,128]{1,0:T(8,128)(2,1)S(1)}, bf16[288,128]{1,0:T(8,128)(2,1)S(1)}, u32[]{:S(2)}, u32[]{:S(2)}) collective-permute-start(bf16[288,128]{1,0:T(8,128)(2,1)S(1)} %get-tuple-element.54), channel_id=1, source_target_pairs={{0,6},{1,7},{2,4},{3,5},{4,2},{5,3},{6,0},{7,1},{8,14},{9,15},{10,... | collective-permute-start | bytes 221192 | tf_op jit(solution)/shard_map/ppermute | solution.py:323
  27.6 1.8 %collective-permute-done.11 = bf16[288,128]{1,0:T(8,128)(2,1)S(1)} collective-permute-done((bf16[288,128]{1,0:T(8,128)(2,1)S(1)}, bf16[288,128]{1,0:T(8,128)(2,1)S(1)}, u32[]{:S(2)}, u32[]{:S(2)}) %collective-permute-start.11) | collective-permute-done | bytes 73760 | tf_op jit(solution)/shard_map/ppermute | solution.py:323
  29.4 1.6 %collective-permute-done.12 = bf16[288,128]{1,0:T(8,128)(2,1)S(1)} collective-permute-done((bf16[288,128]{1,0:T(8,128)(2,1)S(1)}, bf16[288,128]{1,0:T(8,128)(2,1)S(1)}, u32[]{:S(2)}, u32[]{:S(2)}) %collective-permute-start.12) | collective-permute-done | bytes 73760 | tf_op jit(solution)/shard_map/ppermute | solution.py:323
  31.5 2.9 %collective-permute-start.14 = (bf16[288,128]{1,0:T(8,128)(2,1)S(1)}, bf16[288,128]{1,0:T(8,128)(2,1)S(1)}, u32[]{:S(2)}, u32[]{:S(2)}) collective-permute-start(bf16[288,128]{1,0:T(8,128)(2,1)S(1)} %fusion.2), channel_id=1, source_target_pairs={{0,8},{1,9},{2,10},{3,11},{4,12},{5,13},{6,14},{7,15},{8,0},{9,1},... | collective-permute-start | bytes 221192 | tf_op jit(solution)/shard_map/ppermute | solution.py:323
  34.5 0.8 %collective-permute-start.15 = (bf16[288,128]{1,0:T(8,128)(2,1)S(1)}, bf16[288,128]{1,0:T(8,128)(2,1)S(1)}, u32[]{:S(2)}, u32[]{:S(2)}) collective-permute-start(bf16[288,128]{1,0:T(8,128)(2,1)S(1)} %fusion.2), channel_id=1, source_target_pairs={{0,16},{1,17},{2,18},{3,19},{4,20},{5,21},{6,22},{7,23},{8,24},{9,... | collective-permute-start | bytes 221192 | tf_op jit(solution)/shard_map/ppermute | solution.py:323
  35.2 1.7 %collective-permute-start.16 = (bf16[288,128]{1,0:T(8,128)(2,1)S(1)}, bf16[288,128]{1,0:T(8,128)(2,1)S(1)}, u32[]{:S(2)}, u32[]{:S(2)}) collective-permute-start(bf16[288,128]{1,0:T(8,128)(2,1)S(1)} %fusion.2), channel_id=1, source_target_pairs={{0,24},{1,25},{2,26},{3,27},{4,28},{5,29},{6,30},{7,31},{8,16},{9,... | collective-permute-start | bytes 221192 | tf_op jit(solution)/shard_map/ppermute | solution.py:323
  37.0 5.3 %collective-permute-done.15 = bf16[288,128]{1,0:T(8,128)(2,1)S(1)} collective-permute-done((bf16[288,128]{1,0:T(8,128)(2,1)S(1)}, bf16[288,128]{1,0:T(8,128)(2,1)S(1)}, u32[]{:S(2)}, u32[]{:S(2)}) %collective-permute-start.15) | collective-permute-done | bytes 73760 | tf_op jit(solution)/shard_map/ppermute | solution.py:323
  43.1 1.1 %collective-permute-start.18 = (bf16[288,128]{1,0:T(8,128)(2,1)S(1)}, bf16[288,128]{1,0:T(8,128)(2,1)S(1)}, u32[]{:S(2)}, u32[]{:S(2)}) collective-permute-start(bf16[288,128]{1,0:T(8,128)(2,1)S(1)} %add_convert_fusion), channel_id=1, source_target_pairs={{0,4},{1,5},{2,6},{3,7},{4,0},{5,1},{6,2},{7,3},{8,12},{9,13},{10,... | collective-permute-start | bytes 221192 | tf_op jit(solution)/shard_map/ppermute | solution.py:323
  44.2 1.7 %collective-permute-start.19 = (bf16[288,128]{1,0:T(8,128)(2,1)S(1)}, bf16[288,128]{1,0:T(8,128)(2,1)S(1)}, u32[]{:S(2)}, u32[]{:S(2)}) collective-permute-start(bf16[288,128]{1,0:T(8,128)(2,1)S(1)} %add_convert_fusion), channel_id=1, source_target_pairs={{0,6},{1,7},{2,4},{3,5},{4,2},{5,3},{6,0},{7,1},{8,14},{9,15},{10,... | collective-permute-start | bytes 221192 | tf_op jit(solution)/shard_map/ppermute | solution.py:323
  46.0 1.1 %collective-permute-done.17 = bf16[288,128]{1,0:T(8,128)(2,1)S(1)} collective-permute-done((bf16[288,128]{1,0:T(8,128)(2,1)S(1)}, bf16[288,128]{1,0:T(8,128)(2,1)S(1)}, u32[]{:S(2)}, u32[]{:S(2)}) %collective-permute-start.17) | collective-permute-done | bytes 73760 | tf_op jit(solution)/shard_map/ppermute | solution.py:323
  47.5 2.0 %collective-permute-done.19 = bf16[288,128]{1,0:T(8,128)(2,1)S(1)} collective-permute-done((bf16[288,128]{1,0:T(8,128)(2,1)S(1)}, bf16[288,128]{1,0:T(8,128)(2,1)S(1)}, u32[]{:S(2)}, u32[]{:S(2)}) %collective-permute-start.19) | collective-permute-done | bytes 73760 | tf_op jit(solution)/shard_map/ppermute | solution.py:323
  49.7 2.0 %collective-permute-start.5 = (bf16[128,128]{1,0:T(8,128)(2,1)S(1)}, bf16[128,128]{1,0:T(8,128)(2,1)S(1)}, u32[]{:S(2)}, u32[]{:S(2)}) collective-permute-start(bf16[128,128]{1,0:T(8,128)(2,1)S(1)} %get-tuple-element.39), channel_id=1, source_target_pairs={{0,16},{4,20},{8,24},{12,28},{16,0},{20,4},{24,8},{28,12},{1,17},{... | collective-permute-start | bytes 98312 | tf_op jit(solution)/shard_map/ppermute | solution.py:318
  51.7 2.1 %collective-permute-start.6 = (bf16[64,128]{1,0:T(8,128)(2,1)S(1)}, bf16[64,128]{1,0:T(8,128)(2,1)S(1)}, u32[]{:S(2)}, u32[]{:S(2)}) collective-permute-start(bf16[64,128]{1,0:T(8,128)(2,1)S(1)} %get-tuple-element.40), channel_id=1, source_target_pairs={{0,28},{4,0},{8,4},{12,8},{16,12},{20,16},{24,20},{28,24},{1,29},{... | collective-permute-start | bytes 49160 | tf_op jit(solution)/shard_map/ppermute | solution.py:318
  53.9 2.1 %collective-permute-start.8 = (bf16[16,128]{1,0:T(8,128)(2,1)S(1)}, bf16[16,128]{1,0:T(8,128)(2,1)S(1)}, u32[]{:S(2)}, u32[]{:S(2)}) collective-permute-start(bf16[16,128]{1,0:T(8,128)(2,1)S(1)} %get-tuple-element.42), channel_id=1, source_target_pairs={{0,20},{4,24},{8,28},{12,0},{16,4},{20,8},{24,12},{28,16},{1,21},{... | collective-permute-start | bytes 12296 | tf_op jit(solution)/shard_map/ppermute | solution.py:318
  56.0 2.4 %collective-permute-done.8.refs_3_ = bf16[16,128]{1,0:T(8,128)(2,1)S(1)} collective-permute-done((bf16[16,128]{1,0:T(8,128)(2,1)S(1)}, bf16[16,128]{1,0:T(8,128)(2,1)S(1)}, u32[]{:S(2)}, u32[]{:S(2)}) %collective-permute-start.8) | collective-permute-done | bytes 4128 | tf_op jit(solution)/shard_map/ppermute | solution.py:318
  58.4 2.0 %collective-permute-start.9 = (bf16[16,128]{1,0:T(8,128)(2,1)S(1)}, bf16[16,128]{1,0:T(8,128)(2,1)S(1)}, u32[]{:S(2)}, u32[]{:S(2)}) collective-permute-start(bf16[16,128]{1,0:T(8,128)(2,1)S(1)} %get-tuple-element.43), channel_id=1, source_target_pairs={{0,12},{4,16},{8,20},{12,24},{16,28},{20,0},{24,4},{28,8},{1,13},{... | collective-permute-start | bytes 12296 | tf_op jit(solution)/shard_map/ppermute | solution.py:318
  60.3 3.5 %collective-permute-done.9.refs_4_ = bf16[16,128]{1,0:T(8,128)(2,1)S(1)} collective-permute-done((bf16[16,128]{1,0:T(8,128)(2,1)S(1)}, bf16[16,128]{1,0:T(8,128)(2,1)S(1)}, u32[]{:S(2)}, u32[]{:S(2)}) %collective-permute-start.9) | collective-permute-done | bytes 4128 | tf_op jit(solution)/shard_map/ppermute | solution.py:318
  63.8 3.6 %outputs.1 = (bf16[1024,128]{1,0:T(8,128)(2,1)}, bf16[1024,128]{1,0:T(8,128)(2,1)}) custom-call(s32[8,4]{1,0:T(8,128)S(1)} %copy.14.edge_ref, s32[8,4]{1,0:T(8,128)S(1)} %copy.15.corner_ref, bf16[1024,128]{1,0:T(8,128)(2,1)S(1)} %bitcast.31, bf16[1024,128]{1,0:T(8,128)(2,1)S(1)} %bitcast.34, bf16[1024,128]{1,0:T(8,128)(2,1)S(1)} %get-tuple-element.36.hid_ref, ...), custom_call_target="tpu_custom_call" | custom-call | flops 603979776 | bytes 2236672 | tf_op jit(solution)/shard_map/outputs/pallas_call | solution.py:300
  67.4 1.1 %convert_multiply_fusion = (f32[4,288,128]{2,1,0:T(8,128)}, f32[4,288,128]{2,1,0:T(8,128)}) fusion(bf16[4,288,128]{2,1,0:T(8,128)(2,1)S(1)} %collective-permute-done.20, pred[]{:T(512)S(6)} %eq.3, bf16[1,288,128]{2,1,0:T(8,128)(2,1)S(1)} %get-tuple-element.51, bf16[1,288,128]{2,1,0:T(8,128)(2,1)S(1)} %get-tuple-element.52, ...), kind=kLoop, calls=%fused_computation | loop fusion | flops 1327104 | bytes 1769473 | tf_op jit(solution)/shard_map/mul | solution.py:467
  (39 shorter events, 4.0 us)
Async XLA Ops:
  0.6 14.1 %copy-start = (bf16[9,128,128]{2,1,0:T(8,128)(2,1)S(1)}, bf16[9,128,128]{2,1,0:T(8,128)(2,1)}, u32[]{:S(2)}) copy-start(bf16[9,128,128]{2,1,0:T(8,128)(2,1)} %param.7) | copy-start | bytes 884740
  2.2 0.9 %copy-start.1 = (bf16[1,1,32,32,128]{4,3,2,1,0:T(8,128)(2,1)S(1)}, bf16[1,1,32,32,128]{4,3,2,1,0:T(8,128)(2,1)}, u32[]{:S(2)}) copy-start(bf16[1,1,32,32,128]{4,3,2,1,0:T(8,128)(2,1)} %param.6) | copy-start | bytes 786436
  3.1 0.9 %copy-start.3 = (bf16[1,1,32,32,128]{4,3,2,1,0:T(8,128)(2,1)S(1)}, bf16[1,1,32,32,128]{4,3,2,1,0:T(8,128)(2,1)}, u32[]{:S(2)}) copy-start(bf16[1,1,32,32,128]{4,3,2,1,0:T(8,128)(2,1)} %param.9) | copy-start | bytes 786436
  5.2 13.7 %collective-permute-start = (bf16[128,128]{1,0:T(8,128)(2,1)S(1)}, bf16[128,128]{1,0:T(8,128)(2,1)S(1)}, u32[]{:S(2)}, u32[]{:S(2)}) collective-permute-start(bf16[128,128]{1,0:T(8,128)(2,1)S(1)} %get-tuple-element.31), channel_id=1, source_target_pairs={{0,16},{4,20},{8,24},{12,28},{16,0},{20,4},{24,8},{28,12},{1,17},{... | collective-permute-start | bytes 98312 | tf_op jit(solution)/shard_map/ppermute | solution.py:318
  9.3 9.6 %collective-permute-start.1 = (bf16[64,128]{1,0:T(8,128)(2,1)S(1)}, bf16[64,128]{1,0:T(8,128)(2,1)S(1)}, u32[]{:S(2)}, u32[]{:S(2)}) collective-permute-start(bf16[64,128]{1,0:T(8,128)(2,1)S(1)} %get-tuple-element.32), channel_id=1, source_target_pairs={{0,28},{4,0},{8,4},{12,8},{16,12},{20,16},{24,20},{28,24},{1,29},{... | collective-permute-start | bytes 49160 | tf_op jit(solution)/shard_map/ppermute | solution.py:318
  11.6 7.3 %collective-permute-start.2 = (bf16[64,128]{1,0:T(8,128)(2,1)S(1)}, bf16[64,128]{1,0:T(8,128)(2,1)S(1)}, u32[]{:S(2)}, u32[]{:S(2)}) collective-permute-start(bf16[64,128]{1,0:T(8,128)(2,1)S(1)} %get-tuple-element.33), channel_id=1, source_target_pairs={{0,4},{4,8},{8,12},{12,16},{16,20},{20,24},{24,28},{28,0},{1,5},{5... | collective-permute-start | bytes 49160 | tf_op jit(solution)/shard_map/ppermute | solution.py:318
  11.6 5.6 %collective-permute-start.3 = (bf16[16,128]{1,0:T(8,128)(2,1)S(1)}, bf16[16,128]{1,0:T(8,128)(2,1)S(1)}, u32[]{:S(2)}, u32[]{:S(2)}) collective-permute-start(bf16[16,128]{1,0:T(8,128)(2,1)S(1)} %get-tuple-element.34), channel_id=1, source_target_pairs={{0,20},{4,24},{8,28},{12,0},{16,4},{20,8},{24,12},{28,16},{1,21},{... | collective-permute-start | bytes 12296 | tf_op jit(solution)/shard_map/ppermute | solution.py:318
  13.5 5.4 %collective-permute-start.4 = (bf16[16,128]{1,0:T(8,128)(2,1)S(1)}, bf16[16,128]{1,0:T(8,128)(2,1)S(1)}, u32[]{:S(2)}, u32[]{:S(2)}) collective-permute-start(bf16[16,128]{1,0:T(8,128)(2,1)S(1)} %get-tuple-element.35), channel_id=1, source_target_pairs={{0,12},{4,16},{8,20},{12,24},{16,28},{20,0},{24,4},{28,8},{1,13},{... | collective-permute-start | bytes 12296 | tf_op jit(solution)/shard_map/ppermute | solution.py:318
  14.7 1.0 %copy-start.5 = (bf16[9,128,128]{2,1,0:T(8,128)(2,1)S(1)}, bf16[9,128,128]{2,1,0:T(8,128)(2,1)}, u32[]{:S(2)}) copy-start(bf16[9,128,128]{2,1,0:T(8,128)(2,1)} %param.8) | copy-start | bytes 884740
  22.3 1.6 %collective-permute-start.10 = (bf16[1152,128]{1,0:T(8,128)(2,1)S(1)}, bf16[1152,128]{1,0:T(8,128)(2,1)S(1)}, u32[]{:S(2)}, u32[]{:S(2)}) collective-permute-start(bf16[1152,128]{1,0:T(8,128)(2,1)S(1)} %get-tuple-element.47), channel_id=1, source_target_pairs={{0,1},{1,0},{2,3},{3,2},{4,5},{5,4},{6,7},{7,6},{8,9},{9,8},{10,11... | collective-permute-start | bytes 884744 | tf_op jit(solution)/shard_map/ppermute | solution.py:323
  24.1 5.3 %collective-permute-start.11 = (bf16[288,128]{1,0:T(8,128)(2,1)S(1)}, bf16[288,128]{1,0:T(8,128)(2,1)S(1)}, u32[]{:S(2)}, u32[]{:S(2)}) collective-permute-start(bf16[288,128]{1,0:T(8,128)(2,1)S(1)} %get-tuple-element.54), channel_id=1, source_target_pairs={{0,6},{1,7},{2,4},{3,5},{4,2},{5,3},{6,0},{7,1},{8,14},{9,15},{10,... | collective-permute-start | bytes 221192 | tf_op jit(solution)/shard_map/ppermute | solution.py:323
  26.6 4.4 %collective-permute-start.12 = (bf16[288,128]{1,0:T(8,128)(2,1)S(1)}, bf16[288,128]{1,0:T(8,128)(2,1)S(1)}, u32[]{:S(2)}, u32[]{:S(2)}) collective-permute-start(bf16[288,128]{1,0:T(8,128)(2,1)S(1)} %get-tuple-element.56), channel_id=1, source_target_pairs={{0,2},{1,3},{2,0},{3,1},{4,6},{5,7},{6,4},{7,5},{8,10},{9,11},{10,... | collective-permute-start | bytes 221192 | tf_op jit(solution)/shard_map/ppermute | solution.py:323
  27.1 4.4 %collective-permute-start.13 = (bf16[288,128]{1,0:T(8,128)(2,1)S(1)}, bf16[288,128]{1,0:T(8,128)(2,1)S(1)}, u32[]{:S(2)}, u32[]{:S(2)}) collective-permute-start(bf16[288,128]{1,0:T(8,128)(2,1)S(1)} %get-tuple-element.55), channel_id=1, source_target_pairs={{0,4},{1,5},{2,6},{3,7},{4,0},{5,1},{6,2},{7,3},{8,12},{9,13},{10,... | collective-permute-start | bytes 221192 | tf_op jit(solution)/shard_map/ppermute | solution.py:323
  31.5 5.5 %collective-permute-start.14 = (bf16[288,128]{1,0:T(8,128)(2,1)S(1)}, bf16[288,128]{1,0:T(8,128)(2,1)S(1)}, u32[]{:S(2)}, u32[]{:S(2)}) collective-permute-start(bf16[288,128]{1,0:T(8,128)(2,1)S(1)} %fusion.2), channel_id=1, source_target_pairs={{0,8},{1,9},{2,10},{3,11},{4,12},{5,13},{6,14},{7,15},{8,0},{9,1},... | collective-permute-start | bytes 221192 | tf_op jit(solution)/shard_map/ppermute | solution.py:323
  34.5 7.9 %collective-permute-start.15 = (bf16[288,128]{1,0:T(8,128)(2,1)S(1)}, bf16[288,128]{1,0:T(8,128)(2,1)S(1)}, u32[]{:S(2)}, u32[]{:S(2)}) collective-permute-start(bf16[288,128]{1,0:T(8,128)(2,1)S(1)} %fusion.2), channel_id=1, source_target_pairs={{0,16},{1,17},{2,18},{3,19},{4,20},{5,21},{6,22},{7,23},{8,24},{9,... | collective-permute-start | bytes 221192 | tf_op jit(solution)/shard_map/ppermute | solution.py:323
  35.2 7.1 %collective-permute-start.16 = (bf16[288,128]{1,0:T(8,128)(2,1)S(1)}, bf16[288,128]{1,0:T(8,128)(2,1)S(1)}, u32[]{:S(2)}, u32[]{:S(2)}) collective-permute-start(bf16[288,128]{1,0:T(8,128)(2,1)S(1)} %fusion.2), channel_id=1, source_target_pairs={{0,24},{1,25},{2,26},{3,27},{4,28},{5,29},{6,30},{7,31},{8,16},{9,... | collective-permute-start | bytes 221192 | tf_op jit(solution)/shard_map/ppermute | solution.py:323
  42.4 4.7 %collective-permute-start.17 = (bf16[288,128]{1,0:T(8,128)(2,1)S(1)}, bf16[288,128]{1,0:T(8,128)(2,1)S(1)}, u32[]{:S(2)}, u32[]{:S(2)}) collective-permute-start(bf16[288,128]{1,0:T(8,128)(2,1)S(1)} %add_convert_fusion), channel_id=1, source_target_pairs={{0,2},{1,3},{2,0},{3,1},{4,6},{5,7},{6,4},{7,5},{8,10},{9,11},{10,... | collective-permute-start | bytes 221192 | tf_op jit(solution)/shard_map/ppermute | solution.py:323
  43.1 4.4 %collective-permute-start.18 = (bf16[288,128]{1,0:T(8,128)(2,1)S(1)}, bf16[288,128]{1,0:T(8,128)(2,1)S(1)}, u32[]{:S(2)}, u32[]{:S(2)}) collective-permute-start(bf16[288,128]{1,0:T(8,128)(2,1)S(1)} %add_convert_fusion), channel_id=1, source_target_pairs={{0,4},{1,5},{2,6},{3,7},{4,0},{5,1},{6,2},{7,3},{8,12},{9,13},{10,... | collective-permute-start | bytes 221192 | tf_op jit(solution)/shard_map/ppermute | solution.py:323
  44.2 5.3 %collective-permute-start.19 = (bf16[288,128]{1,0:T(8,128)(2,1)S(1)}, bf16[288,128]{1,0:T(8,128)(2,1)S(1)}, u32[]{:S(2)}, u32[]{:S(2)}) collective-permute-start(bf16[288,128]{1,0:T(8,128)(2,1)S(1)} %add_convert_fusion), channel_id=1, source_target_pairs={{0,6},{1,7},{2,4},{3,5},{4,2},{5,3},{6,0},{7,1},{8,14},{9,15},{10,... | collective-permute-start | bytes 221192 | tf_op jit(solution)/shard_map/ppermute | solution.py:323
  49.5 14.3 %copy-start.6 = (bf16[9,128,128]{2,1,0:T(8,128)(2,1)S(1)}, bf16[9,128,128]{2,1,0:T(8,128)(2,1)}, u32[]{:S(2)}) copy-start(bf16[9,128,128]{2,1,0:T(8,128)(2,1)} %param.8) | copy-start | bytes 884740
  49.6 14.2 %copy-start.2 = (bf16[1,1,32,32,128]{4,3,2,1,0:T(8,128)(2,1)S(1)}, bf16[1,1,32,32,128]{4,3,2,1,0:T(8,128)(2,1)}, u32[]{:S(2)}) copy-start(bf16[1,1,32,32,128]{4,3,2,1,0:T(8,128)(2,1)} %param.6) | copy-start | bytes 786436
  49.6 14.2 %copy-start.4 = (bf16[1,1,32,32,128]{4,3,2,1,0:T(8,128)(2,1)S(1)}, bf16[1,1,32,32,128]{4,3,2,1,0:T(8,128)(2,1)}, u32[]{:S(2)}) copy-start(bf16[1,1,32,32,128]{4,3,2,1,0:T(8,128)(2,1)} %param.9) | copy-start | bytes 786436
  49.6 17.8 %collective-permute-start.20 = (bf16[4,288,128]{2,1,0:T(8,128)(2,1)S(1)}, bf16[4,288,128]{2,1,0:T(8,128)(2,1)S(1)}, u32[]{:S(2)}, u32[]{:S(2)}) collective-permute-start(bf16[4,288,128]{2,1,0:T(8,128)(2,1)S(1)} %pad_maximum_fusion.1), channel_id=1, source_target_pairs={{0,1},{1,0},{2,3},{3,2},{4,5},{5,4},{6,7},{7,6},{8,9},{9,8},{10,11... | collective-permute-start | bytes 884744 | tf_op jit(solution)/shard_map/ppermute | solution.py:323
  49.7 14.1 %collective-permute-start.5 = (bf16[128,128]{1,0:T(8,128)(2,1)S(1)}, bf16[128,128]{1,0:T(8,128)(2,1)S(1)}, u32[]{:S(2)}, u32[]{:S(2)}) collective-permute-start(bf16[128,128]{1,0:T(8,128)(2,1)S(1)} %get-tuple-element.39), channel_id=1, source_target_pairs={{0,16},{4,20},{8,24},{12,28},{16,0},{20,4},{24,8},{28,12},{1,17},{... | collective-permute-start | bytes 98312 | tf_op jit(solution)/shard_map/ppermute | solution.py:318
  51.7 12.1 %collective-permute-start.6 = (bf16[64,128]{1,0:T(8,128)(2,1)S(1)}, bf16[64,128]{1,0:T(8,128)(2,1)S(1)}, u32[]{:S(2)}, u32[]{:S(2)}) collective-permute-start(bf16[64,128]{1,0:T(8,128)(2,1)S(1)} %get-tuple-element.40), channel_id=1, source_target_pairs={{0,28},{4,0},{8,4},{12,8},{16,12},{20,16},{24,20},{28,24},{1,29},{... | collective-permute-start | bytes 49160 | tf_op jit(solution)/shard_map/ppermute | solution.py:318
  53.9 9.9 %collective-permute-start.7 = (bf16[64,128]{1,0:T(8,128)(2,1)S(1)}, bf16[64,128]{1,0:T(8,128)(2,1)S(1)}, u32[]{:S(2)}, u32[]{:S(2)}) collective-permute-start(bf16[64,128]{1,0:T(8,128)(2,1)S(1)} %get-tuple-element.41), channel_id=1, source_target_pairs={{0,4},{4,8},{8,12},{12,16},{16,20},{20,24},{24,28},{28,0},{1,5},{5... | collective-permute-start | bytes 49160 | tf_op jit(solution)/shard_map/ppermute | solution.py:318
  53.9 4.5 %collective-permute-start.8 = (bf16[16,128]{1,0:T(8,128)(2,1)S(1)}, bf16[16,128]{1,0:T(8,128)(2,1)S(1)}, u32[]{:S(2)}, u32[]{:S(2)}) collective-permute-start(bf16[16,128]{1,0:T(8,128)(2,1)S(1)} %get-tuple-element.42), channel_id=1, source_target_pairs={{0,20},{4,24},{8,28},{12,0},{16,4},{20,8},{24,12},{28,16},{1,21},{... | collective-permute-start | bytes 12296 | tf_op jit(solution)/shard_map/ppermute | solution.py:318
  58.4 5.4 %collective-permute-start.9 = (bf16[16,128]{1,0:T(8,128)(2,1)S(1)}, bf16[16,128]{1,0:T(8,128)(2,1)S(1)}, u32[]{:S(2)}, u32[]{:S(2)}) collective-permute-start(bf16[16,128]{1,0:T(8,128)(2,1)S(1)} %get-tuple-element.43), channel_id=1, source_target_pairs={{0,12},{4,16},{8,20},{12,24},{16,28},{20,0},{24,4},{28,8},{1,13},{... | collective-permute-start | bytes 12296 | tf_op jit(solution)/shard_map/ppermute | solution.py:318

commit v2 on v1

--- a/solution.py
+++ b/solution.py
@@ -163,6 +163,61 @@
     return result
 
 
+def relayed(tiles):
+    return tiles == 8
+
+
+def write_relay(a_blocks, b_blocks, near_ref, far_ref, extent):
+    for i, block in enumerate((a_blocks[2], a_blocks[3], b_blocks[2], b_blocks[3])):
+        near_ref[i * extent : (i + 1) * extent, :] = block
+    for i, block in enumerate((a_blocks[0], a_blocks[1], b_blocks[0], b_blocks[1])):
+        far_ref[i * extent : (i + 1) * extent, :] = block[:extent]
+    rows = iota((16, 1), 0)
+    tile = jnp.zeros((16, near_ref.shape[1]), F32)
+    at = 0
+    for blocks in (a_blocks, b_blocks):
+        ends = [blocks[i][extent : extent + 16].astype(F32) for i in range(2)]
+        for block, row in ((0, 0), (0, 1), (1, 1), (1, 0)):
+            tile = jnp.where(rows == at, ends[block][row : row + 1], tile)
+            at += 1
+    near_ref[4 * extent : 4 * extent + 16, :] = tile.astype(BF16)
+
+
+def read_relay(refs, extent):
+    across, one, three, far, opposite = refs
+    mine = lax.axis_index("tile")
+    left = mine % 2 == 0
+    even = (mine // 2) % 2 == 0
+
+    def pick(first, second, start, count):
+        whole = [r[start : start + count, :].astype(F32) for r in (across, one, three)]
+        above = jnp.where(even, whole[1], whole[2])
+        below = jnp.where(even, whole[2], whole[1])
+        return jnp.where(left, {"across": whole[0], "above": above, "below": below}[first], {"across": whole[0], "above": above, "below": below}[second])
+
+    def side(i, first, second):
+        return pick(first, second, i * extent, extent).astype(BF16)
+
+    a_east, b_west = side(0, "across", "above"), side(3, "across", "above")
+    a_west, b_east = side(1, "below", "across"), side(2, "below", "across")
+    beside = pick("above", "below", 4 * extent, 16)
+    beyond = opposite[0:16, :].astype(F32)
+    third = jnp.where(left, beside, beyond)
+    fifth = jnp.where(left, beyond, beside)
+    corners = {("a", 0): third[0:1], ("a", 3): third[3:4], ("b", 1): third[5:6], ("b", 2): third[6:7]}
+    corners.update({("a", 1): fifth[1:2], ("a", 2): fifth[2:3], ("b", 0): fifth[4:5], ("b", 3): fifth[7:8]})
+    rows = iota((16, 1), 0)
+    result = []
+    for kind, first, east, west in (("a", 0, a_east, a_west), ("b", 2, b_east, b_west)):
+        blocks = []
+        for i, ends in enumerate(((0, 1), (3, 2))):
+            tile = jnp.where(rows == 0, corners[(kind, ends[0])], jnp.where(rows == 1, corners[(kind, ends[1])], 0.0))
+            strip = far[(first + i) * extent : (first + i + 1) * extent, :]
+            blocks.append(jnp.concatenate([strip, tile.astype(BF16)], axis=0))
+        result.append(blocks + [east, west])
+    return result
+
+
 def shifted(image, by, extent):
     if by == 0:
         return image
@@ -323,25 +378,41 @@
     return lax.ppermute(value, AXES, [(i, i ^ mask) for i in range(total)])
 
 
-def reduce_gradients(keep, send, total):
+def reduce_gradients(keep, send, total, near=None, far=None):
     rows, channels = keep.shape
+    quarter = rows // 4
     wire = BF16 if total <= 32 else F32
     me = lax.axis_index(AXES)
     own = keep + swap(send, 1, total).astype(F32)
     plane = (me >> 1) & 3
-    parts = own.reshape(4, rows // 4, channels)
+    parts = own.reshape(4, quarter, channels)
     sent = parts.astype(wire)
-    arrived = [
-        swap(lax.dynamic_index_in_dim(sent, plane ^ m, 0, keepdims=False), m << 1, total).astype(F32) for m in (3, 1, 2)
-    ]
+    arrived = {}
+    for m in (3, 1, 2):
+        message = lax.dynamic_index_in_dim(sent, plane ^ m, 0, keepdims=False)
+        if m == 2 and near is not None:
+            message = jnp.concatenate([message, near], axis=0)
+        arrived[m] = swap(message, m << 1, total)
     part = lax.dynamic_index_in_dim(parts, plane, 0, keepdims=False)
-    part = part + arrived[0] + arrived[1] + arrived[2]
+    for m in (3, 1, 2):
+        part = part + arrived[m][:quarter].astype(F32)
+    extras = None
+    if near is not None:
+        across = arrived[2][quarter:]
+        riders = {1: (across,), 2: (far, across[-16:]), 3: (across,)}
     bit = 8
     while bit < total:
         mine = part.astype(wire)
         if 2 * bit < total:
-            far, middle, near = [swap(mine, m * bit, total).astype(F32) for m in (3, 2, 1)]
-            part = (mine.astype(F32) + near) + (middle + far)
+            got = {}
+            for m in (3, 2, 1):
+                message = mine
+                if near is not None:
+                    message = jnp.concatenate([mine, *riders[m]], axis=0)
+                got[m] = swap(message, m * bit, total)
+            part = (mine.astype(F32) + got[1][:quarter].astype(F32)) + (got[2][:quarter].astype(F32) + got[3][:quarter].astype(F32))
+            if near is not None:
+                extras = [across, got[1][quarter:], got[3][quarter:], got[2][quarter:-16], got[2][-16:]]
             bit *= 4
         else:
             part = mine.astype(F32) + swap(mine, bit, total).astype(F32)
@@ -349,9 +420,25 @@
     mine = part.astype(wire)
     ring = jnp.stack([mine] + [swap(mine, m << 1, total) for m in (1, 2, 3)])
     whole = jnp.concatenate([lax.dynamic_index_in_dim(ring, plane ^ j, 0) for j in range(4)], axis=0)
+    return whole, extras
+
+
+def join_cores(whole, total):
     other = swap(whole, 1, total)
-    first = (me & 1) == 0
-    return jnp.where(first, whole, other), jnp.where(first, other, whole)
+    low = (lax.axis_index(AXES) & 1) == 0
+    return jnp.where(low, whole, other), jnp.where(low, other, whole)
+
+
+def relay(near, far, total):
+    across = swap(near, 4, total)
+    three = swap(across, 24, total)
+    two = swap(jnp.concatenate([far, across[-16:]], axis=0), 16, total)
+    one = swap(across, 8, total)
+    return [across, one, three, two[:-16], two[-16:]]
+
+
+def relay_direct(near, far, total):
+    return [swap(near, 4, total), swap(near, 12, total), swap(near, 28, total), swap(far, 16, total), swap(near[-16:], 20, total)]
 
 
 def per_device(inputs, weight_one, weight_two, cotangent, edge_code, corner_code):
@@ -364,8 +451,25 @@
     w_one = weight_one.reshape(9 * channels, channels)
     w_two = weight_two.reshape(9 * channels, channels)
     plan = routes(tiles)
-    routed = [sds((route_rows(r, extent), channels), BF16) for r in plan]
-    n_routes = len(plan)
+    total = tiles * members
+    hops = relayed(tiles)
+    if hops:
+        routed = [sds((4 * extent + 16, channels), BF16), sds((4 * extent, channels), BF16)]
+        n_routes = 5
+    else:
+        routed = [sds((route_rows(r, extent), channels), BF16) for r in plan]
+        n_routes = len(plan)
+    n_routed = len(routed)
+
+    def write(a, b, outs):
+        if hops:
+            write_relay(a, b, *outs, extent)
+        else:
+            write_routes(a, b, plan, outs, extent)
+
+    def read(refs):
+        return read_relay(refs, extent) if hops else read_routes(plan, refs, extent)
+
     image_b, image_f = sds((count, channels), BF16), sds((count, channels), F32)
     columns_b = sds((count + 2 * extent, 3 * channels), BF16)
     taps_b, taps_f = sds((9 * channels, channels), BF16), sds((9 * channels, channels), F32)
@@ -376,10 +480,10 @@
         lines, pixels = seam_lines(edge_ref, corner_ref, extent)
         a = gather_blocks(x_ref[...], lines, pixels, extent)
         b = gather_blocks(g_ref[...], *fixed_lines(extent), extent)
-        write_routes(a, b, plan, outs, extent)
+        write(a, b, outs)
 
     first = call(first_strips, "first_strips", routed, "ssvv", (edge_code, corner_code, source, grad_out))
-    first_arrived = exchange(first, plan, tiles)
+    first_arrived = relay(*first, total) if hops else exchange(first, plan, tiles)
 
     def inner(x_ref, g_ref, w1_ref, w2_ref, pre_ref, dh_ref, xt_ref, qg_ref, w1t_ref, w2t_ref, qx_ref):
         transpose_taps(w1t_ref, w1_ref)
@@ -403,10 +507,10 @@
     def middle(edge_ref, corner_ref, pre_ref, dh_ref, xt_ref, qg_ref, w1_ref, w2t_ref, *refs):
         arrived = refs[:n_routes]
         keep_ref, send_ref, hid_ref, dpre_ref = refs[n_routes : n_routes + 4]
-        outs = refs[n_routes + 4 : 2 * n_routes + 4]
-        qd_ref, sum_ref = refs[2 * n_routes + 4 :]
+        outs = refs[n_routes + 4 : n_routes + 4 + n_routed]
+        qd_ref, sum_ref = refs[n_routes + 4 + n_routed :]
         lines, pixels = seam_lines(edge_ref, corner_ref, extent)
-        x_strips, g_strips = read_routes(plan, arrived, extent)
+        x_strips, g_strips = read(arrived)
         columns = strip_columns(g_strips, extent)
         value, slope = gelu_parts(pre_ref[...] + margin_forward(x_strips, w1_ref[...], extent))
         hidden = value.astype(BF16)
@@ -416,7 +520,7 @@
         dpre_ref[...] = d_pre
         a = gather_blocks(hidden, lines, pixels, extent)
         b = gather_blocks(d_pre, *fixed_lines(extent), extent)
-        write_routes(a, b, plan, outs, extent)
+        write(a, b, outs)
         write_columns(qd_ref, d_pre, False, extent)
         weight_sum(sum_ref.at[0], xt_ref[...], qd_ref, x_strips, strip_columns(b, extent), extent)
         weight_sum(sum_ref.at[1], jnp.transpose(value).astype(BF16), qg_ref, a, columns, extent)
@@ -434,13 +538,17 @@
         flops=2 * conv,
     )
     keep, send, hidden, d_pre = results[:4]
-    second_arrived = exchange(results[4:], plan, tiles)
+    if hops:
+        whole, second_arrived = reduce_gradients(keep, send, total, *results[4:])
+    else:
+        second_arrived = exchange(results[4:], plan, tiles)
+        whole, _ = reduce_gradients(keep, send, total)
 
     def last(edge_ref, corner_ref, x_ref, g_ref, hid_ref, dpre_ref, w2_ref, w1t_ref, *refs):
         arrived = refs[:n_routes]
         out_ref, dx_ref, q_ref = refs[n_routes:]
         lines, pixels = seam_lines(edge_ref, corner_ref, extent)
-        h_strips, d_strips = read_routes(plan, arrived, extent)
+        h_strips, d_strips = read(arrived)
         write_columns(q_ref, hid_ref[...], True, extent)
         total = window_product(q_ref, w2_ref[...], True, extent) + margin_forward(h_strips, w2_ref[...], extent)
         out_ref[...] = (x_ref[...].astype(F32) + total).astype(BF16)
@@ -458,7 +566,8 @@
         scratch=[pltpu.VMEM(columns_b.shape, BF16)],
         flops=2 * conv,
     )
-    one, two = reduce_gradients(keep, send, tiles * members)
+    whole, output, d_input = lax.optimization_barrier((whole, output, d_input))
+    one, two = join_cores(whole, total)
     shape = (9, channels, channels)
     return (
         output.reshape(inputs.shape),

time: 68.9 us -> 55.8 us (0.81)
  starting transfers between devices: 30.4 us -> 18.5 us
  local copies, waits for them, and re-layouts: 4.5 us -> 2.85 us
    ppermute x10 -> x0, starting transfers between devices: 17.8 us -> none  [exchange(): lax.ppermute(p, 'tile', [(i, (i + route[0]) % tiles) for i in range(tiles)])]
    ppermute x11 -> x15, waiting for transfers between devices: 14.4 us -> 22.4 us  [swap(): return lax.ppermute(value, AXES, [(i, i ^ mask) for i in range(total)])]
    ppermute x10 -> x0, waiting for transfers between devices: 7.59 us -> none  [exchange(): lax.ppermute(p, 'tile', [(i, (i + route[0]) % tiles) for i in range(tiles)])]
    ppermute x11 -> x15, starting transfers between devices: 12.6 us -> 18.5 us  [swap(): return lax.ppermute(value, AXES, [(i, i ^ mask) for i in range(total)])]
    unnamed x16, local copies, waits for them, and re-layouts: 4.44 us -> 2.76 us
  transfers between devices with their start and end apart: 21 -> 15, of which waited for: 12 -> 12; matrix products, arithmetic and copies ran while one was open for 0% -> 0% of each run, Pallas kernels for 7% -> 9%
where the time goes in v2:
time: 55.8 us; the launch traced here: 55.6 us
  waiting for transfers between devices  22.4 us (40%)
  starting transfers between devices  18.5 us (33%)
  Pallas kernels  9.52 us (17%)
  local copies, waits for them, and re-layouts  2.85 us (5%)
  other arithmetic  1.44 us (3%)
  between operations  0.85 us (2%)
    ppermute x15, waiting for transfers between devices, swap(): return lax.ppermute(value, AXES, [(i, i ^ mask) for i in range(total)])  22.4 us
    ppermute x15, starting transfers between devices, swap(): return lax.ppermute(value, AXES, [(i, i ^ mask) for i in range(total)])  18.5 us
    pallas_call x4, Pallas kernels, call(): pl.pallas_call(kernel, name=name, out_shape=outs, in_specs=specs, out_spe...  9.52 us
    unnamed x16, local copies, waits for them, and re-layouts  2.76 us
    mul x1, other arithmetic, per_device(): two.astype(F32) * factor  1.13 us
  transfers between devices with their start and end apart: 15, of which 12 were waited for; matrix products, arithmetic and copies ran while one was open for 0% of the time, Pallas kernels for 9%

profile of v2, /device:TPU:0, one launch (start us, length us, event | category | flops | bytes accessed | tf_op | source)
XLA Modules:
  0.0 55.6 jit_solution(9241591905676864173)
XLA Ops:
  0.6 0.8 %copy.12.edge_ref = s32[8,4]{1,0:T(8,128)S(1)} copy(s32[8,4]{0,1:T(4,128)} %param.10) | data formatting | bytes 256 | tf_op args[4]
  1.4 0.1 copy.13.corner_ref
  1.5 0.9 %copy-done.1 = bf16[1,1,32,32,128]{4,3,2,1,0:T(8,128)(2,1)S(1)} copy-done((bf16[1,1,32,32,128]{4,3,2,1,0:T(8,128)(2,1)S(1)}, bf16[1,1,32,32,128]{4,3,2,1,0:T(8,128)(2,1)}, u32[]{:S(2)}) %copy-start.1) | copy-done | bytes 262168
  2.4 0.9 %copy-done.3 = bf16[1,1,32,32,128]{4,3,2,1,0:T(8,128)(2,1)S(1)} copy-done((bf16[1,1,32,32,128]{4,3,2,1,0:T(8,128)(2,1)S(1)}, bf16[1,1,32,32,128]{4,3,2,1,0:T(8,128)(2,1)}, u32[]{:S(2)}) %copy-start.3) | copy-done | bytes 262168
  3.4 1.1 %first_strips.1 = (bf16[144,128]{1,0:T(8,128)(2,1)S(1)}, bf16[128,128]{1,0:T(8,128)(2,1)S(1)}) custom-call(s32[8,4]{1,0:T(8,128)S(1)} %copy.12.edge_ref, s32[8,4]{1,0:T(8,128)S(1)} %copy.13.corner_ref, bf16[1024,128]{1,0:T(8,128)(2,1)S(1)} %bitcast.29, bf16[1024,128]{1,0:T(8,128)(2,1)S(1)} %bitcast.32), custom_call_target="tpu_custom_call" | custom-call | bytes 594176 | tf_op jit(solution)/shard_map/first_strips/pallas_call | solution.py:355
  4.5 3.0 %collective-permute-start = (bf16[144,128]{1,0:T(8,128)(2,1)S(1)}, bf16[144,128]{1,0:T(8,128)(2,1)S(1)}, u32[]{:S(2)}, u32[]{:S(2)}) collective-permute-start(bf16[144,128]{1,0:T(8,128)(2,1)S(1)} %get-tuple-element.28), channel_id=1, source_target_pairs={{0,4},{1,5},{2,6},{3,7},{4,0},{5,1},{6,2},{7,3},{8,12},{9,13},{10,... | collective-permute-start | bytes 110600 | tf_op jit(solution)/shard_map/ppermute | solution.py:378
  7.5 1.9 %collective-permute-done.refs_0_ = bf16[144,128]{1,0:T(8,128)(2,1)S(1)} collective-permute-done((bf16[144,128]{1,0:T(8,128)(2,1)S(1)}, bf16[144,128]{1,0:T(8,128)(2,1)S(1)}, u32[]{:S(2)}, u32[]{:S(2)}) %collective-permute-start) | collective-permute-done | bytes 36896 | tf_op jit(solution)/shard_map/ppermute | solution.py:378
  9.4 3.1 %collective-permute-start.3 = (bf16[144,128]{1,0:T(8,128)(2,1)S(1)}, bf16[144,128]{1,0:T(8,128)(2,1)S(1)}, u32[]{:S(2)}, u32[]{:S(2)}) collective-permute-start(bf16[144,128]{1,0:T(8,128)(2,1)S(1)} %pad_maximum_fusion.5), channel_id=1, source_target_pairs={{0,16},{1,17},{2,18},{3,19},{4,20},{5,21},{6,22},{7,23},{8,24},{9,... | collective-permute-start | bytes 110600 | tf_op jit(solution)/shard_map/ppermute | solution.py:378
  12.6 1.6 %collective-permute-start.1 = (bf16[144,128]{1,0:T(8,128)(2,1)S(1)}, bf16[144,128]{1,0:T(8,128)(2,1)S(1)}, u32[]{:S(2)}, u32[]{:S(2)}) collective-permute-start(bf16[144,128]{1,0:T(8,128)(2,1)S(1)} %collective-permute-done.refs_0_), channel_id=1, source_target_pairs={{0,8},{1,9},{2,10},{3,11},{4,12},{5,13},{6,14},{7,15},{8,0},{9,1},... | collective-permute-start | bytes 110600 | tf_op jit(solution)/shard_map/ppermute | solution.py:378
  14.1 1.4 %inner_products.1 = (f32[1024,128]{1,0:T(8,128)S(1)}, f32[1024,128]{1,0:T(8,128)S(1)}, bf16[128,1024]{1,0:T(8,128)(2,1)S(1)}, bf16[1088,384]{1,0:T(8,128)(2,1)S(...) custom-call(bf16[1024,128]{1,0:T(8,128)(2,1)S(1)} %bitcast.30, bf16[1024,128]{1,0:T(8,128)(2,1)S(1)} %bitcast.33, ...), custom_call_target="tpu_custom_call" | custom-call | flops 603979776 | bytes 3850240 | tf_op jit(solution)/shard_map/inner_products/pallas_call | solution.py:355
  15.6 0.9 %collective-permute-done.1.refs_1_ = bf16[144,128]{1,0:T(8,128)(2,1)S(1)} collective-permute-done((bf16[144,128]{1,0:T(8,128)(2,1)S(1)}, bf16[144,128]{1,0:T(8,128)(2,1)S(1)}, u32[]{:S(2)}, u32[]{:S(2)}) %collective-permute-start.1) | collective-permute-done | bytes 36896 | tf_op jit(solution)/shard_map/ppermute | solution.py:378
  16.5 3.4 %collective-permute-done.2.refs_2_ = bf16[144,128]{1,0:T(8,128)(2,1)S(1)} collective-permute-done((bf16[144,128]{1,0:T(8,128)(2,1)S(1)}, bf16[144,128]{1,0:T(8,128)(2,1)S(1)}, u32[]{:S(2)}, u32[]{:S(2)}) %collective-permute-start.2) | collective-permute-done | bytes 36896 | tf_op jit(solution)/shard_map/ppermute | solution.py:378
  19.9 3.4 %gradients.1 = (f32[1152,128]{1,0:T(8,128)S(1)}, bf16[1152,128]{1,0:T(8,128)(2,1)S(1)}, bf16[1024,128]{1,0:T(8,128)(2,1)S(1)}, bf16[1024,128]{1,0:T(8,128)(2,1)S...) custom-call(s32[8,4]{1,0:T(8,128)S(1)} %copy.12.edge_ref, s32[8,4]{1,0:T(8,128)S(1)} %copy.13.corner_ref, ...), custom_call_target="tpu_custom_call" | custom-call | flops 603979776 | bytes 4362496 | tf_op jit(solution)/shard_map/gradients/pallas_call | solution.py:355
  23.4 1.5 %collective-permute-done.4 = bf16[1152,128]{1,0:T(8,128)(2,1)S(1)} collective-permute-done((bf16[1152,128]{1,0:T(8,128)(2,1)S(1)}, bf16[1152,128]{1,0:T(8,128)(2,1)S(1)}, u32[]{:S(2)}, u32[]{:S(2)}) %collective-permute-start.4) | collective-permute-done | bytes 294944 | tf_op jit(solution)/shard_map/ppermute | solution.py:378
  25.1 1.6 %collective-permute-start.7 = (bf16[432,128]{1,0:T(8,128)(2,1)S(1)}, bf16[432,128]{1,0:T(8,128)(2,1)S(1)}, u32[]{:S(2)}, u32[]{:S(2)}) collective-permute-start(bf16[432,128]{1,0:T(8,128)(2,1)S(1)} %pad_maximum_fusion.4), channel_id=1, source_target_pairs={{0,4},{1,5},{2,6},{3,7},{4,0},{5,1},{6,2},{7,3},{8,12},{9,13},{10,... | collective-permute-start | bytes 331784 | tf_op jit(solution)/shard_map/ppermute | solution.py:378
  26.6 1.5 %collective-permute-start.5 = (bf16[288,128]{1,0:T(8,128)(2,1)S(1)}, bf16[288,128]{1,0:T(8,128)(2,1)S(1)}, u32[]{:S(2)}, u32[]{:S(2)}) collective-permute-start(bf16[288,128]{1,0:T(8,128)(2,1)S(1)} %get-tuple-element.50), channel_id=1, source_target_pairs={{0,6},{1,7},{2,4},{3,5},{4,2},{5,3},{6,0},{7,1},{8,14},{9,15},{10,... | collective-permute-start | bytes 221192 | tf_op jit(solution)/shard_map/ppermute | solution.py:378
  28.1 0.5 collective-permute-start.6
  28.6 1.8 %collective-permute-done.7 = bf16[432,128]{1,0:T(8,128)(2,1)S(1)} collective-permute-done((bf16[432,128]{1,0:T(8,128)(2,1)S(1)}, bf16[432,128]{1,0:T(8,128)(2,1)S(1)}, u32[]{:S(2)}, u32[]{:S(2)}) %collective-permute-start.7) | collective-permute-done | bytes 110624 | tf_op jit(solution)/shard_map/ppermute | solution.py:378
  30.4 2.5 %collective-permute-done.5 = bf16[288,128]{1,0:T(8,128)(2,1)S(1)} collective-permute-done((bf16[288,128]{1,0:T(8,128)(2,1)S(1)}, bf16[288,128]{1,0:T(8,128)(2,1)S(1)}, u32[]{:S(2)}, u32[]{:S(2)}) %collective-permute-start.5) | collective-permute-done | bytes 73760 | tf_op jit(solution)/shard_map/ppermute | solution.py:378
  32.9 0.6 %collective-permute-done.6 = bf16[288,128]{1,0:T(8,128)(2,1)S(1)} collective-permute-done((bf16[288,128]{1,0:T(8,128)(2,1)S(1)}, bf16[288,128]{1,0:T(8,128)(2,1)S(1)}, u32[]{:S(2)}, u32[]{:S(2)}) %collective-permute-start.6) | collective-permute-done | bytes 73760 | tf_op jit(solution)/shard_map/ppermute | solution.py:378
  33.6 0.5 collective-permute-start.10
  34.1 3.0 %collective-permute-start.9 = (bf16[432,128]{1,0:T(8,128)(2,1)S(1)}, bf16[432,128]{1,0:T(8,128)(2,1)S(1)}, u32[]{:S(2)}, u32[]{:S(2)}) collective-permute-start(bf16[432,128]{1,0:T(8,128)(2,1)S(1)} %get-tuple-element.51), channel_id=1, source_target_pairs={{0,16},{1,17},{2,18},{3,19},{4,20},{5,21},{6,22},{7,23},{8,24},{9,... | collective-permute-start | bytes 331784 | tf_op jit(solution)/shard_map/ppermute | solution.py:378
  37.1 2.0 %collective-permute-done.8 = bf16[432,128]{1,0:T(8,128)(2,1)S(1)} collective-permute-done((bf16[432,128]{1,0:T(8,128)(2,1)S(1)}, bf16[432,128]{1,0:T(8,128)(2,1)S(1)}, u32[]{:S(2)}, u32[]{:S(2)}) %collective-permute-start.8) | collective-permute-done | bytes 110624 | tf_op jit(solution)/shard_map/ppermute | solution.py:378
  39.1 1.2 %collective-permute-done.10 = bf16[432,128]{1,0:T(8,128)(2,1)S(1)} collective-permute-done((bf16[432,128]{1,0:T(8,128)(2,1)S(1)}, bf16[432,128]{1,0:T(8,128)(2,1)S(1)}, u32[]{:S(2)}, u32[]{:S(2)}) %collective-permute-start.10) | collective-permute-done | bytes 110624 | tf_op jit(solution)/shard_map/ppermute | solution.py:378
  40.3 4.9 %collective-permute-done.9 = bf16[432,128]{1,0:T(8,128)(2,1)S(1)} collective-permute-done((bf16[432,128]{1,0:T(8,128)(2,1)S(1)}, bf16[432,128]{1,0:T(8,128)(2,1)S(1)}, u32[]{:S(2)}, u32[]{:S(2)}) %collective-permute-start.9) | collective-permute-done | bytes 110624 | tf_op jit(solution)/shard_map/ppermute | solution.py:378
  45.2 0.6 %collective-permute-start.11 = (bf16[288,128]{1,0:T(8,128)(2,1)S(1)}, bf16[288,128]{1,0:T(8,128)(2,1)S(1)}, u32[]{:S(2)}, u32[]{:S(2)}) collective-permute-start(bf16[288,128]{1,0:T(8,128)(2,1)S(1)} %add_convert_fusion), channel_id=1, source_target_pairs={{0,2},{1,3},{2,0},{3,1},{4,6},{5,7},{6,4},{7,5},{8,10},{9,11},{10,... | collective-permute-start | bytes 221192 | tf_op jit(solution)/shard_map/ppermute | solution.py:378
  45.9 1.5 %collective-permute-start.12 = (bf16[288,128]{1,0:T(8,128)(2,1)S(1)}, bf16[288,128]{1,0:T(8,128)(2,1)S(1)}, u32[]{:S(2)}, u32[]{:S(2)}) collective-permute-start(bf16[288,128]{1,0:T(8,128)(2,1)S(1)} %add_convert_fusion), channel_id=1, source_target_pairs={{0,4},{1,5},{2,6},{3,7},{4,0},{5,1},{6,2},{7,3},{8,12},{9,13},{10,... | collective-permute-start | bytes 221192 | tf_op jit(solution)/shard_map/ppermute | solution.py:378
  47.4 1.4 %collective-permute-start.13 = (bf16[288,128]{1,0:T(8,128)(2,1)S(1)}, bf16[288,128]{1,0:T(8,128)(2,1)S(1)}, u32[]{:S(2)}, u32[]{:S(2)}) collective-permute-start(bf16[288,128]{1,0:T(8,128)(2,1)S(1)} %add_convert_fusion), channel_id=1, source_target_pairs={{0,6},{1,7},{2,4},{3,5},{4,2},{5,3},{6,0},{7,1},{8,14},{9,15},{10,... | collective-permute-start | bytes 221192 | tf_op jit(solution)/shard_map/ppermute | solution.py:378
  48.9 3.6 %outputs.1 = (bf16[1024,128]{1,0:T(8,128)(2,1)}, bf16[1024,128]{1,0:T(8,128)(2,1)}) custom-call(s32[8,4]{1,0:T(8,128)S(1)} %copy.12.edge_ref, s32[8,4]{1,0:T(8,128)S(1)} %copy.13.corner_ref, bf16[1024,128]{1,0:T(8,128)(2,1)S(1)} %bitcast.31, bf16[1024,128]{1,0:T(8,128)(2,1)S(1)} %bitcast.34, bf16[1024,128]{1,0:T(8,128)(2,1)S(1)} %get-tuple-element.34.hid_ref, ...), custom_call_target="tpu_custom_call" | custom-call | flops 603979776 | bytes 2310400 | tf_op jit(solution)/shard_map/outputs/pallas_call | solution.py:355
  52.5 0.2 collective-permute-done.13
  52.9 1.6 %collective-permute-done.14 = bf16[4,288,128]{2,1,0:T(8,128)(2,1)S(1)} collective-permute-done((bf16[4,288,128]{2,1,0:T(8,128)(2,1)S(1)}, bf16[4,288,128]{2,1,0:T(8,128)(2,1)S(1)}, u32[]{:S(2)}, u32[]{:S(2)}) %collective-permute-start.14) | collective-permute-done | bytes 294944 | tf_op jit(solution)/shard_map/ppermute | solution.py:378
  54.4 1.1 %convert_multiply_fusion = (f32[4,288,128]{2,1,0:T(8,128)}, f32[4,288,128]{2,1,0:T(8,128)}) fusion(bf16[4,288,128]{2,1,0:T(8,128)(2,1)S(1)} %collective-permute-done.14, bf16[4,288,128]{2,1,0:T(8,128)(2,1)S(1)} %pad_maximum_fusion.1, pred[]{:T(512)S(6)} %eq.3), kind=kLoop, calls=%fused_computation | loop fusion | flops 884736 | bytes 1769473 | tf_op jit(solution)/shard_map/mul | solution.py:576
  (39 shorter events, 0.6 us)
Async XLA Ops:
  0.6 0.8 %copy-start.6 = (s32[8,4]{0,1:T(4,128)S(1)}, s32[8,4]{0,1:T(4,128)}, u32[]{:S(2)}) copy-start(s32[8,4]{0,1:T(4,128)} %param.11) | copy-start | bytes 388
  1.5 1.0 %copy-start.1 = (bf16[1,1,32,32,128]{4,3,2,1,0:T(8,128)(2,1)S(1)}, bf16[1,1,32,32,128]{4,3,2,1,0:T(8,128)(2,1)}, u32[]{:S(2)}) copy-start(bf16[1,1,32,32,128]{4,3,2,1,0:T(8,128)(2,1)} %param.6) | copy-start | bytes 786436
  2.4 0.9 %copy-start.3 = (bf16[1,1,32,32,128]{4,3,2,1,0:T(8,128)(2,1)S(1)}, bf16[1,1,32,32,128]{4,3,2,1,0:T(8,128)(2,1)}, u32[]{:S(2)}) copy-start(bf16[1,1,32,32,128]{4,3,2,1,0:T(8,128)(2,1)} %param.9) | copy-start | bytes 786436
  3.4 10.7 %copy-start = (bf16[9,128,128]{2,1,0:T(8,128)(2,1)S(1)}, bf16[9,128,128]{2,1,0:T(8,128)(2,1)}, u32[]{:S(2)}) copy-start(bf16[9,128,128]{2,1,0:T(8,128)(2,1)} %param.7) | copy-start | bytes 884740
  3.4 10.8 %copy-start.5 = (bf16[9,128,128]{2,1,0:T(8,128)(2,1)S(1)}, bf16[9,128,128]{2,1,0:T(8,128)(2,1)}, u32[]{:S(2)}) copy-start(bf16[9,128,128]{2,1,0:T(8,128)(2,1)} %param.8) | copy-start | bytes 884740
  4.5 4.9 %collective-permute-start = (bf16[144,128]{1,0:T(8,128)(2,1)S(1)}, bf16[144,128]{1,0:T(8,128)(2,1)S(1)}, u32[]{:S(2)}, u32[]{:S(2)}) collective-permute-start(bf16[144,128]{1,0:T(8,128)(2,1)S(1)} %get-tuple-element.28), channel_id=1, source_target_pairs={{0,4},{1,5},{2,6},{3,7},{4,0},{5,1},{6,2},{7,3},{8,12},{9,13},{10,... | collective-permute-start | bytes 110600 | tf_op jit(solution)/shard_map/ppermute | solution.py:378
  9.4 6.2 %collective-permute-start.3 = (bf16[144,128]{1,0:T(8,128)(2,1)S(1)}, bf16[144,128]{1,0:T(8,128)(2,1)S(1)}, u32[]{:S(2)}, u32[]{:S(2)}) collective-permute-start(bf16[144,128]{1,0:T(8,128)(2,1)S(1)} %pad_maximum_fusion.5), channel_id=1, source_target_pairs={{0,16},{1,17},{2,18},{3,19},{4,20},{5,21},{6,22},{7,23},{8,24},{9,... | collective-permute-start | bytes 110600 | tf_op jit(solution)/shard_map/ppermute | solution.py:378
  12.6 4.0 %collective-permute-start.1 = (bf16[144,128]{1,0:T(8,128)(2,1)S(1)}, bf16[144,128]{1,0:T(8,128)(2,1)S(1)}, u32[]{:S(2)}, u32[]{:S(2)}) collective-permute-start(bf16[144,128]{1,0:T(8,128)(2,1)S(1)} %collective-permute-done.refs_0_), channel_id=1, source_target_pairs={{0,8},{1,9},{2,10},{3,11},{4,12},{5,13},{6,14},{7,15},{8,0},{9,1},... | collective-permute-start | bytes 110600 | tf_op jit(solution)/shard_map/ppermute | solution.py:378
  14.1 5.8 %collective-permute-start.2 = (bf16[144,128]{1,0:T(8,128)(2,1)S(1)}, bf16[144,128]{1,0:T(8,128)(2,1)S(1)}, u32[]{:S(2)}, u32[]{:S(2)}) collective-permute-start(bf16[144,128]{1,0:T(8,128)(2,1)S(1)} %collective-permute-done.refs_0_), channel_id=1, source_target_pairs={{0,24},{1,25},{2,26},{3,27},{4,28},{5,29},{6,30},{7,31},{8,16},{9,... | collective-permute-start | bytes 110600 | tf_op jit(solution)/shard_map/ppermute | solution.py:378
  23.3 1.6 %collective-permute-start.4 = (bf16[1152,128]{1,0:T(8,128)(2,1)S(1)}, bf16[1152,128]{1,0:T(8,128)(2,1)S(1)}, u32[]{:S(2)}, u32[]{:S(2)}) collective-permute-start(bf16[1152,128]{1,0:T(8,128)(2,1)S(1)} %get-tuple-element.31), channel_id=1, source_target_pairs={{0,1},{1,0},{2,3},{3,2},{4,5},{5,4},{6,7},{7,6},{8,9},{9,8},{10,11... | collective-permute-start | bytes 884744 | tf_op jit(solution)/shard_map/ppermute | solution.py:378
  25.1 5.3 %collective-permute-start.7 = (bf16[432,128]{1,0:T(8,128)(2,1)S(1)}, bf16[432,128]{1,0:T(8,128)(2,1)S(1)}, u32[]{:S(2)}, u32[]{:S(2)}) collective-permute-start(bf16[432,128]{1,0:T(8,128)(2,1)S(1)} %pad_maximum_fusion.4), channel_id=1, source_target_pairs={{0,4},{1,5},{2,6},{3,7},{4,0},{5,1},{6,2},{7,3},{8,12},{9,13},{10,... | collective-permute-start | bytes 331784 | tf_op jit(solution)/shard_map/ppermute | solution.py:378
  26.6 6.3 %collective-permute-start.5 = (bf16[288,128]{1,0:T(8,128)(2,1)S(1)}, bf16[288,128]{1,0:T(8,128)(2,1)S(1)}, u32[]{:S(2)}, u32[]{:S(2)}) collective-permute-start(bf16[288,128]{1,0:T(8,128)(2,1)S(1)} %get-tuple-element.50), channel_id=1, source_target_pairs={{0,6},{1,7},{2,4},{3,5},{4,2},{5,3},{6,0},{7,1},{8,14},{9,15},{10,... | collective-permute-start | bytes 221192 | tf_op jit(solution)/shard_map/ppermute | solution.py:378
  28.1 5.3 %collective-permute-start.6 = (bf16[288,128]{1,0:T(8,128)(2,1)S(1)}, bf16[288,128]{1,0:T(8,128)(2,1)S(1)}, u32[]{:S(2)}, u32[]{:S(2)}) collective-permute-start(bf16[288,128]{1,0:T(8,128)(2,1)S(1)} %get-tuple-element.49), channel_id=1, source_target_pairs={{0,2},{1,3},{2,0},{3,1},{4,6},{5,7},{6,4},{7,5},{8,10},{9,11},{10,... | collective-permute-start | bytes 221192 | tf_op jit(solution)/shard_map/ppermute | solution.py:378
  33.5 5.6 %collective-permute-start.8 = (bf16[432,128]{1,0:T(8,128)(2,1)S(1)}, bf16[432,128]{1,0:T(8,128)(2,1)S(1)}, u32[]{:S(2)}, u32[]{:S(2)}) collective-permute-start(bf16[432,128]{1,0:T(8,128)(2,1)S(1)} %get-tuple-element.52), channel_id=1, source_target_pairs={{0,8},{1,9},{2,10},{3,11},{4,12},{5,13},{6,14},{7,15},{8,0},{9,1},... | collective-permute-start | bytes 331784 | tf_op jit(solution)/shard_map/ppermute | solution.py:378
  33.6 6.7 %collective-permute-start.10 = (bf16[432,128]{1,0:T(8,128)(2,1)S(1)}, bf16[432,128]{1,0:T(8,128)(2,1)S(1)}, u32[]{:S(2)}, u32[]{:S(2)}) collective-permute-start(bf16[432,128]{1,0:T(8,128)(2,1)S(1)} %get-tuple-element.52), channel_id=1, source_target_pairs={{0,24},{1,25},{2,26},{3,27},{4,28},{5,29},{6,30},{7,31},{8,16},{9,... | collective-permute-start | bytes 331784 | tf_op jit(solution)/shard_map/ppermute | solution.py:378
  34.1 14.8 %copy-start.2 = (bf16[1,1,32,32,128]{4,3,2,1,0:T(8,128)(2,1)S(1)}, bf16[1,1,32,32,128]{4,3,2,1,0:T(8,128)(2,1)}, u32[]{:S(2)}) copy-start(bf16[1,1,32,32,128]{4,3,2,1,0:T(8,128)(2,1)} %param.6) | copy-start | bytes 786436
  34.1 14.8 %copy-start.4 = (bf16[1,1,32,32,128]{4,3,2,1,0:T(8,128)(2,1)S(1)}, bf16[1,1,32,32,128]{4,3,2,1,0:T(8,128)(2,1)}, u32[]{:S(2)}) copy-start(bf16[1,1,32,32,128]{4,3,2,1,0:T(8,128)(2,1)} %param.9) | copy-start | bytes 786436
  34.1 11.1 %collective-permute-start.9 = (bf16[432,128]{1,0:T(8,128)(2,1)S(1)}, bf16[432,128]{1,0:T(8,128)(2,1)S(1)}, u32[]{:S(2)}, u32[]{:S(2)}) collective-permute-start(bf16[432,128]{1,0:T(8,128)(2,1)S(1)} %get-tuple-element.51), channel_id=1, source_target_pairs={{0,16},{1,17},{2,18},{3,19},{4,20},{5,21},{6,22},{7,23},{8,24},{9,... | collective-permute-start | bytes 331784 | tf_op jit(solution)/shard_map/ppermute | solution.py:378
  45.2 7.2 %collective-permute-start.11 = (bf16[288,128]{1,0:T(8,128)(2,1)S(1)}, bf16[288,128]{1,0:T(8,128)(2,1)S(1)}, u32[]{:S(2)}, u32[]{:S(2)}) collective-permute-start(bf16[288,128]{1,0:T(8,128)(2,1)S(1)} %add_convert_fusion), channel_id=1, source_target_pairs={{0,2},{1,3},{2,0},{3,1},{4,6},{5,7},{6,4},{7,5},{8,10},{9,11},{10,... | collective-permute-start | bytes 221192 | tf_op jit(solution)/shard_map/ppermute | solution.py:378
  45.9 6.6 %collective-permute-start.12 = (bf16[288,128]{1,0:T(8,128)(2,1)S(1)}, bf16[288,128]{1,0:T(8,128)(2,1)S(1)}, u32[]{:S(2)}, u32[]{:S(2)}) collective-permute-start(bf16[288,128]{1,0:T(8,128)(2,1)S(1)} %add_convert_fusion), channel_id=1, source_target_pairs={{0,4},{1,5},{2,6},{3,7},{4,0},{5,1},{6,2},{7,3},{8,12},{9,13},{10,... | collective-permute-start | bytes 221192 | tf_op jit(solution)/shard_map/ppermute | solution.py:378
  47.4 5.3 %collective-permute-start.13 = (bf16[288,128]{1,0:T(8,128)(2,1)S(1)}, bf16[288,128]{1,0:T(8,128)(2,1)S(1)}, u32[]{:S(2)}, u32[]{:S(2)}) collective-permute-start(bf16[288,128]{1,0:T(8,128)(2,1)S(1)} %add_convert_fusion), channel_id=1, source_target_pairs={{0,6},{1,7},{2,4},{3,5},{4,2},{5,3},{6,0},{7,1},{8,14},{9,15},{10,... | collective-permute-start | bytes 221192 | tf_op jit(solution)/shard_map/ppermute | solution.py:378
  52.8 1.6 %collective-permute-start.14 = (bf16[4,288,128]{2,1,0:T(8,128)(2,1)S(1)}, bf16[4,288,128]{2,1,0:T(8,128)(2,1)S(1)}, u32[]{:S(2)}, u32[]{:S(2)}) collective-permute-start(bf16[4,288,128]{2,1,0:T(8,128)(2,1)S(1)} %pad_maximum_fusion.1), channel_id=1, source_target_pairs={{0,1},{1,0},{2,3},{3,2},{4,5},{5,4},{6,7},{7,6},{8,9},{9,8},{10,11... | collective-permute-start | bytes 884744 | tf_op jit(solution)/shard_map/ppermute | solution.py:378

commit v3 on v2

--- a/solution.py
+++ b/solution.py
@@ -13,7 +13,8 @@
 F32 = jnp.float32
 BF16 = jnp.bfloat16
 AXES = ("tile", "dp")
-LIMIT = 48 * 1024 * 1024
+LIMIT = 20 * 1024 * 1024
+ALONE = 60 * 1024 * 1024
 
 BLOCKS = ((0, (0, 1)), (2, (3, 2)), (1, ()), (3, ()))
 
@@ -57,6 +58,10 @@
     return lax.dot_general(a, b, (((1,), (0,)), ((), ())), preferred_element_type=F32)
 
 
+def dot_nt(a, b):
+    return lax.dot_general(a, b, (((1,), (1,)), ((), ())), preferred_element_type=F32)
+
+
 def dot_t(a, b):
     return lax.dot_general(a, b, (((0,), (0,)), ((), ())), preferred_element_type=F32)
 
@@ -75,10 +80,10 @@
 
 
 def seam_lines(edge_ref, corner_ref, extent):
-    tiles = edge_ref.shape[0]
+    tiles = edge_ref.shape[1]
     mine = lax.axis_index("tile")
-    lines = [side_line(edge_ref[(mine - o + tiles + RW * tiles) % tiles, k], extent) for k, o in enumerate(SIDES)]
-    pixels = [corner_pixel(corner_ref[(mine - o + tiles + RW * tiles) % tiles, q], extent) for q, o in enumerate(CORNERS)]
+    lines = [side_line(edge_ref[k, (mine - o + tiles + RW * tiles) % tiles], extent) for k, o in enumerate(SIDES)]
+    pixels = [corner_pixel(corner_ref[q, (mine - o + tiles + RW * tiles) % tiles], extent) for q, o in enumerate(CORNERS)]
     return lines, pixels
 
 
@@ -104,17 +109,38 @@
     return pick_rows(index, count)
 
 
-def gather_block(image, position, lines, pixels, extent):
-    side, corners = BLOCKS[position]
-    count = image.shape[0]
-    rows = line_rows(lines[side], extent, count)
-    if corners:
-        rows = jnp.concatenate([rows, spot_rows([(i, pixels[q]) for i, q in enumerate(corners)], count)], axis=0)
-    return dot(rows, image).astype(BF16)
-
-
-def gather_blocks(image, lines, pixels, extent):
-    return [gather_block(image, i, lines, pixels, extent) for i in range(4)]
+def block_choice(lines, pixels, extent):
+    count = extent * extent
+    rows = []
+    for side, corners in BLOCKS:
+        rows.append(line_rows(lines[side], extent, count))
+        if corners:
+            rows.append(spot_rows([(i, pixels[q]) for i, q in enumerate(corners)], count))
+    return jnp.concatenate(rows, axis=0)
+
+
+def seam_scatter(lines, pixels, extent):
+    starts = block_starts(extent)
+    lane = iota((1, starts[3] + extent), 1)
+    index = jnp.full(lane.shape, -1, jnp.int32)
+    for start, (side, ends) in zip(starts, BLOCKS):
+        base, step = lines[side]
+        index = jnp.where((lane >= start) & (lane < start + extent), base + step * (lane - start), index)
+        for i, q in enumerate(ends):
+            index = jnp.where(lane == start + extent + i, pixels[q], index)
+    return (iota((extent * extent, 1), 0) == index).astype(F32).astype(BF16)
+
+
+def column_scatter(extent):
+    lane = iota((1, 4 * extent), 1)
+    target = (lane % extent) * extent + jnp.where(lane < 2 * extent, extent - 1, 0)
+    return (iota((extent * extent, 1), 0) == target).astype(F32).astype(BF16)
+
+
+def gather_blocks(choice, image, extent):
+    strips = dot(choice, image).astype(BF16)
+    starts = block_starts(extent)
+    return [strips[start : start + rows] for start, rows in zip(starts, block_rows(extent))]
 
 
 def write_routes(a_blocks, b_blocks, plan, out_refs, extent):
@@ -167,11 +193,9 @@
     return tiles == 8
 
 
-def write_relay(a_blocks, b_blocks, near_ref, far_ref, extent):
-    for i, block in enumerate((a_blocks[2], a_blocks[3], b_blocks[2], b_blocks[3])):
+def write_near(a_blocks, b_blocks, near_ref, extent):
+    for i, block in enumerate((a_blocks[3], b_blocks[2], a_blocks[2], b_blocks[3])):
         near_ref[i * extent : (i + 1) * extent, :] = block
-    for i, block in enumerate((a_blocks[0], a_blocks[1], b_blocks[0], b_blocks[1])):
-        far_ref[i * extent : (i + 1) * extent, :] = block[:extent]
     rows = iota((16, 1), 0)
     tile = jnp.zeros((16, near_ref.shape[1]), F32)
     at = 0
@@ -183,24 +207,42 @@
     near_ref[4 * extent : 4 * extent + 16, :] = tile.astype(BF16)
 
 
+def write_far(a_blocks, b_blocks, far_ref, extent):
+    for i, block in enumerate((a_blocks[0], a_blocks[1], b_blocks[0], b_blocks[1])):
+        far_ref[i * extent : (i + 1) * extent, :] = block[:extent]
+
+
+def near_starts(tile, extent):
+    right = tile % 2
+    odd = (tile // 2) % 2
+    corners = 2 * extent + 16
+    side = jnp.where(right == 1, 0, 2 * extent)
+    one = jnp.where(right == odd, corners, side)
+    three = jnp.where(right == odd, side, corners)
+    return side_of_partner(right, extent), one, three
+
+
+def side_of_partner(right, extent):
+    return jnp.where(right == 1, 2 * extent, 0)
+
+
 def read_relay(refs, extent):
     across, one, three, far, opposite = refs
     mine = lax.axis_index("tile")
     left = mine % 2 == 0
-    even = (mine // 2) % 2 == 0
-
-    def pick(first, second, start, count):
-        whole = [r[start : start + count, :].astype(F32) for r in (across, one, three)]
-        above = jnp.where(even, whole[1], whole[2])
-        below = jnp.where(even, whole[2], whole[1])
-        return jnp.where(left, {"across": whole[0], "above": above, "below": below}[first], {"across": whole[0], "above": above, "below": below}[second])
-
-    def side(i, first, second):
-        return pick(first, second, i * extent, extent).astype(BF16)
-
-    a_east, b_west = side(0, "across", "above"), side(3, "across", "above")
-    a_west, b_east = side(1, "below", "across"), side(2, "below", "across")
-    beside = pick("above", "below", 4 * extent, 16)
+    odd = (mine // 2 + mine) % 2 == 1
+
+    def rows_of(ref, start, count):
+        return ref[start : start + count, :].astype(F32)
+
+    def choose(start, count):
+        return jnp.where(odd, rows_of(one, start, count), rows_of(three, start, count))
+
+    pair = [(rows_of(across, i * extent, extent), choose(i * extent, extent)) for i in range(2)]
+    a_east, b_west = [jnp.where(left, here, there).astype(BF16) for here, there in pair]
+    a_west, b_east = [jnp.where(left, there, here).astype(BF16) for here, there in pair]
+    tail = 2 * extent - 16
+    beside = jnp.where(odd, rows_of(three, tail, 16), rows_of(one, tail, 16))
     beyond = opposite[0:16, :].astype(F32)
     third = jnp.where(left, beside, beyond)
     fifth = jnp.where(left, beyond, beside)
@@ -239,15 +281,22 @@
 
 def window_product(q_ref, weight, forward, extent, chunk=256):
     count = q_ref.shape[0] - 2 * extent
+    channels = weight.shape[1]
+    if not forward:
+        weight = tap_columns(weight, range(9), channels)
     pieces = []
     for start in range(0, count, chunk):
         rows = [q_ref[(a if forward else 2 - a) * extent + start : (a if forward else 2 - a) * extent + start + chunk, :] for a in range(3)]
-        pieces.append(dot(jnp.concatenate(rows, axis=1), weight))
+        pieces.append((dot if forward else dot_nt)(jnp.concatenate(rows, axis=1), weight))
     return jnp.concatenate(pieces, axis=0)
 
 
 def tap_weight(weight, taps, channels):
     return jnp.concatenate([weight[t * channels : (t + 1) * channels, :] for t in taps], axis=0)
+
+
+def tap_columns(weight, taps, channels):
+    return jnp.concatenate([weight[t * channels : (t + 1) * channels, :] for t in taps], axis=1)
 
 
 def halves(values):
@@ -255,7 +304,7 @@
     return high, (values - high.astype(F32)).astype(BF16)
 
 
-def margin_forward(strips, weight, extent):
+def margin_forward(strips, weight, columns, extent):
     channels = strips[0].shape[1]
     count = extent * extent
     adds = []
@@ -268,12 +317,10 @@
             before, after = tile[0:1], tile[1:2]
         left = jnp.where(row == 0, before, pltpu.roll(middle, 1, 0))
         right = jnp.where(row == extent - 1, after, pltpu.roll(middle, extent - 1, 0))
-        columns = jnp.concatenate([left, middle, right], axis=1).astype(BF16)
-        adds.append(dot(columns, tap_weight(weight, block_taps(position), channels)))
+        window = jnp.concatenate([left, middle, right], axis=1).astype(BF16)
+        adds.append(dot(window, tap_weight(weight, block_taps(position), channels)))
     spread = jnp.concatenate(list(halves(adds[2])) + list(halves(adds[3])), axis=0)
-    lane = iota((1, 4 * extent), 1)
-    target = (lane % extent) * extent + jnp.where(lane < 2 * extent, extent - 1, 0)
-    image = dot((iota((count, 1), 0) == target).astype(F32).astype(BF16), spread)
+    image = dot(columns, spread)
     top = image[:extent] + adds[0]
     bottom = image[count - extent :] + adds[1]
     return jnp.concatenate([top, image[extent : count - extent], bottom], axis=0)
@@ -297,21 +344,10 @@
     return result
 
 
-def margin_backward(columns, weight_t, lines, pixels, extent):
-    channels = weight_t.shape[1]
-    count = extent * extent
-    adds = [dot(columns[i], tap_weight(weight_t, block_taps(i), channels)) for i in range(4)]
-    stacked = jnp.concatenate(adds, axis=0)
-    total = stacked.shape[0]
-    lane = iota((1, total), 1)
-    index = jnp.full((1, total), -1, jnp.int32)
-    for start, (side, ends) in zip(block_starts(extent), BLOCKS):
-        base, step = lines[side]
-        index = jnp.where((lane >= start) & (lane < start + extent), base + step * (lane - start), index)
-        for i, q in enumerate(ends):
-            index = jnp.where(lane == start + extent + i, pixels[q], index)
-    scatter = (iota((count, 1), 0) == index).astype(F32).astype(BF16)
-    high, low = halves(stacked)
+def margin_backward(columns, weight, scatter, extent):
+    channels = weight.shape[1]
+    adds = [dot_nt(columns[i], tap_columns(weight, block_taps(i), channels)) for i in range(4)]
+    high, low = halves(jnp.concatenate(adds, axis=0))
     return dot(scatter, high) + dot(scatter, low)
 
 
@@ -333,13 +369,6 @@
             out_ref[tap * channels : (tap + 1) * channels, :] = value
 
 
-def transpose_taps(out_ref, weight_ref):
-    channels = out_ref.shape[1]
-    for tap in range(9):
-        block = weight_ref[tap * channels : (tap + 1) * channels, :]
-        out_ref[tap * channels : (tap + 1) * channels, :] = jnp.transpose(block.astype(F32)).astype(BF16)
-
-
 def gelu_parts(u):
     scale = math.sqrt(2.0 / math.pi)
     square = u * u
@@ -349,8 +378,8 @@
     return value, slope
 
 
-def call(kernel, name, outs, ins, operands, scratch=(), flops=0):
-    specs = [pl.BlockSpec(memory_space=pltpu.SMEM if i == "s" else pltpu.VMEM) for i in ins]
+def call(kernel, name, outs, ins, operands, scratch=(), flops=0, limit=LIMIT):
+    specs = [pl.BlockSpec(memory_space={"a": pl.ANY, "s": pltpu.SMEM, "v": pltpu.VMEM}[i]) for i in ins]
     moved = sum(math.prod(o.shape) * o.dtype.itemsize for o in list(outs) + list(operands))
     return pl.pallas_call(
         kernel,
@@ -360,7 +389,7 @@
         out_specs=[pl.BlockSpec(memory_space=pltpu.VMEM) for _ in outs],
         scratch_shapes=list(scratch),
         cost_estimate=pl.CostEstimate(flops=flops, bytes_accessed=moved, transcendentals=0),
-        compiler_params=pltpu.CompilerParams(vmem_limit_bytes=LIMIT),
+        compiler_params=pltpu.CompilerParams(vmem_limit_bytes=limit),
     )(*operands)
 
 
@@ -378,28 +407,36 @@
     return lax.ppermute(value, AXES, [(i, i ^ mask) for i in range(total)])
 
 
-def reduce_gradients(keep, send, total, near=None, far=None):
+def reduce_gradients(keep, send, total, work, near=None, far=None):
     rows, channels = keep.shape
     quarter = rows // 4
     wire = BF16 if total <= 32 else F32
     me = lax.axis_index(AXES)
-    own = keep + swap(send, 1, total).astype(F32)
+    other = swap(send, 1, total)
     plane = (me >> 1) & 3
-    parts = own.reshape(4, quarter, channels)
-    sent = parts.astype(wire)
+
+    def chunk(index):
+        first = lax.dynamic_index_in_dim(keep.reshape(4, quarter, channels), index, 0, keepdims=False)
+        second = lax.dynamic_index_in_dim(other.reshape(4, quarter, channels), index, 0, keepdims=False)
+        return first + second.astype(F32)
+
     arrived = {}
     for m in (3, 1, 2):
-        message = lax.dynamic_index_in_dim(sent, plane ^ m, 0, keepdims=False)
+        message = chunk(plane ^ m).astype(wire)
         if m == 2 and near is not None:
             message = jnp.concatenate([message, near], axis=0)
         arrived[m] = swap(message, m << 1, total)
-    part = lax.dynamic_index_in_dim(parts, plane, 0, keepdims=False)
+    part = chunk(plane)
     for m in (3, 1, 2):
         part = part + arrived[m][:quarter].astype(F32)
+    part, done = work(part)
     extras = None
     if near is not None:
         across = arrived[2][quarter:]
-        riders = {1: (across,), 2: (far, across[-16:]), 3: (across,)}
+        extent = far.shape[0] // 4
+        starts = near_starts(lax.axis_index("tile") ^ 1, extent)
+        direct, one, three = [lax.dynamic_slice_in_dim(across, start, 2 * extent, 0) for start in starts]
+        riders = {1: (one,), 2: (far, across[-16:]), 3: (three,)}
     bit = 8
     while bit < total:
         mine = part.astype(wire)
@@ -412,15 +449,16 @@
                 got[m] = swap(message, m * bit, total)
             part = (mine.astype(F32) + got[1][:quarter].astype(F32)) + (got[2][:quarter].astype(F32) + got[3][:quarter].astype(F32))
             if near is not None:
-                extras = [across, got[1][quarter:], got[3][quarter:], got[2][quarter:-16], got[2][-16:]]
+                extras = [direct, got[1][quarter:], got[3][quarter:], got[2][quarter:-16], got[2][-16:]]
             bit *= 4
         else:
             part = mine.astype(F32) + swap(mine, bit, total).astype(F32)
             bit *= 2
+    part, done = lax.optimization_barrier((part, done))
     mine = part.astype(wire)
     ring = jnp.stack([mine] + [swap(mine, m << 1, total) for m in (1, 2, 3)])
     whole = jnp.concatenate([lax.dynamic_index_in_dim(ring, plane ^ j, 0) for j in range(4)], axis=0)
-    return whole, extras
+    return whole, extras, done
 
 
 def join_cores(whole, total):
@@ -429,16 +467,8 @@
     return jnp.where(low, whole, other), jnp.where(low, other, whole)
 
 
-def relay(near, far, total):
-    across = swap(near, 4, total)
-    three = swap(across, 24, total)
-    two = swap(jnp.concatenate([far, across[-16:]], axis=0), 16, total)
-    one = swap(across, 8, total)
-    return [across, one, three, two[:-16], two[-16:]]
-
-
-def relay_direct(near, far, total):
-    return [swap(near, 4, total), swap(near, 12, total), swap(near, 28, total), swap(far, 16, total), swap(near[-16:], 20, total)]
+def reach_neighbours(across, one, three, far, corners, total):
+    return [swap(across, 4, total), swap(one, 12, total), swap(three, 28, total), swap(far, 16, total), swap(corners, 20, total)]
 
 
 def per_device(inputs, weight_one, weight_two, cotangent, edge_code, corner_code):
@@ -453,17 +483,30 @@
     plan = routes(tiles)
     total = tiles * members
     hops = relayed(tiles)
+    near_b, far_b, corner_b = sds((4 * extent + 16, channels), BF16), sds((4 * extent, channels), BF16), sds((16, channels), BF16)
+    pair_b = sds((2 * extent, channels), BF16)
     if hops:
-        routed = [sds((4 * extent + 16, channels), BF16), sds((4 * extent, channels), BF16)]
+        first_routed, second_routed = [pair_b, pair_b, pair_b, far_b, corner_b], [near_b, far_b]
         n_routes = 5
     else:
-        routed = [sds((route_rows(r, extent), channels), BF16) for r in plan]
+        first_routed = second_routed = [sds((route_rows(r, extent), channels), BF16) for r in plan]
         n_routes = len(plan)
-    n_routed = len(routed)
-
-    def write(a, b, outs):
+    n_first, n_second = len(first_routed), len(second_routed)
+
+    def write_first(a, b, outs, near_ref):
         if hops:
-            write_relay(a, b, *outs, extent)
+            write_near(a, b, near_ref, extent)
+            write_far(a, b, outs[3], extent)
+            for start, out in zip(near_starts(lax.axis_index("tile"), extent), outs):
+                out[...] = near_ref[pl.ds(pl.multiple_of(start, 16), 2 * extent), :]
+            outs[4][...] = near_ref[4 * extent : 4 * extent + 16, :]
+        else:
+            write_routes(a, b, plan, outs, extent)
+
+    def write_second(a, b, outs):
+        if hops:
+            write_near(a, b, outs[0], extent)
+            write_far(a, b, outs[1], extent)
         else:
             write_routes(a, b, plan, outs, extent)
 
@@ -476,51 +519,99 @@
     turned_b = sds((channels, count), BF16)
     conv = 2 * count * 9 * channels * channels
 
-    def first_strips(edge_ref, corner_ref, x_ref, g_ref, *outs):
+    strip_rows = block_starts(extent)[3] + extent
+    choice_b = sds((strip_rows, count), BF16)
+    scatter_b, column_b = sds((count, strip_rows), BF16), sds((count, 4 * extent), BF16)
+    pieces = 2
+
+    def first_strips(x_hbm, g_hbm, edge_hbm, corner_hbm, *refs):
+        outs = refs[:n_first]
+        x_ref, g_ref, near_ref, edge_ref, corner_ref, sems = refs[n_first:]
+        pairs = [(edge_hbm, edge_ref), (corner_hbm, corner_ref)]
+        step = count // pieces
+        for source_ref, target_ref in ((x_hbm, x_ref), (g_hbm, g_ref)):
+            for i in range(pieces):
+                pairs.append((source_ref.at[pl.ds(i * step, step)], target_ref.at[pl.ds(i * step, step)]))
+        copies = [pltpu.make_async_copy(a, b, sems.at[i]) for i, (a, b) in enumerate(pairs)]
+        for copy in copies:
+            copy.start()
+        fixed = block_choice(*fixed_lines(extent), extent)
+        for copy in copies[:2]:
+            copy.wait()
+        seam = block_choice(*seam_lines(edge_ref, corner_ref, extent), extent)
+        for copy in copies[2:]:
+            copy.wait()
+        a = gather_blocks(seam, x_ref[...], extent)
+        b = gather_blocks(fixed, g_ref[...], extent)
+        write_first(a, b, outs, near_ref)
+
+    first = call(
+        first_strips,
+        "first_strips",
+        first_routed,
+        "aaaa",
+        (source, grad_out, edge_code.T, corner_code.T),
+        scratch=[
+            pltpu.VMEM((count, channels), BF16),
+            pltpu.VMEM((count, channels), BF16),
+            pltpu.VMEM(near_b.shape, BF16),
+            pltpu.SMEM((4, tiles), jnp.int32),
+            pltpu.SMEM((4, tiles), jnp.int32),
+            pltpu.SemaphoreType.DMA((2 + 2 * pieces,)),
+        ],
+        limit=ALONE,
+        flops=10 * conv,
+    )
+    first_arrived = reach_neighbours(*first, total) if hops else exchange(first, plan, tiles)
+
+    def selections(edge_ref, corner_ref, seam_ref, fixed_ref, scatter_ref, column_ref):
         lines, pixels = seam_lines(edge_ref, corner_ref, extent)
-        a = gather_blocks(x_ref[...], lines, pixels, extent)
-        b = gather_blocks(g_ref[...], *fixed_lines(extent), extent)
-        write(a, b, outs)
-
-    first = call(first_strips, "first_strips", routed, "ssvv", (edge_code, corner_code, source, grad_out))
-    first_arrived = relay(*first, total) if hops else exchange(first, plan, tiles)
-
-    def inner(x_ref, g_ref, w1_ref, w2_ref, pre_ref, dh_ref, xt_ref, qg_ref, w1t_ref, w2t_ref, qx_ref):
-        transpose_taps(w1t_ref, w1_ref)
-        transpose_taps(w2t_ref, w2_ref)
+        seam_ref[...] = block_choice(lines, pixels, extent)
+        scatter_ref[...] = seam_scatter(lines, pixels, extent)
+        fixed_ref[...] = block_choice(*fixed_lines(extent), extent)
+        column_ref[...] = column_scatter(extent)
+
+    seam, fixed, scatter, column = call(
+        selections,
+        "selections",
+        [choice_b, choice_b, scatter_b, column_b],
+        "ss",
+        (edge_code.T, corner_code.T),
+    )
+
+    def inner(x_ref, g_ref, w1_ref, w2_ref, pre_ref, dh_ref, xt_ref, qg_ref, qx_ref):
         write_columns(qx_ref, x_ref[...], True, extent)
         pre_ref[...] = window_product(qx_ref, w1_ref[...], True, extent)
         write_columns(qg_ref, g_ref[...], False, extent)
-        dh_ref[...] = window_product(qg_ref, w2t_ref[...], False, extent)
+        dh_ref[...] = window_product(qg_ref, w2_ref[...], False, extent)
         xt_ref[...] = jnp.transpose(x_ref[...].astype(F32)).astype(BF16)
 
-    pre, dh, xt, qg, w1t, w2t = call(
+    pre, dh, xt, qg = call(
         inner,
         "inner_products",
-        [image_f, image_f, turned_b, columns_b, taps_b, taps_b],
+        [image_f, image_f, turned_b, columns_b],
         "vvvv",
         (source, grad_out, w_one, w_two),
         scratch=[pltpu.VMEM(columns_b.shape, BF16)],
         flops=2 * conv,
     )
 
-    def middle(edge_ref, corner_ref, pre_ref, dh_ref, xt_ref, qg_ref, w1_ref, w2t_ref, *refs):
+    def middle(seam_ref, fixed_ref, scatter_ref, column_ref, pre_ref, dh_ref, xt_ref, qg_ref, w1_ref, w2_ref, *refs):
         arrived = refs[:n_routes]
         keep_ref, send_ref, hid_ref, dpre_ref = refs[n_routes : n_routes + 4]
-        outs = refs[n_routes + 4 : n_routes + 4 + n_routed]
-        qd_ref, sum_ref = refs[n_routes + 4 + n_routed :]
-        lines, pixels = seam_lines(edge_ref, corner_ref, extent)
+        outs = refs[n_routes + 4 : n_routes + 4 + n_second]
+        qd_ref, sum_ref = refs[n_routes + 4 + n_second :]
         x_strips, g_strips = read(arrived)
         columns = strip_columns(g_strips, extent)
-        value, slope = gelu_parts(pre_ref[...] + margin_forward(x_strips, w1_ref[...], extent))
+        value, slope = gelu_parts(pre_ref[...] + margin_forward(x_strips, w1_ref[...], column_ref[...], extent))
         hidden = value.astype(BF16)
         hid_ref[...] = hidden
-        d_hidden = dh_ref[...] + margin_backward(columns, w2t_ref[...], lines, pixels, extent)
+        d_hidden = dh_ref[...] + margin_backward(columns, w2_ref[...], scatter_ref[...], extent)
         d_pre = (d_hidden * slope).astype(BF16)
         dpre_ref[...] = d_pre
-        a = gather_blocks(hidden, lines, pixels, extent)
-        b = gather_blocks(d_pre, *fixed_lines(extent), extent)
-        write(a, b, outs)
+        a = gather_blocks(seam_ref[...], hidden, extent)
+        b = gather_blocks(fixed_ref[...], d_pre, extent)
+        write_second(a, b, outs)
         write_columns(qd_ref, d_pre, False, extent)
         weight_sum(sum_ref.at[0], xt_ref[...], qd_ref, x_strips, strip_columns(b, extent), extent)
         weight_sum(sum_ref.at[1], jnp.transpose(value).astype(BF16), qg_ref, a, columns, extent)
@@ -531,40 +622,55 @@
     results = call(
         middle,
         "gradients",
-        [taps_f, taps_b, image_b, image_b] + routed,
-        "ss" + "v" * (6 + n_routes),
-        (edge_code, corner_code, pre, dh, xt, qg, w_one, w2t, *first_arrived),
+        [taps_f, taps_b, image_b, image_b] + second_routed,
+        "v" * (10 + n_routes),
+        (seam, fixed, scatter, column, pre, dh, xt, qg, w_one, w_two, *first_arrived),
         scratch=[pltpu.VMEM(columns_b.shape, BF16), pltpu.VMEM((2,) + taps_f.shape, F32)],
         flops=2 * conv,
     )
     keep, send, hidden, d_pre = results[:4]
+    def later(edge_ref, corner_ref, x_ref, g_ref, hid_ref, dpre_ref, w1_ref, w2_ref, out_ref, dx_ref, scatter_ref, column_ref, q_ref):
+        lines, pixels = seam_lines(edge_ref, corner_ref, extent)
+        scatter_ref[...] = seam_scatter(lines, pixels, extent)
+        column_ref[...] = column_scatter(extent)
+        write_columns(q_ref, hid_ref[...], True, extent)
+        out_ref[...] = x_ref[...].astype(F32) + window_product(q_ref, w2_ref[...], True, extent)
+        write_columns(q_ref, dpre_ref[...], False, extent)
+        dx_ref[...] = g_ref[...].astype(F32) + window_product(q_ref, w1_ref[...], False, extent)
+
+    def later_parts(token):
+        token, inner_arrays = lax.optimization_barrier((token, (hidden, d_pre)))
+        return token, call(
+            later,
+            "later_products",
+            [image_f, image_f, scatter_b, column_b],
+            "ssvvvvvv",
+            (edge_code.T, corner_code.T, source, grad_out, *inner_arrays, w_one, w_two),
+            scratch=[pltpu.VMEM(columns_b.shape, BF16)],
+            flops=2 * conv,
+        )
+
     if hops:
-        whole, second_arrived = reduce_gradients(keep, send, total, *results[4:])
+        whole, second_arrived, parts = reduce_gradients(keep, send, total, later_parts, *results[4:])
     else:
         second_arrived = exchange(results[4:], plan, tiles)
-        whole, _ = reduce_gradients(keep, send, total)
-
-    def last(edge_ref, corner_ref, x_ref, g_ref, hid_ref, dpre_ref, w2_ref, w1t_ref, *refs):
+        whole, _, parts = reduce_gradients(keep, send, total, later_parts)
+
+    def last(part_ref, dpart_ref, scatter_ref, column_ref, w1_ref, w2_ref, *refs):
         arrived = refs[:n_routes]
-        out_ref, dx_ref, q_ref = refs[n_routes:]
-        lines, pixels = seam_lines(edge_ref, corner_ref, extent)
+        out_ref, dx_ref = refs[n_routes:]
         h_strips, d_strips = read(arrived)
-        write_columns(q_ref, hid_ref[...], True, extent)
-        total = window_product(q_ref, w2_ref[...], True, extent) + margin_forward(h_strips, w2_ref[...], extent)
-        out_ref[...] = (x_ref[...].astype(F32) + total).astype(BF16)
-        write_columns(q_ref, dpre_ref[...], False, extent)
-        total = window_product(q_ref, w1t_ref[...], False, extent)
-        total = total + margin_backward(strip_columns(d_strips, extent), w1t_ref[...], lines, pixels, extent)
-        dx_ref[...] = (g_ref[...].astype(F32) + total).astype(BF16)
+        out_ref[...] = (part_ref[...] + margin_forward(h_strips, w2_ref[...], column_ref[...], extent)).astype(BF16)
+        add = margin_backward(strip_columns(d_strips, extent), w1_ref[...], scatter_ref[...], extent)
+        dx_ref[...] = (dpart_ref[...] + add).astype(BF16)
 
     output, d_input = call(
         last,
         "outputs",
         [image_b, image_b],
-        "ss" + "v" * (6 + n_routes),
-        (edge_code, corner_code, source, grad_out, hidden, d_pre, w_two, w1t, *second_arrived),
-        scratch=[pltpu.VMEM(columns_b.shape, BF16)],
-        flops=2 * conv,
+        "v" * (6 + n_routes),
+        (*parts, w_one, w_two, *second_arrived),
+        flops=conv // 4,
     )
     whole, output, d_input = lax.optimization_barrier((whole, output, d_input))
     one, two = join_cores(whole, total)

time: 55.8 us -> 49.5 us (0.89)
  waiting for transfers between devices: 22.4 us -> 14.7 us
  starting transfers between devices: 18.5 us -> 21.4 us
  local copies, waits for them, and re-layouts: 2.85 us -> 0.09 us
  Pallas kernels: 9.52 us -> 10.9 us
    ppermute x15 -> x16, waiting for transfers between devices: 22.4 us -> 14.7 us  [swap(): return lax.ppermute(value, AXES, [(i, i ^ mask) for i in range(total)])]
    ppermute x15 -> x16, starting transfers between devices: 18.5 us -> 21.4 us  [swap(): return lax.ppermute(value, AXES, [(i, i ^ mask) for i in range(total)])]
    unnamed x16 -> x14, local copies, waits for them, and re-layouts: 2.76 us -> 0.03 us
    pallas_call x4 -> x6, Pallas kernels: 9.52 us -> 10.9 us  [call(): pl.pallas_call(kernel, name=name, out_shape=outs, in_specs=specs, out_spe...]
  transfers between devices with their start and end apart: 15 -> 16, of which waited for: 12 -> 8; matrix products, arithmetic and copies ran while one was open for 0% -> 0% of each run, Pallas kernels for 9% -> 12%
where the time goes in v3:
time: 49.5 us; the launch traced here: 49.3 us
  starting transfers between devices  21.4 us (43%)
  waiting for transfers between devices  14.7 us (30%)
  Pallas kernels  10.9 us (22%)
  other arithmetic  1.39 us (3%)
  between operations  0.88 us (2%)
    ppermute x16, starting transfers between devices, swap(): return lax.ppermute(value, AXES, [(i, i ^ mask) for i in range(total)])  21.4 us
    ppermute x16, waiting for transfers between devices, swap(): return lax.ppermute(value, AXES, [(i, i ^ mask) for i in range(total)])  14.7 us
    pallas_call x6, Pallas kernels, call(): pl.pallas_call(kernel, name=name, out_shape=outs, in_specs=specs, out_spe...  10.9 us
    mul x1, other arithmetic, per_device(): two.astype(F32) * factor  1.13 us
  transfers between devices with their start and end apart: 16, of which 8 were waited for; matrix products, arithmetic and copies ran while one was open for 0% of the time, Pallas kernels for 12%

profile of v3, /device:TPU:0, one launch (start us, length us, event | category | flops | bytes accessed | tf_op | source)
XLA Modules:
  0.0 49.3 jit_solution(15970113844959842111)
XLA Ops:
  0.7 2.2 %first_strips.1 = (bf16[64,128]{1,0:T(8,128)(2,1)}, bf16[64,128]{1,0:T(8,128)(2,1)}, bf16[64,128]{1,0:T(8,128)(2,1)}, bf16[128,128]{1,0:T(8,128)(2,1)}, bf16[16,128]{1,0:T(8,128)(2,1)}) custom-call(bf16[1024,128]{1,0:T(8,128)(2,1)} %bitcast.44, bf16[1024,128]{1,0:T(8,128)(2,1)} %bitcast.47, s32[4,8]{1,0:T(4,128)} %bitcast.38, s32[4,8]{1,0:T(4,128)} %bitcast.41), custom_call_target="tpu_custom_call" | custom-call | flops 3019898880 | bytes 610560 | tf_op jit(solution)/shard_map/first_strips/pallas_call | solution.py:384
  2.9 4.1 %collective-permute-start.3 = (bf16[128,128]{1,0:T(8,128)(2,1)}, bf16[128,128]{1,0:T(8,128)(2,1)S(1)}, u32[]{:S(2)}, u32[]{:S(2)}) collective-permute-start(bf16[128,128]{1,0:T(8,128)(2,1)} %get-tuple-element.51), channel_id=1, source_target_pairs={{0,16},{1,17},{2,18},{3,19},{4,20},{5,21},{6,22},{7,23},{8,24},{9,... | collective-permute-start | bytes 98312 | tf_op jit(solution)/shard_map/ppermute | solution.py:407
  7.0 1.5 %collective-permute-start = (bf16[64,128]{1,0:T(8,128)(2,1)}, bf16[64,128]{1,0:T(8,128)(2,1)S(1)}, u32[]{:S(2)}, u32[]{:S(2)}) collective-permute-start(bf16[64,128]{1,0:T(8,128)(2,1)} %get-tuple-element.48), channel_id=1, source_target_pairs={{0,4},{1,5},{2,6},{3,7},{4,0},{5,1},{6,2},{7,3},{8,12},{9,13},{10,... | collective-permute-start | bytes 49160 | tf_op jit(solution)/shard_map/ppermute | solution.py:407
  8.5 1.5 %collective-permute-start.1 = (bf16[64,128]{1,0:T(8,128)(2,1)}, bf16[64,128]{1,0:T(8,128)(2,1)S(1)}, u32[]{:S(2)}, u32[]{:S(2)}) collective-permute-start(bf16[64,128]{1,0:T(8,128)(2,1)} %get-tuple-element.49), channel_id=1, source_target_pairs={{0,12},{1,13},{2,14},{3,15},{4,8},{5,9},{6,10},{7,11},{8,4},{9,5},... | collective-permute-start | bytes 49160 | tf_op jit(solution)/shard_map/ppermute | solution.py:407
  10.0 1.1 %collective-permute-start.2 = (bf16[64,128]{1,0:T(8,128)(2,1)}, bf16[64,128]{1,0:T(8,128)(2,1)S(1)}, u32[]{:S(2)}, u32[]{:S(2)}) collective-permute-start(bf16[64,128]{1,0:T(8,128)(2,1)} %get-tuple-element.50), channel_id=1, source_target_pairs={{0,28},{1,29},{2,30},{3,31},{4,24},{5,25},{6,26},{7,27},{8,20},{9,... | collective-permute-start | bytes 49160 | tf_op jit(solution)/shard_map/ppermute | solution.py:407
  11.2 1.7 %collective-permute-start.4 = (bf16[16,128]{1,0:T(8,128)(2,1)S(1)}, bf16[16,128]{1,0:T(8,128)(2,1)S(1)}, u32[]{:S(2)}, u32[]{:S(2)}) collective-permute-start(bf16[16,128]{1,0:T(8,128)(2,1)S(1)} %copy-done.6), channel_id=1, source_target_pairs={{0,20},{1,21},{2,22},{3,23},{4,16},{5,17},{6,18},{7,19},{8,28},{9,... | collective-permute-start | bytes 12296 | tf_op jit(solution)/shard_map/ppermute | solution.py:407
  12.9 1.4 %inner_products.1 = (f32[1024,128]{1,0:T(8,128)S(1)}, f32[1024,128]{1,0:T(8,128)S(1)}, bf16[128,1024]{1,0:T(8,128)(2,1)S(1)}, bf16[1088,384]{1,0:T(8,128)(2,1)S(1)}) custom-call(bf16[1024,128]{1,0:T(8,128)(2,1)S(1)} %bitcast.45, bf16[1024,128]{1,0:T(8,128)(2,1)S(1)} %bitcast.48, bf16[1152,128]{1,0:T(8,128)(2,1)S(1)} %bitcast.28, bf16[1152,128]{1,0:T(8,128)(2,1)S(1)} %bitcast.32), custom_call_target="tpu_custom_call" | custom-call | flops 603979776 | bytes 3260416 | tf_op jit(solution)/shard_map/inner_products/pallas_call | solution.py:384
  14.3 0.9 %selections.1 = (bf16[160,1024]{1,0:T(8,128)(2,1)S(1)}, bf16[160,1024]{1,0:T(8,128)(2,1)S(1)}, bf16[1024,160]{1,0:T(8,128)(2,1)S(1)}, bf16[1024,128]{1,0:T(8,128)(2,1)S(1)}) custom-call(s32[4,8]{1,0:T(4,128)S(1)} %bitcast.39, s32[4,8]{1,0:T(4,128)S(1)} %bitcast.42), custom_call_target="tpu_custom_call" | custom-call | bytes 1245440 | tf_op jit(solution)/shard_map/selections/pallas_call | solution.py:384
  15.2 1.5 %collective-permute-done.4.refs_4_ = bf16[16,128]{1,0:T(8,128)(2,1)S(1)} collective-permute-done((bf16[16,128]{1,0:T(8,128)(2,1)S(1)}, bf16[16,128]{1,0:T(8,128)(2,1)S(1)}, u32[]{:S(2)}, u32[]{:S(2)}) %collective-permute-start.4) | collective-permute-done | bytes 4128 | tf_op jit(solution)/shard_map/ppermute | solution.py:407
  16.8 2.6 %gradients.1 = (f32[1152,128]{1,0:T(8,128)S(1)}, bf16[1152,128]{1,0:T(8,128)(2,1)S(1)}, bf16[1024,128]{1,0:T(8,128)(2,1)S(1)}, bf16[1024,128]{1,0:T(8,128)(2,1)S...) custom-call(bf16[160,1024]{1,0:T(8,128)(2,1)S(1)} %get-tuple-element.40.seam_ref, ...), custom_call_target="tpu_custom_call" | custom-call | flops 603979776 | bytes 5545984 | tf_op jit(solution)/shard_map/gradients/pallas_call | solution.py:384
  19.4 0.1 collective-permute-start.5
  19.5 1.5 %collective-permute-done.5 = bf16[1152,128]{1,0:T(8,128)(2,1)S(1)} collective-permute-done((bf16[1152,128]{1,0:T(8,128)(2,1)S(1)}, bf16[1152,128]{1,0:T(8,128)(2,1)S(1)}, u32[]{:S(2)}, u32[]{:S(2)}) %collective-permute-start.5) | collective-permute-done | bytes 294944 | tf_op jit(solution)/shard_map/ppermute | solution.py:407
  21.0 0.1 fusion.4
  21.1 1.4 %collective-permute-start.8 = (bf16[432,128]{1,0:T(8,128)(2,1)S(1)}, bf16[432,128]{1,0:T(8,128)(2,1)S(1)}, u32[]{:S(2)}, u32[]{:S(2)}) collective-permute-start(bf16[432,128]{1,0:T(8,128)(2,1)S(1)} %pad_maximum_fusion.2), channel_id=1, source_target_pairs={{0,4},{1,5},{2,6},{3,7},{4,0},{5,1},{6,2},{7,3},{8,12},{9,13},{10,... | collective-permute-start | bytes 331784 | tf_op jit(solution)/shard_map/ppermute | solution.py:407
  22.5 1.6 %collective-permute-start.6 = (bf16[288,128]{1,0:T(8,128)(2,1)S(1)}, bf16[288,128]{1,0:T(8,128)(2,1)S(1)}, u32[]{:S(2)}, u32[]{:S(2)}) collective-permute-start(bf16[288,128]{1,0:T(8,128)(2,1)S(1)} %get-tuple-element.78), channel_id=1, source_target_pairs={{0,6},{1,7},{2,4},{3,5},{4,2},{5,3},{6,0},{7,1},{8,14},{9,15},{10,... | collective-permute-start | bytes 221192 | tf_op jit(solution)/shard_map/ppermute | solution.py:407
  24.1 0.5 %collective-permute-start.7 = (bf16[288,128]{1,0:T(8,128)(2,1)S(1)}, bf16[288,128]{1,0:T(8,128)(2,1)S(1)}, u32[]{:S(2)}, u32[]{:S(2)}) collective-permute-start(bf16[288,128]{1,0:T(8,128)(2,1)S(1)} %get-tuple-element.77), channel_id=1, source_target_pairs={{0,2},{1,3},{2,0},{3,1},{4,6},{5,7},{6,4},{7,5},{8,10},{9,11},{10,... | collective-permute-start | bytes 221192 | tf_op jit(solution)/shard_map/ppermute | solution.py:407
  24.6 4.3 %collective-permute-done.6 = bf16[288,128]{1,0:T(8,128)(2,1)S(1)} collective-permute-done((bf16[288,128]{1,0:T(8,128)(2,1)S(1)}, bf16[288,128]{1,0:T(8,128)(2,1)S(1)}, u32[]{:S(2)}, u32[]{:S(2)}) %collective-permute-start.6) | collective-permute-done | bytes 73760 | tf_op jit(solution)/shard_map/ppermute | solution.py:407
  28.9 0.6 %collective-permute-done.7 = bf16[288,128]{1,0:T(8,128)(2,1)S(1)} collective-permute-done((bf16[288,128]{1,0:T(8,128)(2,1)S(1)}, bf16[288,128]{1,0:T(8,128)(2,1)S(1)}, u32[]{:S(2)}, u32[]{:S(2)}) %collective-permute-start.7) | collective-permute-done | bytes 73760 | tf_op jit(solution)/shard_map/ppermute | solution.py:407
  29.6 1.6 %collective-permute-start.10 = (bf16[432,128]{1,0:T(8,128)(2,1)S(1)}, bf16[432,128]{1,0:T(8,128)(2,1)S(1)}, u32[]{:S(2)}, u32[]{:S(2)}) collective-permute-start(bf16[432,128]{1,0:T(8,128)(2,1)S(1)} %pad_maximum_fusion.3), channel_id=1, source_target_pairs={{0,16},{1,17},{2,18},{3,19},{4,20},{5,21},{6,22},{7,23},{8,24},{9,... | collective-permute-start | bytes 331784 | tf_op jit(solution)/shard_map/ppermute | solution.py:407
  31.2 2.0 %collective-permute-start.11 = (bf16[352,128]{1,0:T(8,128)(2,1)S(1)}, bf16[352,128]{1,0:T(8,128)(2,1)S(1)}, u32[]{:S(2)}, u32[]{:S(2)}) collective-permute-start(bf16[352,128]{1,0:T(8,128)(2,1)S(1)} %get-tuple-element.86), channel_id=1, source_target_pairs={{0,24},{1,25},{2,26},{3,27},{4,28},{5,29},{6,30},{7,31},{8,16},{9,... | collective-permute-start | bytes 270344 | tf_op jit(solution)/shard_map/ppermute | solution.py:407
  33.2 0.6 %collective-permute-start.9 = (bf16[352,128]{1,0:T(8,128)(2,1)S(1)}, bf16[352,128]{1,0:T(8,128)(2,1)S(1)}, u32[]{:S(2)}, u32[]{:S(2)}) collective-permute-start(bf16[352,128]{1,0:T(8,128)(2,1)S(1)} %get-tuple-element.85), channel_id=1, source_target_pairs={{0,8},{1,9},{2,10},{3,11},{4,12},{5,13},{6,14},{7,15},{8,0},{9,1},... | collective-permute-start | bytes 270344 | tf_op jit(solution)/shard_map/ppermute | solution.py:407
  33.8 2.2 %later_products.1 = (f32[1024,128]{1,0:T(8,128)S(1)}, f32[1024,128]{1,0:T(8,128)S(1)}, bf16[1024,160]{1,0:T(8,128)(2,1)S(1)}, bf16[1024,128]{1,0:T(8,128)(2,1)S(1)}) custom-call(s32[4,8]{1,0:T(4,128)S(1)} %bitcast.40, s32[4,8]{1,0:T(4,128)S(1)} %bitcast.43, bf16[1024,128]{1,0:T(8,128)(2,1)S(1)} %bitcast.46, bf16[1024,128]{1,0:T(8,128)(2,1)S(1)} %bitcast.49, ...), custom_call_target="tpu_custom_call" | custom-call | flops 603979776 | bytes 3277056 | tf_op jit(solution)/shard_map/later_products/pallas_call | solution.py:384
  36.0 1.8 %collective-permute-done.11 = bf16[352,128]{1,0:T(8,128)(2,1)S(1)} collective-permute-done((bf16[352,128]{1,0:T(8,128)(2,1)S(1)}, bf16[352,128]{1,0:T(8,128)(2,1)S(1)}, u32[]{:S(2)}, u32[]{:S(2)}) %collective-permute-start.11) | collective-permute-done | bytes 90144 | tf_op jit(solution)/shard_map/ppermute | solution.py:407
  37.8 1.6 %collective-permute-done.9 = bf16[352,128]{1,0:T(8,128)(2,1)S(1)} collective-permute-done((bf16[352,128]{1,0:T(8,128)(2,1)S(1)}, bf16[352,128]{1,0:T(8,128)(2,1)S(1)}, u32[]{:S(2)}, u32[]{:S(2)}) %collective-permute-start.9) | collective-permute-done | bytes 90144 | tf_op jit(solution)/shard_map/ppermute | solution.py:407
  39.5 0.6 %collective-permute-start.12 = (bf16[288,128]{1,0:T(8,128)(2,1)S(1)}, bf16[288,128]{1,0:T(8,128)(2,1)S(1)}, u32[]{:S(2)}, u32[]{:S(2)}) collective-permute-start(bf16[288,128]{1,0:T(8,128)(2,1)S(1)} %add_add_fusion), channel_id=1, source_target_pairs={{0,2},{1,3},{2,0},{3,1},{4,6},{5,7},{6,4},{7,5},{8,10},{9,11},{10,... | collective-permute-start | bytes 221192 | tf_op jit(solution)/shard_map/ppermute | solution.py:407
  40.1 1.1 %collective-permute-start.13 = (bf16[288,128]{1,0:T(8,128)(2,1)S(1)}, bf16[288,128]{1,0:T(8,128)(2,1)S(1)}, u32[]{:S(2)}, u32[]{:S(2)}) collective-permute-start(bf16[288,128]{1,0:T(8,128)(2,1)S(1)} %add_add_fusion), channel_id=1, source_target_pairs={{0,4},{1,5},{2,6},{3,7},{4,0},{5,1},{6,2},{7,3},{8,12},{9,13},{10,... | collective-permute-start | bytes 221192 | tf_op jit(solution)/shard_map/ppermute | solution.py:407
  41.2 1.9 %collective-permute-start.14 = (bf16[288,128]{1,0:T(8,128)(2,1)S(1)}, bf16[288,128]{1,0:T(8,128)(2,1)S(1)}, u32[]{:S(2)}, u32[]{:S(2)}) collective-permute-start(bf16[288,128]{1,0:T(8,128)(2,1)S(1)} %add_add_fusion), channel_id=1, source_target_pairs={{0,6},{1,7},{2,4},{3,5},{4,2},{5,3},{6,0},{7,1},{8,14},{9,15},{10,... | collective-permute-start | bytes 221192 | tf_op jit(solution)/shard_map/ppermute | solution.py:407
  43.0 1.6 %outputs.1 = (bf16[1024,128]{1,0:T(8,128)(2,1)}, bf16[1024,128]{1,0:T(8,128)(2,1)}) custom-call(f32[1024,128]{1,0:T(8,128)S(1)} %get-tuple-element.67.part_ref, f32[1024,128]{1,0:T(8,128)S(1)} %get-tuple-element.68.dpart_ref, bf16[1024,160]{1,0:T(8,128)(2,1)S(1)} %get-tuple-element.69.scatter_ref, bf16[1024,128]{1,0:T(8,128)(2,1)S(1)} %get-tuple-element.70.column_ref, ...), custom_call_target="tpu_custom_call" | custom-call | flops 75497472 | bytes 2838528 | tf_op jit(solution)/shard_map/outputs/pallas_call | solution.py:384
  44.7 1.7 %collective-permute-done.14 = bf16[288,128]{1,0:T(8,128)(2,1)S(1)} collective-permute-done((bf16[288,128]{1,0:T(8,128)(2,1)S(1)}, bf16[288,128]{1,0:T(8,128)(2,1)S(1)}, u32[]{:S(2)}, u32[]{:S(2)}) %collective-permute-start.14) | collective-permute-done | bytes 73760 | tf_op jit(solution)/shard_map/ppermute | solution.py:407
  46.6 0.1 collective-permute-start.15
  46.6 1.6 %collective-permute-done.15 = bf16[4,288,128]{2,1,0:T(8,128)(2,1)S(1)} collective-permute-done((bf16[4,288,128]{2,1,0:T(8,128)(2,1)S(1)}, bf16[4,288,128]{2,1,0:T(8,128)(2,1)S(1)}, u32[]{:S(2)}, u32[]{:S(2)}) %collective-permute-start.15) | collective-permute-done | bytes 294944 | tf_op jit(solution)/shard_map/ppermute | solution.py:407
  48.2 1.1 %convert_multiply_fusion = (f32[4,288,128]{2,1,0:T(8,128)}, f32[4,288,128]{2,1,0:T(8,128)}) fusion(bf16[4,288,128]{2,1,0:T(8,128)(2,1)S(1)} %collective-permute-done.15, bf16[4,288,128]{2,1,0:T(8,128)(2,1)S(1)} %pad_maximum_fusion.1, pred[]{:T(512)S(6)} %eq.16), kind=kLoop, calls=%fused_computation | loop fusion | flops 884736 | bytes 1769473 | tf_op jit(solution)/shard_map/mul | solution.py:682
  (37 shorter events, 0.3 us)
Async XLA Ops:
  0.6 12.2 %copy-start = (bf16[9,128,128]{2,1,0:T(8,128)(2,1)S(1)}, bf16[9,128,128]{2,1,0:T(8,128)(2,1)}, u32[]{:S(2)}) copy-start(bf16[9,128,128]{2,1,0:T(8,128)(2,1)} %param.7) | copy-start | bytes 884740
  0.6 12.2 %copy-start.1 = (bf16[9,128,128]{2,1,0:T(8,128)(2,1)S(1)}, bf16[9,128,128]{2,1,0:T(8,128)(2,1)}, u32[]{:S(2)}) copy-start(bf16[9,128,128]{2,1,0:T(8,128)(2,1)} %param.8) | copy-start | bytes 884740
  0.7 12.2 %copy-start.4 = (bf16[1,1,32,32,128]{4,3,2,1,0:T(8,128)(2,1)S(1)}, bf16[1,1,32,32,128]{4,3,2,1,0:T(8,128)(2,1)}, u32[]{:S(2)}) copy-start(bf16[1,1,32,32,128]{4,3,2,1,0:T(8,128)(2,1)} %param.6) | copy-start | bytes 786436
  0.7 12.2 %copy-start.5 = (bf16[1,1,32,32,128]{4,3,2,1,0:T(8,128)(2,1)S(1)}, bf16[1,1,32,32,128]{4,3,2,1,0:T(8,128)(2,1)}, u32[]{:S(2)}) copy-start(bf16[1,1,32,32,128]{4,3,2,1,0:T(8,128)(2,1)} %param.9) | copy-start | bytes 786436
  2.9 8.3 %copy-start.6 = (bf16[16,128]{1,0:T(8,128)(2,1)S(1)}, bf16[16,128]{1,0:T(8,128)(2,1)}, u32[]{:S(2)}) copy-start(bf16[16,128]{1,0:T(8,128)(2,1)} %get-tuple-element.52) | copy-start | bytes 12292
  2.9 13.9 %collective-permute-start.3 = (bf16[128,128]{1,0:T(8,128)(2,1)}, bf16[128,128]{1,0:T(8,128)(2,1)S(1)}, u32[]{:S(2)}, u32[]{:S(2)}) collective-permute-start(bf16[128,128]{1,0:T(8,128)(2,1)} %get-tuple-element.51), channel_id=1, source_target_pairs={{0,16},{1,17},{2,18},{3,19},{4,20},{5,21},{6,22},{7,23},{8,24},{9,... | collective-permute-start | bytes 98312 | tf_op jit(solution)/shard_map/ppermute | solution.py:407
  7.0 9.8 %collective-permute-start = (bf16[64,128]{1,0:T(8,128)(2,1)}, bf16[64,128]{1,0:T(8,128)(2,1)S(1)}, u32[]{:S(2)}, u32[]{:S(2)}) collective-permute-start(bf16[64,128]{1,0:T(8,128)(2,1)} %get-tuple-element.48), channel_id=1, source_target_pairs={{0,4},{1,5},{2,6},{3,7},{4,0},{5,1},{6,2},{7,3},{8,12},{9,13},{10,... | collective-permute-start | bytes 49160 | tf_op jit(solution)/shard_map/ppermute | solution.py:407
  8.5 8.3 %collective-permute-start.1 = (bf16[64,128]{1,0:T(8,128)(2,1)}, bf16[64,128]{1,0:T(8,128)(2,1)S(1)}, u32[]{:S(2)}, u32[]{:S(2)}) collective-permute-start(bf16[64,128]{1,0:T(8,128)(2,1)} %get-tuple-element.49), channel_id=1, source_target_pairs={{0,12},{1,13},{2,14},{3,15},{4,8},{5,9},{6,10},{7,11},{8,4},{9,5},... | collective-permute-start | bytes 49160 | tf_op jit(solution)/shard_map/ppermute | solution.py:407
  10.0 6.7 %collective-permute-start.2 = (bf16[64,128]{1,0:T(8,128)(2,1)}, bf16[64,128]{1,0:T(8,128)(2,1)S(1)}, u32[]{:S(2)}, u32[]{:S(2)}) collective-permute-start(bf16[64,128]{1,0:T(8,128)(2,1)} %get-tuple-element.50), channel_id=1, source_target_pairs={{0,28},{1,29},{2,30},{3,31},{4,24},{5,25},{6,26},{7,27},{8,20},{9,... | collective-permute-start | bytes 49160 | tf_op jit(solution)/shard_map/ppermute | solution.py:407
  11.2 5.6 %collective-permute-start.4 = (bf16[16,128]{1,0:T(8,128)(2,1)S(1)}, bf16[16,128]{1,0:T(8,128)(2,1)S(1)}, u32[]{:S(2)}, u32[]{:S(2)}) collective-permute-start(bf16[16,128]{1,0:T(8,128)(2,1)S(1)} %copy-done.6), channel_id=1, source_target_pairs={{0,20},{1,21},{2,22},{3,23},{4,16},{5,17},{6,18},{7,19},{8,28},{9,... | collective-permute-start | bytes 12296 | tf_op jit(solution)/shard_map/ppermute | solution.py:407
  12.8 1.4 %copy-start.2 = (s32[8,4]{0,1:T(4,128)S(1)}, s32[8,4]{0,1:T(4,128)}, u32[]{:S(2)}) copy-start(s32[8,4]{0,1:T(4,128)} %param.10) | copy-start | bytes 388
  12.9 1.4 %copy-start.3 = (s32[8,4]{0,1:T(4,128)S(1)}, s32[8,4]{0,1:T(4,128)}, u32[]{:S(2)}) copy-start(s32[8,4]{0,1:T(4,128)} %param.11) | copy-start | bytes 388
  19.4 1.6 %collective-permute-start.5 = (bf16[1152,128]{1,0:T(8,128)(2,1)S(1)}, bf16[1152,128]{1,0:T(8,128)(2,1)S(1)}, u32[]{:S(2)}, u32[]{:S(2)}) collective-permute-start(bf16[1152,128]{1,0:T(8,128)(2,1)S(1)} %get-tuple-element.54), channel_id=1, source_target_pairs={{0,1},{1,0},{2,3},{3,2},{4,5},{5,4},{6,7},{7,6},{8,9},{9,8},{10,11... | collective-permute-start | bytes 884744 | tf_op jit(solution)/shard_map/ppermute | solution.py:407
  21.1 8.4 %collective-permute-start.8 = (bf16[432,128]{1,0:T(8,128)(2,1)S(1)}, bf16[432,128]{1,0:T(8,128)(2,1)S(1)}, u32[]{:S(2)}, u32[]{:S(2)}) collective-permute-start(bf16[432,128]{1,0:T(8,128)(2,1)S(1)} %pad_maximum_fusion.2), channel_id=1, source_target_pairs={{0,4},{1,5},{2,6},{3,7},{4,0},{5,1},{6,2},{7,3},{8,12},{9,13},{10,... | collective-permute-start | bytes 331784 | tf_op jit(solution)/shard_map/ppermute | solution.py:407
  22.5 6.4 %collective-permute-start.6 = (bf16[288,128]{1,0:T(8,128)(2,1)S(1)}, bf16[288,128]{1,0:T(8,128)(2,1)S(1)}, u32[]{:S(2)}, u32[]{:S(2)}) collective-permute-start(bf16[288,128]{1,0:T(8,128)(2,1)S(1)} %get-tuple-element.78), channel_id=1, source_target_pairs={{0,6},{1,7},{2,4},{3,5},{4,2},{5,3},{6,0},{7,1},{8,14},{9,15},{10,... | collective-permute-start | bytes 221192 | tf_op jit(solution)/shard_map/ppermute | solution.py:407
  24.1 5.3 %collective-permute-start.7 = (bf16[288,128]{1,0:T(8,128)(2,1)S(1)}, bf16[288,128]{1,0:T(8,128)(2,1)S(1)}, u32[]{:S(2)}, u32[]{:S(2)}) collective-permute-start(bf16[288,128]{1,0:T(8,128)(2,1)S(1)} %get-tuple-element.77), channel_id=1, source_target_pairs={{0,2},{1,3},{2,0},{3,1},{4,6},{5,7},{6,4},{7,5},{8,10},{9,11},{10,... | collective-permute-start | bytes 221192 | tf_op jit(solution)/shard_map/ppermute | solution.py:407
  29.6 9.9 %collective-permute-start.10 = (bf16[432,128]{1,0:T(8,128)(2,1)S(1)}, bf16[432,128]{1,0:T(8,128)(2,1)S(1)}, u32[]{:S(2)}, u32[]{:S(2)}) collective-permute-start(bf16[432,128]{1,0:T(8,128)(2,1)S(1)} %pad_maximum_fusion.3), channel_id=1, source_target_pairs={{0,16},{1,17},{2,18},{3,19},{4,20},{5,21},{6,22},{7,23},{8,24},{9,... | collective-permute-start | bytes 331784 | tf_op jit(solution)/shard_map/ppermute | solution.py:407
  31.2 6.7 %collective-permute-start.11 = (bf16[352,128]{1,0:T(8,128)(2,1)S(1)}, bf16[352,128]{1,0:T(8,128)(2,1)S(1)}, u32[]{:S(2)}, u32[]{:S(2)}) collective-permute-start(bf16[352,128]{1,0:T(8,128)(2,1)S(1)} %get-tuple-element.86), channel_id=1, source_target_pairs={{0,24},{1,25},{2,26},{3,27},{4,28},{5,29},{6,30},{7,31},{8,16},{9,... | collective-permute-start | bytes 270344 | tf_op jit(solution)/shard_map/ppermute | solution.py:407
  33.2 6.2 %collective-permute-start.9 = (bf16[352,128]{1,0:T(8,128)(2,1)S(1)}, bf16[352,128]{1,0:T(8,128)(2,1)S(1)}, u32[]{:S(2)}, u32[]{:S(2)}) collective-permute-start(bf16[352,128]{1,0:T(8,128)(2,1)S(1)} %get-tuple-element.85), channel_id=1, source_target_pairs={{0,8},{1,9},{2,10},{3,11},{4,12},{5,13},{6,14},{7,15},{8,0},{9,1},... | collective-permute-start | bytes 270344 | tf_op jit(solution)/shard_map/ppermute | solution.py:407
  39.5 5.2 %collective-permute-start.12 = (bf16[288,128]{1,0:T(8,128)(2,1)S(1)}, bf16[288,128]{1,0:T(8,128)(2,1)S(1)}, u32[]{:S(2)}, u32[]{:S(2)}) collective-permute-start(bf16[288,128]{1,0:T(8,128)(2,1)S(1)} %add_add_fusion), channel_id=1, source_target_pairs={{0,2},{1,3},{2,0},{3,1},{4,6},{5,7},{6,4},{7,5},{8,10},{9,11},{10,... | collective-permute-start | bytes 221192 | tf_op jit(solution)/shard_map/ppermute | solution.py:407
  40.1 4.6 %collective-permute-start.13 = (bf16[288,128]{1,0:T(8,128)(2,1)S(1)}, bf16[288,128]{1,0:T(8,128)(2,1)S(1)}, u32[]{:S(2)}, u32[]{:S(2)}) collective-permute-start(bf16[288,128]{1,0:T(8,128)(2,1)S(1)} %add_add_fusion), channel_id=1, source_target_pairs={{0,4},{1,5},{2,6},{3,7},{4,0},{5,1},{6,2},{7,3},{8,12},{9,13},{10,... | collective-permute-start | bytes 221192 | tf_op jit(solution)/shard_map/ppermute | solution.py:407
  41.2 5.3 %collective-permute-start.14 = (bf16[288,128]{1,0:T(8,128)(2,1)S(1)}, bf16[288,128]{1,0:T(8,128)(2,1)S(1)}, u32[]{:S(2)}, u32[]{:S(2)}) collective-permute-start(bf16[288,128]{1,0:T(8,128)(2,1)S(1)} %add_add_fusion), channel_id=1, source_target_pairs={{0,6},{1,7},{2,4},{3,5},{4,2},{5,3},{6,0},{7,1},{8,14},{9,15},{10,... | collective-permute-start | bytes 221192 | tf_op jit(solution)/shard_map/ppermute | solution.py:407
  46.6 1.6 %collective-permute-start.15 = (bf16[4,288,128]{2,1,0:T(8,128)(2,1)S(1)}, bf16[4,288,128]{2,1,0:T(8,128)(2,1)S(1)}, u32[]{:S(2)}, u32[]{:S(2)}) collective-permute-start(bf16[4,288,128]{2,1,0:T(8,128)(2,1)S(1)} %pad_maximum_fusion.1), channel_id=1, source_target_pairs={{0,1},{1,0},{2,3},{3,2},{4,5},{5,4},{6,7},{7,6},{8,9},{9,8},{10,11... | collective-permute-start | bytes 884744 | tf_op jit(solution)/shard_map/ppermute | solution.py:407

commit v4 on v3

--- a/solution.py
+++ b/solution.py
@@ -119,16 +119,21 @@
     return jnp.concatenate(rows, axis=0)
 
 
-def seam_scatter(lines, pixels, extent):
+def block_index(lines, pixels, axis, extent):
     starts = block_starts(extent)
-    lane = iota((1, starts[3] + extent), 1)
-    index = jnp.full(lane.shape, -1, jnp.int32)
+    total = starts[3] + extent
+    place = iota((total, 1) if axis == 0 else (1, total), axis)
+    index = jnp.full(place.shape, -1, jnp.int32)
     for start, (side, ends) in zip(starts, BLOCKS):
         base, step = lines[side]
-        index = jnp.where((lane >= start) & (lane < start + extent), base + step * (lane - start), index)
+        index = jnp.where((place >= start) & (place < start + extent), base + step * (place - start), index)
         for i, q in enumerate(ends):
-            index = jnp.where(lane == start + extent + i, pixels[q], index)
-    return (iota((extent * extent, 1), 0) == index).astype(F32).astype(BF16)
+            index = jnp.where(place == start + extent + i, pixels[q], index)
+    return index
+
+
+def seam_scatter(lines, pixels, extent):
+    return (iota((extent * extent, 1), 0) == block_index(lines, pixels, 1, extent)).astype(F32).astype(BF16)
 
 
 def column_scatter(extent):
@@ -304,9 +309,8 @@
     return high, (values - high.astype(F32)).astype(BF16)
 
 
-def margin_forward(strips, weight, columns, extent):
+def margin_adds(strips, weight, extent):
     channels = strips[0].shape[1]
-    count = extent * extent
     adds = []
     for position, (side, ends) in enumerate(BLOCKS):
         middle = strips[position][:extent].astype(F32)
@@ -319,6 +323,12 @@
         right = jnp.where(row == extent - 1, after, pltpu.roll(middle, extent - 1, 0))
         window = jnp.concatenate([left, middle, right], axis=1).astype(BF16)
         adds.append(dot(window, tap_weight(weight, block_taps(position), channels)))
+    return adds
+
+
+def margin_forward(strips, weight, columns, extent):
+    count = extent * extent
+    adds = margin_adds(strips, weight, extent)
     spread = jnp.concatenate(list(halves(adds[2])) + list(halves(adds[3])), axis=0)
     image = dot(columns, spread)
     top = image[:extent] + adds[0]
@@ -351,22 +361,82 @@
     return dot(scatter, high) + dot(scatter, low)
 
 
-def weight_sum(out_ref, image_t, q_ref, strips, columns, extent):
+def weight_sum(out_ref, image_t, q_ref, extent):
     channels = image_t.shape[0]
     count = image_t.shape[1]
-    wide = [dot_t(strips[i], columns[i]) for i in range(4)]
     for a in range(3):
-        rows = q_ref[(2 - a) * extent : (2 - a) * extent + count, :]
-        product = dot(image_t, rows)
+        product = dot(image_t, q_ref[(2 - a) * extent : (2 - a) * extent + count, :])
         for b in range(3):
             tap = 3 * a + b
-            value = product[:, b * channels : (b + 1) * channels]
-            for position in range(4):
-                taps = block_taps(position)
-                if tap in taps:
-                    at = taps.index(tap)
-                    value = value + wide[position][:, at * channels : (at + 1) * channels]
-            out_ref[tap * channels : (tap + 1) * channels, :] = value
+            out_ref[tap * channels : (tap + 1) * channels, :] = product[:, b * channels : (b + 1) * channels]
+
+
+def margin_weight(strips, columns):
+    channels = strips[0].shape[1]
+    wide = [dot_t(strips[i], columns[i]) for i in range(4)]
+    result = []
+    for tap in range(9):
+        value = None
+        for position in range(4):
+            taps = block_taps(position)
+            if tap in taps:
+                at = taps.index(tap)
+                part = wide[position][:, at * channels : (at + 1) * channels]
+                value = part if value is None else value + part
+        result.append(value)
+    return result
+
+
+def border_index(place, extent, unique):
+    last = extent - 1
+    part, j = place // extent, place % extent
+    index = jnp.where(part == 0, j, jnp.where(part == 1, extent * last + j, jnp.where(part == 2, extent * j + last, extent * j)))
+    if unique:
+        index = jnp.where((part >= 2) & ((j == 0) | (j == last)), -2, index)
+    return index
+
+
+def border_choice(extent):
+    return pick_rows(border_index(iota((4 * extent, 1), 0), extent, True), extent * extent)
+
+
+def border_of(ref, extent):
+    count = extent * extent
+    east = ref[pl.ds(extent - 1, extent, stride=extent), :]
+    west = ref[pl.ds(0, extent, stride=extent), :]
+    return jnp.concatenate([ref[0:extent, :], ref[count - extent : count, :], east, west], axis=0)
+
+
+def without_repeats(border, extent):
+    place = iota((border.shape[0], 1), 0)
+    return jnp.where(border_index(place, extent, True) < 0, 0.0, border)
+
+
+def moved(column, by, extent):
+    if by == 0:
+        return column
+    row = iota((extent, 1), 0)
+    return jnp.where(row == (extent - 1 if by == 1 else 0), 0.0, pltpu.roll(column, (-by) % extent, 0))
+
+
+def border_windows(out_ref, wide_ref, q_ref, forward, extent):
+    count, channels = wide_ref.shape
+    columns = {c: wide_ref[pl.ds(c, extent, stride=extent), :] for c in (0, 1, extent - 2, extent - 1)}
+    nothing = jnp.zeros((extent, channels), F32)
+    row = iota((extent, 1), 0)
+    inside = (row > 0) & (row < extent - 1)
+    for a in range(3):
+        start = (a if forward else 2 - a) * extent
+        lanes = slice(a * 3 * channels, (a + 1) * 3 * channels)
+        out_ref[0:extent, lanes] = q_ref[start : start + extent, :]
+        out_ref[extent : 2 * extent, lanes] = q_ref[start + count - extent : start + count, :]
+        for part, column in ((2, extent - 1), (3, 0)):
+            pieces = []
+            for b in range(3):
+                at = column + (b - 1 if forward else 1 - b)
+                pieces.append(moved(columns[at], a - 1 if forward else 1 - a, extent) if at in columns else nothing)
+            value = jnp.where(inside, jnp.concatenate(pieces, axis=1), 0.0)
+            out_ref[part * extent : (part + 1) * extent, lanes] = value.astype(BF16)
 
 
 def gelu_parts(u):
@@ -516,11 +586,9 @@
     image_b, image_f = sds((count, channels), BF16), sds((count, channels), F32)
     columns_b = sds((count + 2 * extent, 3 * channels), BF16)
     taps_b, taps_f = sds((9 * channels, channels), BF16), sds((9 * channels, channels), F32)
-    turned_b = sds((channels, count), BF16)
     conv = 2 * count * 9 * channels * channels
 
     strip_rows = block_starts(extent)[3] + extent
-    choice_b = sds((strip_rows, count), BF16)
     scatter_b, column_b = sds((count, strip_rows), BF16), sds((count, 4 * extent), BF16)
     pieces = 2
 
@@ -564,57 +632,116 @@
     )
     first_arrived = reach_neighbours(*first, total) if hops else exchange(first, plan, tiles)
 
-    def selections(edge_ref, corner_ref, seam_ref, fixed_ref, scatter_ref, column_ref):
+    border = 4 * extent
+    border_b, border_f = sds((border, channels), BF16), sds((border, channels), F32)
+    windows_b = sds((border, 9 * channels), BF16)
+
+    def inner(edge_ref, corner_ref, x_ref, g_ref, w1_ref, w2_ref, *refs):
+        hid_ref, dpre_ref, preb_ref, dhb_ref, sum_ref, seam_ref, back_ref, wx_ref, wg_ref = refs[:9]
+        qx_ref, qg_ref, qd_ref, pre_ref, dh_ref, wide_ref = refs[9:]
+        wide_ref[...] = x_ref[...].astype(F32)
+        write_columns(qx_ref, x_ref[...], True, extent)
+        border_windows(wx_ref, wide_ref, qx_ref, True, extent)
+        pre_ref[...] = window_product(qx_ref, w1_ref[...], True, extent)
+        wide_ref[...] = g_ref[...].astype(F32)
+        write_columns(qg_ref, g_ref[...], False, extent)
+        border_windows(wg_ref, wide_ref, qg_ref, False, extent)
+        dh_ref[...] = window_product(qg_ref, w2_ref[...], False, extent)
+        preb_ref[...] = border_of(pre_ref, extent)
+        dhb_ref[...] = border_of(dh_ref, extent)
+        place = iota((count, 1), 0)
+        row, column = place // extent, place % extent
+        inside = (row > 0) & (row < extent - 1) & (column > 0) & (column < extent - 1)
+        value, slope = gelu_parts(pre_ref[...])
+        value = jnp.where(inside, value, 0.0)
+        hid_ref[...] = value.astype(BF16)
+        dpre_ref[...] = jnp.where(inside, dh_ref[...] * slope, 0.0).astype(BF16)
+        write_columns(qd_ref, dpre_ref[...], False, extent)
+        weight_sum(sum_ref.at[0], jnp.transpose(x_ref[...].astype(F32)).astype(BF16), qd_ref, extent)
+        weight_sum(sum_ref.at[1], jnp.transpose(value).astype(BF16), qg_ref, extent)
         lines, pixels = seam_lines(edge_ref, corner_ref, extent)
-        seam_ref[...] = block_choice(lines, pixels, extent)
-        scatter_ref[...] = seam_scatter(lines, pixels, extent)
-        fixed_ref[...] = block_choice(*fixed_lines(extent), extent)
-        column_ref[...] = column_scatter(extent)
-
-    seam, fixed, scatter, column = call(
-        selections,
-        "selections",
-        [choice_b, choice_b, scatter_b, column_b],
-        "ss",
-        (edge_code.T, corner_code.T),
-    )
-
-    def inner(x_ref, g_ref, w1_ref, w2_ref, pre_ref, dh_ref, xt_ref, qg_ref, qx_ref):
-        write_columns(qx_ref, x_ref[...], True, extent)
-        pre_ref[...] = window_product(qx_ref, w1_ref[...], True, extent)
-        write_columns(qg_ref, g_ref[...], False, extent)
-        dh_ref[...] = window_product(qg_ref, w2_ref[...], False, extent)
-        xt_ref[...] = jnp.transpose(x_ref[...].astype(F32)).astype(BF16)
-
-    pre, dh, xt, qg = call(
+        across = border_index(iota((1, border), 1), extent, True)
+        seam_ref[...] = (block_index(lines, pixels, 0, extent) == across).astype(F32).astype(BF16)
+        down = border_index(iota((border, 1), 0), extent, False)
+        back_ref[...] = (down == block_index(lines, pixels, 1, extent)).astype(F32).astype(BF16)
+
+    hid_in, dpre_in, pre_b, dh_b, sums, seam_b, back_b, wx_b, wg_b = call(
         inner,
         "inner_products",
-        [image_f, image_f, turned_b, columns_b],
-        "vvvv",
-        (source, grad_out, w_one, w_two),
-        scratch=[pltpu.VMEM(columns_b.shape, BF16)],
-        flops=2 * conv,
+        [
+            image_b,
+            image_b,
+            border_f,
+            border_f,
+            sds((2,) + taps_f.shape, F32),
+            sds((strip_rows, border), BF16),
+            sds((border, strip_rows), BF16),
+            windows_b,
+            windows_b,
+        ],
+        "ssvvvv",
+        (edge_code.T, corner_code.T, source, grad_out, w_one, w_two),
+        scratch=[pltpu.VMEM(columns_b.shape, BF16)] * 3 + [pltpu.VMEM(image_f.shape, F32)] * 3,
+        flops=4 * conv,
     )
 
-    def middle(seam_ref, fixed_ref, scatter_ref, column_ref, pre_ref, dh_ref, xt_ref, qg_ref, w1_ref, w2_ref, *refs):
+    def middle(preb_ref, dhb_ref, sums_ref, seam_ref, back_ref, wx_ref, wg_ref, w1_ref, w2_ref, *refs):
         arrived = refs[:n_routes]
         keep_ref, send_ref, hid_ref, dpre_ref = refs[n_routes : n_routes + 4]
         outs = refs[n_routes + 4 : n_routes + 4 + n_second]
-        qd_ref, sum_ref = refs[n_routes + 4 + n_second :]
+        (sum_ref,) = refs[n_routes + 4 + n_second :]
         x_strips, g_strips = read(arrived)
         columns = strip_columns(g_strips, extent)
-        value, slope = gelu_parts(pre_ref[...] + margin_forward(x_strips, w1_ref[...], column_ref[...], extent))
-        hidden = value.astype(BF16)
+        adds = margin_adds(x_strips, w1_ref[...], extent)
+        row = iota((extent, 1), 0)
+        first, final = row == 0, row == extent - 1
+
+        def ends(low, high):
+            return jnp.where(first, low, 0.0) + jnp.where(final, high, 0.0)
+
+        def end_rows(part):
+            return adds[part][0:1], adds[part][extent - 1 : extent]
+
+        (east_low, east_high), (west_low, west_high) = end_rows(2), end_rows(3)
+        north = preb_ref[0:extent, :] + adds[0] + ends(west_low, east_low)
+        south = preb_ref[extent : 2 * extent, :] + adds[1] + ends(west_high, east_high)
+
+        def side(part, at):
+            value = preb_ref[part * extent : (part + 1) * extent, :] + adds[part]
+            return jnp.where(first, north[at : at + 1], jnp.where(final, south[at : at + 1], value))
+
+        value, slope = gelu_parts(jnp.concatenate([north, south, side(2, extent - 1), side(3, 0)], axis=0))
+        dadds = [dot_nt(columns[i], tap_columns(w2_ref[...], block_taps(i), channels)) for i in range(4)]
+        high, low = halves(jnp.concatenate(dadds, axis=0))
+        d_hidden = dhb_ref[...] + dot(back_ref[...], high) + dot(back_ref[...], low)
+        d_pre = d_hidden * slope
+        hidden = without_repeats(value, extent).astype(BF16)
         hid_ref[...] = hidden
-        d_hidden = dh_ref[...] + margin_backward(columns, w2_ref[...], scatter_ref[...], extent)
-        d_pre = (d_hidden * slope).astype(BF16)
-        dpre_ref[...] = d_pre
-        a = gather_blocks(seam_ref[...], hidden, extent)
-        b = gather_blocks(fixed_ref[...], d_pre, extent)
+        d_once = without_repeats(d_pre, extent).astype(BF16)
+        dpre_ref[...] = d_once
+        strips = dot(seam_ref[...], hidden).astype(BF16)
+        a = [strips[start : start + rows] for start, rows in zip(block_starts(extent), block_rows(extent))]
+        b = []
+        tall = iota((16, 1), 0)
+        for part in range(4):
+            block = d_pre[part * extent : (part + 1) * extent]
+            if part < 2:
+                tile = jnp.where(tall == 0, block[0:1], jnp.where(tall == 1, block[extent - 1 : extent], 0.0))
+                block = jnp.concatenate([block, tile], axis=0)
+            b.append(block.astype(BF16))
         write_second(a, b, outs)
-        write_columns(qd_ref, d_pre, False, extent)
-        weight_sum(sum_ref.at[0], xt_ref[...], qd_ref, x_strips, strip_columns(b, extent), extent)
-        weight_sum(sum_ref.at[1], jnp.transpose(value).astype(BF16), qg_ref, a, columns, extent)
+        own = dot_t(wx_ref[...], d_once)
+        margin = margin_weight(x_strips, strip_columns(b, extent))
+        for tap in range(9):
+            span = slice(tap * channels, (tap + 1) * channels)
+            total = sums_ref[0, span, :] + own[span]
+            sum_ref[0, span, :] = total if margin[tap] is None else total + margin[tap]
+        own = dot_t(hidden, wg_ref[...])
+        margin = margin_weight(a, columns)
+        for tap in range(9):
+            span = slice(tap * channels, (tap + 1) * channels)
+            total = sums_ref[1, span, :] + own[:, span]
+            sum_ref[1, span, :] = total if margin[tap] is None else total + margin[tap]
         core = lax.axis_index("dp") % 2
         keep_ref[...] = sum_ref[core]
         send_ref[...] = sum_ref[1 - core].astype(BF16)
@@ -622,29 +749,33 @@
     results = call(
         middle,
         "gradients",
-        [taps_f, taps_b, image_b, image_b] + second_routed,
-        "v" * (10 + n_routes),
-        (seam, fixed, scatter, column, pre, dh, xt, qg, w_one, w_two, *first_arrived),
-        scratch=[pltpu.VMEM(columns_b.shape, BF16), pltpu.VMEM((2,) + taps_f.shape, F32)],
-        flops=2 * conv,
+        [taps_f, taps_b, border_b, border_b] + second_routed,
+        "v" * (9 + n_routes),
+        (pre_b, dh_b, sums, seam_b, back_b, wx_b, wg_b, w_one, w_two, *first_arrived),
+        scratch=[pltpu.VMEM((2,) + taps_f.shape, F32)],
+        flops=conv // 4,
     )
-    keep, send, hidden, d_pre = results[:4]
-    def later(edge_ref, corner_ref, x_ref, g_ref, hid_ref, dpre_ref, w1_ref, w2_ref, out_ref, dx_ref, scatter_ref, column_ref, q_ref):
+    keep, send, hid_edge, dpre_edge = results[:4]
+
+    def later(edge_ref, corner_ref, x_ref, g_ref, hid_ref, dpre_ref, hidb_ref, dpreb_ref, w1_ref, w2_ref, out_ref, dx_ref, scatter_ref, column_ref, q_ref):
         lines, pixels = seam_lines(edge_ref, corner_ref, extent)
         scatter_ref[...] = seam_scatter(lines, pixels, extent)
         column_ref[...] = column_scatter(extent)
-        write_columns(q_ref, hid_ref[...], True, extent)
+        choice = border_choice(extent)
+        hidden = hid_ref[...].astype(F32) + dot_t(choice, hidb_ref[...])
+        d_pre = dpre_ref[...].astype(F32) + dot_t(choice, dpreb_ref[...])
+        write_columns(q_ref, hidden, True, extent)
         out_ref[...] = x_ref[...].astype(F32) + window_product(q_ref, w2_ref[...], True, extent)
-        write_columns(q_ref, dpre_ref[...], False, extent)
+        write_columns(q_ref, d_pre, False, extent)
         dx_ref[...] = g_ref[...].astype(F32) + window_product(q_ref, w1_ref[...], False, extent)
 
     def later_parts(token):
-        token, inner_arrays = lax.optimization_barrier((token, (hidden, d_pre)))
+        token, inner_arrays = lax.optimization_barrier((token, (hid_in, dpre_in, hid_edge, dpre_edge)))
         return token, call(
             later,
             "later_products",
             [image_f, image_f, scatter_b, column_b],
-            "ssvvvvvv",
+            "ss" + "v" * 8,
             (edge_code.T, corner_code.T, source, grad_out, *inner_arrays, w_one, w_two),
             scratch=[pltpu.VMEM(columns_b.shape, BF16)],
             flops=2 * conv,

time: 49.5 us -> 49.1 us (level)
  waiting for transfers between devices: 14.7 us -> 13.7 us
    ppermute x16, waiting for transfers between devices: 14.7 us -> 13.7 us  [swap(): return lax.ppermute(value, AXES, [(i, i ^ mask) for i in range(total)])]
    pallas_call x6 -> x5, Pallas kernels: 10.9 us -> 11.2 us  [call(): pl.pallas_call(kernel, name=name, out_shape=outs, in_specs=specs, out_spe...]
  transfers between devices with their start and end apart: 16 -> 16, of which waited for: 8 -> 8; matrix products, arithmetic and copies ran while one was open for 0% -> 0% of each run, Pallas kernels for 12% -> 16%
where the time goes in v4:
time: 49.1 us; the launch traced here: 49 us
  starting transfers between devices  21.7 us (44%)
  waiting for transfers between devices  13.7 us (28%)
  Pallas kernels  11.2 us (23%)
  other arithmetic  1.39 us (3%)
  between operations  0.87 us (2%)
    ppermute x16, starting transfers between devices, swap(): return lax.ppermute(value, AXES, [(i, i ^ mask) for i in range(total)])  21.7 us
    ppermute x16, waiting for transfers between devices, swap(): return lax.ppermute(value, AXES, [(i, i ^ mask) for i in range(total)])  13.7 us
    pallas_call x5, Pallas kernels, call(): pl.pallas_call(kernel, name=name, out_shape=outs, in_specs=specs, out_spe...  11.2 us
    mul x1, other arithmetic, per_device(): two.astype(F32) * factor  1.13 us
  transfers between devices with their start and end apart: 16, of which 8 were waited for; matrix products, arithmetic and copies ran while one was open for 0% of the time, Pallas kernels for 16%

profile of v4, /device:TPU:0, one launch (start us, length us, event | category | flops | bytes accessed | tf_op | source)
XLA Modules:
  0.0 49.0 jit_solution(1760341302415890057)
XLA Ops:
  0.7 2.2 %first_strips.1 = (bf16[64,128]{1,0:T(8,128)(2,1)}, bf16[64,128]{1,0:T(8,128)(2,1)}, bf16[64,128]{1,0:T(8,128)(2,1)}, bf16[128,128]{1,0:T(8,128)(2,1)}, bf16[16,128]{1,0:T(8,128)(2,1)}) custom-call(bf16[1024,128]{1,0:T(8,128)(2,1)} %bitcast.38, bf16[1024,128]{1,0:T(8,128)(2,1)} %bitcast.41, s32[4,8]{1,0:T(4,128)} %bitcast.44, s32[4,8]{1,0:T(4,128)} %bitcast.47), custom_call_target="tpu_custom_call" | custom-call | flops 3019898880 | bytes 610560 | tf_op jit(solution)/shard_map/first_strips/pallas_call | solution.py:454
  2.9 4.1 %collective-permute-start.3 = (bf16[128,128]{1,0:T(8,128)(2,1)}, bf16[128,128]{1,0:T(8,128)(2,1)S(1)}, u32[]{:S(2)}, u32[]{:S(2)}) collective-permute-start(bf16[128,128]{1,0:T(8,128)(2,1)} %get-tuple-element.53), channel_id=1, source_target_pairs={{0,16},{1,17},{2,18},{3,19},{4,20},{5,21},{6,22},{7,23},{8,24},{9,... | collective-permute-start | bytes 98312 | tf_op jit(solution)/shard_map/ppermute | solution.py:477
  7.0 1.5 %collective-permute-start = (bf16[64,128]{1,0:T(8,128)(2,1)}, bf16[64,128]{1,0:T(8,128)(2,1)S(1)}, u32[]{:S(2)}, u32[]{:S(2)}) collective-permute-start(bf16[64,128]{1,0:T(8,128)(2,1)} %get-tuple-element.50), channel_id=1, source_target_pairs={{0,4},{1,5},{2,6},{3,7},{4,0},{5,1},{6,2},{7,3},{8,12},{9,13},{10,... | collective-permute-start | bytes 49160 | tf_op jit(solution)/shard_map/ppermute | solution.py:477
  8.5 1.5 %collective-permute-start.1 = (bf16[64,128]{1,0:T(8,128)(2,1)}, bf16[64,128]{1,0:T(8,128)(2,1)S(1)}, u32[]{:S(2)}, u32[]{:S(2)}) collective-permute-start(bf16[64,128]{1,0:T(8,128)(2,1)} %get-tuple-element.51), channel_id=1, source_target_pairs={{0,12},{1,13},{2,14},{3,15},{4,8},{5,9},{6,10},{7,11},{8,4},{9,5},... | collective-permute-start | bytes 49160 | tf_op jit(solution)/shard_map/ppermute | solution.py:477
  10.0 1.1 %collective-permute-start.2 = (bf16[64,128]{1,0:T(8,128)(2,1)}, bf16[64,128]{1,0:T(8,128)(2,1)S(1)}, u32[]{:S(2)}, u32[]{:S(2)}) collective-permute-start(bf16[64,128]{1,0:T(8,128)(2,1)} %get-tuple-element.52), channel_id=1, source_target_pairs={{0,28},{1,29},{2,30},{3,31},{4,24},{5,25},{6,26},{7,27},{8,20},{9,... | collective-permute-start | bytes 49160 | tf_op jit(solution)/shard_map/ppermute | solution.py:477
  11.2 1.7 %collective-permute-start.4 = (bf16[16,128]{1,0:T(8,128)(2,1)}, bf16[16,128]{1,0:T(8,128)(2,1)S(1)}, u32[]{:S(2)}, u32[]{:S(2)}) collective-permute-start(bf16[16,128]{1,0:T(8,128)(2,1)} %get-tuple-element.54), channel_id=1, source_target_pairs={{0,20},{1,21},{2,22},{3,23},{4,16},{5,17},{6,18},{7,19},{8,28},{9,... | collective-permute-start | bytes 12296 | tf_op jit(solution)/shard_map/ppermute | solution.py:477
  12.9 3.4 %inner_products.1 = (bf16[1024,128]{1,0:T(8,128)(2,1)S(1)}, bf16[1024,128]{1,0:T(8,128)(2,1)S(1)}, f32[128,128]{1,0:T(8,128)S(1)}, f32[128,128]{1,0:T(8,128)S(1)...) custom-call(s32[4,8]{1,0:T(4,128)S(1)} %bitcast.45, ...), custom_call_target="tpu_custom_call" | custom-call | flops 1207959552 | bytes 3621120 | tf_op jit(solution)/shard_map/inner_products/pallas_call | solution.py:454
  16.3 0.5 collective-permute-done.4.refs_4_
  16.8 0.0 collective-permute-done.3.refs_3_
  16.8 1.2 %gradients.1 = (f32[1152,128]{1,0:T(8,128)S(1)}, bf16[1152,128]{1,0:T(8,128)(2,1)S(1)}, bf16[128,128]{1,0:T(8,128)(2,1)S(1)}, bf16[128,128]{1,0:T(8,128)(2,1)S(1...) custom-call(f32[128,128]{1,0:T(8,128)S(1)} %get-tuple-element.43.preb_ref, ...), custom_call_target="tpu_custom_call" | custom-call | flops 75497472 | bytes 3678208 | tf_op jit(solution)/shard_map/gradients/pallas_call | solution.py:454
  18.0 0.1 collective-permute-start.5
  18.2 1.5 %collective-permute-done.5 = bf16[1152,128]{1,0:T(8,128)(2,1)S(1)} collective-permute-done((bf16[1152,128]{1,0:T(8,128)(2,1)S(1)}, bf16[1152,128]{1,0:T(8,128)(2,1)S(1)}, u32[]{:S(2)}, u32[]{:S(2)}) %collective-permute-start.5) | collective-permute-done | bytes 294944 | tf_op jit(solution)/shard_map/ppermute | solution.py:477
  19.7 0.1 fusion.4
  19.8 1.4 %collective-permute-start.8 = (bf16[432,128]{1,0:T(8,128)(2,1)S(1)}, bf16[432,128]{1,0:T(8,128)(2,1)S(1)}, u32[]{:S(2)}, u32[]{:S(2)}) collective-permute-start(bf16[432,128]{1,0:T(8,128)(2,1)S(1)} %pad_maximum_fusion.2), channel_id=1, source_target_pairs={{0,4},{1,5},{2,6},{3,7},{4,0},{5,1},{6,2},{7,3},{8,12},{9,13},{10,... | collective-permute-start | bytes 331784 | tf_op jit(solution)/shard_map/ppermute | solution.py:477
  21.2 1.6 %collective-permute-start.6 = (bf16[288,128]{1,0:T(8,128)(2,1)S(1)}, bf16[288,128]{1,0:T(8,128)(2,1)S(1)}, u32[]{:S(2)}, u32[]{:S(2)}) collective-permute-start(bf16[288,128]{1,0:T(8,128)(2,1)S(1)} %get-tuple-element.84), channel_id=1, source_target_pairs={{0,6},{1,7},{2,4},{3,5},{4,2},{5,3},{6,0},{7,1},{8,14},{9,15},{10,... | collective-permute-start | bytes 221192 | tf_op jit(solution)/shard_map/ppermute | solution.py:477
  22.8 0.5 %collective-permute-start.7 = (bf16[288,128]{1,0:T(8,128)(2,1)S(1)}, bf16[288,128]{1,0:T(8,128)(2,1)S(1)}, u32[]{:S(2)}, u32[]{:S(2)}) collective-permute-start(bf16[288,128]{1,0:T(8,128)(2,1)S(1)} %get-tuple-element.83), channel_id=1, source_target_pairs={{0,2},{1,3},{2,0},{3,1},{4,6},{5,7},{6,4},{7,5},{8,10},{9,11},{10,... | collective-permute-start | bytes 221192 | tf_op jit(solution)/shard_map/ppermute | solution.py:477
  23.3 4.3 %collective-permute-done.6 = bf16[288,128]{1,0:T(8,128)(2,1)S(1)} collective-permute-done((bf16[288,128]{1,0:T(8,128)(2,1)S(1)}, bf16[288,128]{1,0:T(8,128)(2,1)S(1)}, u32[]{:S(2)}, u32[]{:S(2)}) %collective-permute-start.6) | collective-permute-done | bytes 73760 | tf_op jit(solution)/shard_map/ppermute | solution.py:477
  27.6 0.6 %collective-permute-done.7 = bf16[288,128]{1,0:T(8,128)(2,1)S(1)} collective-permute-done((bf16[288,128]{1,0:T(8,128)(2,1)S(1)}, bf16[288,128]{1,0:T(8,128)(2,1)S(1)}, u32[]{:S(2)}, u32[]{:S(2)}) %collective-permute-start.7) | collective-permute-done | bytes 73760 | tf_op jit(solution)/shard_map/ppermute | solution.py:477
  28.2 0.1 fusion.1
  28.2 1.8 %collective-permute-start.10 = (bf16[432,128]{1,0:T(8,128)(2,1)S(1)}, bf16[432,128]{1,0:T(8,128)(2,1)S(1)}, u32[]{:S(2)}, u32[]{:S(2)}) collective-permute-start(bf16[432,128]{1,0:T(8,128)(2,1)S(1)} %pad_maximum_fusion.3), channel_id=1, source_target_pairs={{0,16},{1,17},{2,18},{3,19},{4,20},{5,21},{6,22},{7,23},{8,24},{9,... | collective-permute-start | bytes 331784 | tf_op jit(solution)/shard_map/ppermute | solution.py:477
  30.0 2.8 %collective-permute-start.11 = (bf16[352,128]{1,0:T(8,128)(2,1)S(1)}, bf16[352,128]{1,0:T(8,128)(2,1)S(1)}, u32[]{:S(2)}, u32[]{:S(2)}) collective-permute-start(bf16[352,128]{1,0:T(8,128)(2,1)S(1)} %get-tuple-element.92), channel_id=1, source_target_pairs={{0,24},{1,25},{2,26},{3,27},{4,28},{5,29},{6,30},{7,31},{8,16},{9,... | collective-permute-start | bytes 270344 | tf_op jit(solution)/shard_map/ppermute | solution.py:477
  32.8 2.7 %later_products.1 = (f32[1024,128]{1,0:T(8,128)S(1)}, f32[1024,128]{1,0:T(8,128)S(1)}, bf16[1024,160]{1,0:T(8,128)(2,1)S(1)}, bf16[1024,128]{1,0:T(8,128)(2,1)S(1)}) custom-call(s32[4,8]{1,0:T(4,128)S(1)} %bitcast.46, s32[4,8]{1,0:T(4,128)S(1)} %bitcast.49, bf16[1024,128]{1,0:T(8,128)(2,1)S(1)} %bitcast.40, bf16[1024,128]{1,0:T(8,128)(2,1)S(1)} %bitcast.43, ...), custom_call_target="tpu_custom_call" | custom-call | flops 603979776 | bytes 3342592 | tf_op jit(solution)/shard_map/later_products/pallas_call | solution.py:454
  35.5 1.5 %collective-permute-done.11 = bf16[352,128]{1,0:T(8,128)(2,1)S(1)} collective-permute-done((bf16[352,128]{1,0:T(8,128)(2,1)S(1)}, bf16[352,128]{1,0:T(8,128)(2,1)S(1)}, u32[]{:S(2)}, u32[]{:S(2)}) %collective-permute-start.11) | collective-permute-done | bytes 90144 | tf_op jit(solution)/shard_map/ppermute | solution.py:477
  37.0 1.6 %collective-permute-done.9 = bf16[352,128]{1,0:T(8,128)(2,1)S(1)} collective-permute-done((bf16[352,128]{1,0:T(8,128)(2,1)S(1)}, bf16[352,128]{1,0:T(8,128)(2,1)S(1)}, u32[]{:S(2)}, u32[]{:S(2)}) %collective-permute-start.9) | collective-permute-done | bytes 90144 | tf_op jit(solution)/shard_map/ppermute | solution.py:477
  38.6 0.6 %collective-permute-start.12 = (bf16[288,128]{1,0:T(8,128)(2,1)S(1)}, bf16[288,128]{1,0:T(8,128)(2,1)S(1)}, u32[]{:S(2)}, u32[]{:S(2)}) collective-permute-start(bf16[288,128]{1,0:T(8,128)(2,1)S(1)} %add_add_fusion), channel_id=1, source_target_pairs={{0,2},{1,3},{2,0},{3,1},{4,6},{5,7},{6,4},{7,5},{8,10},{9,11},{10,... | collective-permute-start | bytes 221192 | tf_op jit(solution)/shard_map/ppermute | solution.py:477
  39.3 1.5 %collective-permute-start.13 = (bf16[288,128]{1,0:T(8,128)(2,1)S(1)}, bf16[288,128]{1,0:T(8,128)(2,1)S(1)}, u32[]{:S(2)}, u32[]{:S(2)}) collective-permute-start(bf16[288,128]{1,0:T(8,128)(2,1)S(1)} %add_add_fusion), channel_id=1, source_target_pairs={{0,4},{1,5},{2,6},{3,7},{4,0},{5,1},{6,2},{7,3},{8,12},{9,13},{10,... | collective-permute-start | bytes 221192 | tf_op jit(solution)/shard_map/ppermute | solution.py:477
  40.8 1.4 %collective-permute-start.14 = (bf16[288,128]{1,0:T(8,128)(2,1)S(1)}, bf16[288,128]{1,0:T(8,128)(2,1)S(1)}, u32[]{:S(2)}, u32[]{:S(2)}) collective-permute-start(bf16[288,128]{1,0:T(8,128)(2,1)S(1)} %add_add_fusion), channel_id=1, source_target_pairs={{0,6},{1,7},{2,4},{3,5},{4,2},{5,3},{6,0},{7,1},{8,14},{9,15},{10,... | collective-permute-start | bytes 221192 | tf_op jit(solution)/shard_map/ppermute | solution.py:477
  42.2 1.6 %outputs.1 = (bf16[1024,128]{1,0:T(8,128)(2,1)}, bf16[1024,128]{1,0:T(8,128)(2,1)}) custom-call(f32[1024,128]{1,0:T(8,128)S(1)} %get-tuple-element.73.part_ref, f32[1024,128]{1,0:T(8,128)S(1)} %get-tuple-element.74.dpart_ref, bf16[1024,160]{1,0:T(8,128)(2,1)S(1)} %get-tuple-element.75.scatter_ref, bf16[1024,128]{1,0:T(8,128)(2,1)S(1)} %get-tuple-element.76.column_ref, ...), custom_call_target="tpu_custom_call" | custom-call | flops 75497472 | bytes 2838528 | tf_op jit(solution)/shard_map/outputs/pallas_call | solution.py:454
  43.9 2.2 %collective-permute-done.14 = bf16[288,128]{1,0:T(8,128)(2,1)S(1)} collective-permute-done((bf16[288,128]{1,0:T(8,128)(2,1)S(1)}, bf16[288,128]{1,0:T(8,128)(2,1)S(1)}, u32[]{:S(2)}, u32[]{:S(2)}) %collective-permute-start.14) | collective-permute-done | bytes 73760 | tf_op jit(solution)/shard_map/ppermute | solution.py:477
  46.2 0.1 collective-permute-start.15
  46.3 1.6 %collective-permute-done.15 = bf16[4,288,128]{2,1,0:T(8,128)(2,1)S(1)} collective-permute-done((bf16[4,288,128]{2,1,0:T(8,128)(2,1)S(1)}, bf16[4,288,128]{2,1,0:T(8,128)(2,1)S(1)}, u32[]{:S(2)}, u32[]{:S(2)}) %collective-permute-start.15) | collective-permute-done | bytes 294944 | tf_op jit(solution)/shard_map/ppermute | solution.py:477
  47.8 1.1 %convert_multiply_fusion = (f32[4,288,128]{2,1,0:T(8,128)}, f32[4,288,128]{2,1,0:T(8,128)}) fusion(bf16[4,288,128]{2,1,0:T(8,128)(2,1)S(1)} %collective-permute-done.15, bf16[4,288,128]{2,1,0:T(8,128)(2,1)S(1)} %pad_maximum_fusion.1, pred[]{:T(512)S(6)} %eq.16), kind=kLoop, calls=%fused_computation | loop fusion | flops 884736 | bytes 1769473 | tf_op jit(solution)/shard_map/mul | solution.py:813
  (34 shorter events, 0.3 us)
Async XLA Ops:
  0.6 12.2 %copy-start = (bf16[9,128,128]{2,1,0:T(8,128)(2,1)S(1)}, bf16[9,128,128]{2,1,0:T(8,128)(2,1)}, u32[]{:S(2)}) copy-start(bf16[9,128,128]{2,1,0:T(8,128)(2,1)} %param.7) | copy-start | bytes 884740
  0.6 12.2 %copy-start.1 = (bf16[9,128,128]{2,1,0:T(8,128)(2,1)S(1)}, bf16[9,128,128]{2,1,0:T(8,128)(2,1)}, u32[]{:S(2)}) copy-start(bf16[9,128,128]{2,1,0:T(8,128)(2,1)} %param.8) | copy-start | bytes 884740
  0.7 12.2 %copy-start.2 = (bf16[1,1,32,32,128]{4,3,2,1,0:T(8,128)(2,1)S(1)}, bf16[1,1,32,32,128]{4,3,2,1,0:T(8,128)(2,1)}, u32[]{:S(2)}) copy-start(bf16[1,1,32,32,128]{4,3,2,1,0:T(8,128)(2,1)} %param.6) | copy-start | bytes 786436
  0.7 12.2 %copy-start.3 = (bf16[1,1,32,32,128]{4,3,2,1,0:T(8,128)(2,1)S(1)}, bf16[1,1,32,32,128]{4,3,2,1,0:T(8,128)(2,1)}, u32[]{:S(2)}) copy-start(bf16[1,1,32,32,128]{4,3,2,1,0:T(8,128)(2,1)} %param.9) | copy-start | bytes 786436
  0.7 12.2 %copy-start.4 = (s32[8,4]{0,1:T(4,128)S(1)}, s32[8,4]{0,1:T(4,128)}, u32[]{:S(2)}) copy-start(s32[8,4]{0,1:T(4,128)} %param.10) | copy-start | bytes 388
  0.7 12.2 %copy-start.5 = (s32[8,4]{0,1:T(4,128)S(1)}, s32[8,4]{0,1:T(4,128)}, u32[]{:S(2)}) copy-start(s32[8,4]{0,1:T(4,128)} %param.11) | copy-start | bytes 388
  2.9 13.9 %collective-permute-start.3 = (bf16[128,128]{1,0:T(8,128)(2,1)}, bf16[128,128]{1,0:T(8,128)(2,1)S(1)}, u32[]{:S(2)}, u32[]{:S(2)}) collective-permute-start(bf16[128,128]{1,0:T(8,128)(2,1)} %get-tuple-element.53), channel_id=1, source_target_pairs={{0,16},{1,17},{2,18},{3,19},{4,20},{5,21},{6,22},{7,23},{8,24},{9,... | collective-permute-start | bytes 98312 | tf_op jit(solution)/shard_map/ppermute | solution.py:477
  7.0 9.8 %collective-permute-start = (bf16[64,128]{1,0:T(8,128)(2,1)}, bf16[64,128]{1,0:T(8,128)(2,1)S(1)}, u32[]{:S(2)}, u32[]{:S(2)}) collective-permute-start(bf16[64,128]{1,0:T(8,128)(2,1)} %get-tuple-element.50), channel_id=1, source_target_pairs={{0,4},{1,5},{2,6},{3,7},{4,0},{5,1},{6,2},{7,3},{8,12},{9,13},{10,... | collective-permute-start | bytes 49160 | tf_op jit(solution)/shard_map/ppermute | solution.py:477
  8.5 8.3 %collective-permute-start.1 = (bf16[64,128]{1,0:T(8,128)(2,1)}, bf16[64,128]{1,0:T(8,128)(2,1)S(1)}, u32[]{:S(2)}, u32[]{:S(2)}) collective-permute-start(bf16[64,128]{1,0:T(8,128)(2,1)} %get-tuple-element.51), channel_id=1, source_target_pairs={{0,12},{1,13},{2,14},{3,15},{4,8},{5,9},{6,10},{7,11},{8,4},{9,5},... | collective-permute-start | bytes 49160 | tf_op jit(solution)/shard_map/ppermute | solution.py:477
  10.0 6.8 %collective-permute-start.2 = (bf16[64,128]{1,0:T(8,128)(2,1)}, bf16[64,128]{1,0:T(8,128)(2,1)S(1)}, u32[]{:S(2)}, u32[]{:S(2)}) collective-permute-start(bf16[64,128]{1,0:T(8,128)(2,1)} %get-tuple-element.52), channel_id=1, source_target_pairs={{0,28},{1,29},{2,30},{3,31},{4,24},{5,25},{6,26},{7,27},{8,20},{9,... | collective-permute-start | bytes 49160 | tf_op jit(solution)/shard_map/ppermute | solution.py:477
  11.2 5.6 %collective-permute-start.4 = (bf16[16,128]{1,0:T(8,128)(2,1)}, bf16[16,128]{1,0:T(8,128)(2,1)S(1)}, u32[]{:S(2)}, u32[]{:S(2)}) collective-permute-start(bf16[16,128]{1,0:T(8,128)(2,1)} %get-tuple-element.54), channel_id=1, source_target_pairs={{0,20},{1,21},{2,22},{3,23},{4,16},{5,17},{6,18},{7,19},{8,28},{9,... | collective-permute-start | bytes 12296 | tf_op jit(solution)/shard_map/ppermute | solution.py:477
  18.0 1.6 %collective-permute-start.5 = (bf16[1152,128]{1,0:T(8,128)(2,1)S(1)}, bf16[1152,128]{1,0:T(8,128)(2,1)S(1)}, u32[]{:S(2)}, u32[]{:S(2)}) collective-permute-start(bf16[1152,128]{1,0:T(8,128)(2,1)S(1)} %get-tuple-element.56), channel_id=1, source_target_pairs={{0,1},{1,0},{2,3},{3,2},{4,5},{5,4},{6,7},{7,6},{8,9},{9,8},{10,11... | collective-permute-start | bytes 884744 | tf_op jit(solution)/shard_map/ppermute | solution.py:477
  19.8 8.4 %collective-permute-start.8 = (bf16[432,128]{1,0:T(8,128)(2,1)S(1)}, bf16[432,128]{1,0:T(8,128)(2,1)S(1)}, u32[]{:S(2)}, u32[]{:S(2)}) collective-permute-start(bf16[432,128]{1,0:T(8,128)(2,1)S(1)} %pad_maximum_fusion.2), channel_id=1, source_target_pairs={{0,4},{1,5},{2,6},{3,7},{4,0},{5,1},{6,2},{7,3},{8,12},{9,13},{10,... | collective-permute-start | bytes 331784 | tf_op jit(solution)/shard_map/ppermute | solution.py:477
  21.2 6.4 %collective-permute-start.6 = (bf16[288,128]{1,0:T(8,128)(2,1)S(1)}, bf16[288,128]{1,0:T(8,128)(2,1)S(1)}, u32[]{:S(2)}, u32[]{:S(2)}) collective-permute-start(bf16[288,128]{1,0:T(8,128)(2,1)S(1)} %get-tuple-element.84), channel_id=1, source_target_pairs={{0,6},{1,7},{2,4},{3,5},{4,2},{5,3},{6,0},{7,1},{8,14},{9,15},{10,... | collective-permute-start | bytes 221192 | tf_op jit(solution)/shard_map/ppermute | solution.py:477
  22.8 5.3 %collective-permute-start.7 = (bf16[288,128]{1,0:T(8,128)(2,1)S(1)}, bf16[288,128]{1,0:T(8,128)(2,1)S(1)}, u32[]{:S(2)}, u32[]{:S(2)}) collective-permute-start(bf16[288,128]{1,0:T(8,128)(2,1)S(1)} %get-tuple-element.83), channel_id=1, source_target_pairs={{0,2},{1,3},{2,0},{3,1},{4,6},{5,7},{6,4},{7,5},{8,10},{9,11},{10,... | collective-permute-start | bytes 221192 | tf_op jit(solution)/shard_map/ppermute | solution.py:477
  28.2 10.4 %collective-permute-start.10 = (bf16[432,128]{1,0:T(8,128)(2,1)S(1)}, bf16[432,128]{1,0:T(8,128)(2,1)S(1)}, u32[]{:S(2)}, u32[]{:S(2)}) collective-permute-start(bf16[432,128]{1,0:T(8,128)(2,1)S(1)} %pad_maximum_fusion.3), channel_id=1, source_target_pairs={{0,16},{1,17},{2,18},{3,19},{4,20},{5,21},{6,22},{7,23},{8,24},{9,... | collective-permute-start | bytes 331784 | tf_op jit(solution)/shard_map/ppermute | solution.py:477
  30.0 7.0 %collective-permute-start.11 = (bf16[352,128]{1,0:T(8,128)(2,1)S(1)}, bf16[352,128]{1,0:T(8,128)(2,1)S(1)}, u32[]{:S(2)}, u32[]{:S(2)}) collective-permute-start(bf16[352,128]{1,0:T(8,128)(2,1)S(1)} %get-tuple-element.92), channel_id=1, source_target_pairs={{0,24},{1,25},{2,26},{3,27},{4,28},{5,29},{6,30},{7,31},{8,16},{9,... | collective-permute-start | bytes 270344 | tf_op jit(solution)/shard_map/ppermute | solution.py:477
  32.8 5.8 %collective-permute-start.9 = (bf16[352,128]{1,0:T(8,128)(2,1)S(1)}, bf16[352,128]{1,0:T(8,128)(2,1)S(1)}, u32[]{:S(2)}, u32[]{:S(2)}) collective-permute-start(bf16[352,128]{1,0:T(8,128)(2,1)S(1)} %get-tuple-element.91), channel_id=1, source_target_pairs={{0,8},{1,9},{2,10},{3,11},{4,12},{5,13},{6,14},{7,15},{8,0},{9,1},... | collective-permute-start | bytes 270344 | tf_op jit(solution)/shard_map/ppermute | solution.py:477
  38.6 5.2 %collective-permute-start.12 = (bf16[288,128]{1,0:T(8,128)(2,1)S(1)}, bf16[288,128]{1,0:T(8,128)(2,1)S(1)}, u32[]{:S(2)}, u32[]{:S(2)}) collective-permute-start(bf16[288,128]{1,0:T(8,128)(2,1)S(1)} %add_add_fusion), channel_id=1, source_target_pairs={{0,2},{1,3},{2,0},{3,1},{4,6},{5,7},{6,4},{7,5},{8,10},{9,11},{10,... | collective-permute-start | bytes 221192 | tf_op jit(solution)/shard_map/ppermute | solution.py:477
  39.3 4.6 %collective-permute-start.13 = (bf16[288,128]{1,0:T(8,128)(2,1)S(1)}, bf16[288,128]{1,0:T(8,128)(2,1)S(1)}, u32[]{:S(2)}, u32[]{:S(2)}) collective-permute-start(bf16[288,128]{1,0:T(8,128)(2,1)S(1)} %add_add_fusion), channel_id=1, source_target_pairs={{0,4},{1,5},{2,6},{3,7},{4,0},{5,1},{6,2},{7,3},{8,12},{9,13},{10,... | collective-permute-start | bytes 221192 | tf_op jit(solution)/shard_map/ppermute | solution.py:477
  40.8 5.3 %collective-permute-start.14 = (bf16[288,128]{1,0:T(8,128)(2,1)S(1)}, bf16[288,128]{1,0:T(8,128)(2,1)S(1)}, u32[]{:S(2)}, u32[]{:S(2)}) collective-permute-start(bf16[288,128]{1,0:T(8,128)(2,1)S(1)} %add_add_fusion), channel_id=1, source_target_pairs={{0,6},{1,7},{2,4},{3,5},{4,2},{5,3},{6,0},{7,1},{8,14},{9,15},{10,... | collective-permute-start | bytes 221192 | tf_op jit(solution)/shard_map/ppermute | solution.py:477
  46.2 1.6 %collective-permute-start.15 = (bf16[4,288,128]{2,1,0:T(8,128)(2,1)S(1)}, bf16[4,288,128]{2,1,0:T(8,128)(2,1)S(1)}, u32[]{:S(2)}, u32[]{:S(2)}) collective-permute-start(bf16[4,288,128]{2,1,0:T(8,128)(2,1)S(1)} %pad_maximum_fusion.1), channel_id=1, source_target_pairs={{0,1},{1,0},{2,3},{3,2},{4,5},{5,4},{6,7},{7,6},{8,9},{9,8},{10,11... | collective-permute-start | bytes 884744 | tf_op jit(solution)/shard_map/ppermute | solution.py:477

commit v5 on v4

--- a/solution.py
+++ b/solution.py
@@ -284,16 +284,25 @@
         q_ref[extent : extent + count, b * channels : (b + 1) * channels] = shifted(wide, by, extent).astype(BF16)
 
 
-def window_product(q_ref, weight, forward, extent, chunk=256):
-    count = q_ref.shape[0] - 2 * extent
+def window_product(q_ref, weight, forward, extent, out_ref, chunk=8):
     channels = weight.shape[1]
-    if not forward:
-        weight = tap_columns(weight, range(9), channels)
-    pieces = []
-    for start in range(0, count, chunk):
-        rows = [q_ref[(a if forward else 2 - a) * extent + start : (a if forward else 2 - a) * extent + start + chunk, :] for a in range(3)]
-        pieces.append((dot if forward else dot_nt)(jnp.concatenate(rows, axis=1), weight))
-    return jnp.concatenate(pieces, axis=0)
+    if forward:
+        taps = tap_weight(weight, range(9), channels)
+        nothing = jnp.zeros((3 * channels, channels), weight.dtype)
+        both = jnp.concatenate([jnp.concatenate([taps, nothing], axis=0), jnp.concatenate([nothing, taps], axis=0)], axis=1)
+    else:
+        taps = tap_columns(weight, (6, 7, 8, 3, 4, 5, 0, 1, 2), channels)
+        nothing = jnp.zeros((channels, 3 * channels), weight.dtype)
+        both = jnp.concatenate([jnp.concatenate([taps, nothing], axis=1), jnp.concatenate([nothing, taps], axis=1)], axis=0)
+    for start in range(0, extent // 2, chunk):
+        rows = []
+        for a in range(4):
+            rows.append(jnp.concatenate([q_ref[(2 * i + a) * extent : (2 * i + a + 1) * extent, :] for i in range(start, start + chunk)], axis=0))
+        product = (dot if forward else dot_nt)(jnp.concatenate(rows, axis=1), both)
+        for i in range(chunk):
+            for half in range(2):
+                at = (2 * (start + i) + half) * extent
+                out_ref[at : at + extent, :] = product[i * extent : (i + 1) * extent, half * channels : (half + 1) * channels]
 
 
 def tap_weight(weight, taps, channels):
@@ -364,11 +373,10 @@
 def weight_sum(out_ref, image_t, q_ref, extent):
     channels = image_t.shape[0]
     count = image_t.shape[1]
-    for a in range(3):
-        product = dot(image_t, q_ref[(2 - a) * extent : (2 - a) * extent + count, :])
-        for b in range(3):
-            tap = 3 * a + b
-            out_ref[tap * channels : (tap + 1) * channels, :] = product[:, b * channels : (b + 1) * channels]
+    rows = jnp.concatenate([q_ref[(2 - a) * extent : (2 - a) * extent + count, :] for a in range(3)], axis=1)
+    product = dot(image_t, rows)
+    for tap in range(9):
+        out_ref[tap * channels : (tap + 1) * channels, :] = product[:, tap * channels : (tap + 1) * channels]
 
 
 def margin_weight(strips, columns):
@@ -442,9 +450,10 @@
 def gelu_parts(u):
     scale = math.sqrt(2.0 / math.pi)
     square = u * u
-    t = jnp.tanh(scale * (u + 0.044715 * (square * u)))
-    value = 0.5 * u * (1.0 + t)
-    slope = 0.5 * (1.0 + t) + (0.5 * u) * (1.0 - t * t) * (scale * (1.0 + 3.0 * 0.044715 * square))
+    half = 0.5 * u
+    t = jnp.tanh(u * (scale + (scale * 0.044715) * square))
+    value = half + half * t
+    slope = (0.5 + 0.5 * t) + (half * (1.0 - t * t)) * (scale + (scale * 3.0 * 0.044715) * square)
     return value, slope
 
 
@@ -537,8 +546,10 @@
     return jnp.where(low, whole, other), jnp.where(low, other, whole)
 
 
-def reach_neighbours(across, one, three, far, corners, total):
-    return [swap(across, 4, total), swap(one, 12, total), swap(three, 28, total), swap(far, 16, total), swap(corners, 20, total)]
+def reach_neighbours(across, one, three, far, total):
+    across, three, one = swap(across, 4, total), swap(three, 28, total), swap(one, 12, total)
+    two = swap(jnp.concatenate([far, across[-16:]], axis=0), 16, total)
+    return [across, one, three, two[:-16], two[-16:]]
 
 
 def per_device(inputs, weight_one, weight_two, cotangent, edge_code, corner_code):
@@ -556,7 +567,7 @@
     near_b, far_b, corner_b = sds((4 * extent + 16, channels), BF16), sds((4 * extent, channels), BF16), sds((16, channels), BF16)
     pair_b = sds((2 * extent, channels), BF16)
     if hops:
-        first_routed, second_routed = [pair_b, pair_b, pair_b, far_b, corner_b], [near_b, far_b]
+        first_routed, second_routed = [sds((2 * extent + 16, channels), BF16), pair_b, pair_b, far_b], [near_b, far_b]
         n_routes = 5
     else:
         first_routed = second_routed = [sds((route_rows(r, extent), channels), BF16) for r in plan]
@@ -568,8 +579,8 @@
             write_near(a, b, near_ref, extent)
             write_far(a, b, outs[3], extent)
             for start, out in zip(near_starts(lax.axis_index("tile"), extent), outs):
-                out[...] = near_ref[pl.ds(pl.multiple_of(start, 16), 2 * extent), :]
-            outs[4][...] = near_ref[4 * extent : 4 * extent + 16, :]
+                out[0 : 2 * extent, :] = near_ref[pl.ds(pl.multiple_of(start, 16), 2 * extent), :]
+            outs[0][2 * extent : 2 * extent + 16, :] = near_ref[4 * extent : 4 * extent + 16, :]
         else:
             write_routes(a, b, plan, outs, extent)
 
@@ -642,11 +653,11 @@
         wide_ref[...] = x_ref[...].astype(F32)
         write_columns(qx_ref, x_ref[...], True, extent)
         border_windows(wx_ref, wide_ref, qx_ref, True, extent)
-        pre_ref[...] = window_product(qx_ref, w1_ref[...], True, extent)
+        window_product(qx_ref, w1_ref[...], True, extent, pre_ref)
         wide_ref[...] = g_ref[...].astype(F32)
         write_columns(qg_ref, g_ref[...], False, extent)
         border_windows(wg_ref, wide_ref, qg_ref, False, extent)
-        dh_ref[...] = window_product(qg_ref, w2_ref[...], False, extent)
+        window_product(qg_ref, w2_ref[...], False, extent, dh_ref)
         preb_ref[...] = border_of(pre_ref, extent)
         dhb_ref[...] = border_of(dh_ref, extent)
         place = iota((count, 1), 0)
@@ -765,9 +776,11 @@
         hidden = hid_ref[...].astype(F32) + dot_t(choice, hidb_ref[...])
         d_pre = dpre_ref[...].astype(F32) + dot_t(choice, dpreb_ref[...])
         write_columns(q_ref, hidden, True, extent)
-        out_ref[...] = x_ref[...].astype(F32) + window_product(q_ref, w2_ref[...], True, extent)
+        window_product(q_ref, w2_ref[...], True, extent, out_ref)
+        out_ref[...] = out_ref[...] + x_ref[...].astype(F32)
         write_columns(q_ref, d_pre, False, extent)
-        dx_ref[...] = g_ref[...].astype(F32) + window_product(q_ref, w1_ref[...], False, extent)
+        window_product(q_ref, w1_ref[...], False, extent, dx_ref)
+        dx_ref[...] = dx_ref[...] + g_ref[...].astype(F32)
 
     def later_parts(token):
         token, inner_arrays = lax.optimization_barrier((token, (hid_in, dpre_in, hid_edge, dpre_edge)))

time: 49.1 us -> 47.5 us (0.967)
  starting transfers between devices: 21.7 us -> 19 us
  waiting for transfers between devices: 13.7 us -> 14.8 us
  Pallas kernels: 11.2 us -> 10.4 us
  other arithmetic: 1.39 us -> 2.16 us
    ppermute x16 -> x15, starting transfers between devices: 21.7 us -> 19 us  [swap(): return lax.ppermute(value, AXES, [(i, i ^ mask) for i in range(total)])]
    ppermute x16 -> x15, waiting for transfers between devices: 13.7 us -> 14.8 us  [swap(): return lax.ppermute(value, AXES, [(i, i ^ mask) for i in range(total)])]
    pallas_call x5, Pallas kernels: 11.2 us -> 10.4 us  [call(): pl.pallas_call(kernel, name=name, out_shape=outs, in_specs=specs, out_spe...]
    concatenate x0 -> x1, other arithmetic: none -> 0.76 us  [reach_neighbours(): two = swap(jnp.concatenate([far, across[-16:]], axis=0), 16, total)]
  transfers between devices with their start and end apart: 16 -> 15, of which waited for: 8 -> 8; matrix products, arithmetic and copies ran while one was open for 0% -> 2% of each run, Pallas kernels for 16% -> 15%
where the time goes in v5:
time: 47.5 us; the launch traced here: 47.3 us
  starting transfers between devices  19 us (40%)
  waiting for transfers between devices  14.8 us (31%)
  Pallas kernels  10.4 us (22%)
  other arithmetic  2.16 us (5%)
  between operations  0.87 us (2%)
    ppermute x15, starting transfers between devices, swap(): return lax.ppermute(value, AXES, [(i, i ^ mask) for i in range(total)])  19 us
    ppermute x15, waiting for transfers between devices, swap(): return lax.ppermute(value, AXES, [(i, i ^ mask) for i in range(total)])  14.8 us
    pallas_call x5, Pallas kernels, call(): pl.pallas_call(kernel, name=name, out_shape=outs, in_specs=specs, out_spe...  10.4 us
    mul x1, other arithmetic, per_device(): two.astype(F32) * factor  1.13 us
  transfers between devices with their start and end apart: 15, of which 8 were waited for; matrix products, arithmetic and copies ran while one was open for 2% of the time, Pallas kernels for 15%

profile of v5, /device:TPU:0, one launch (start us, length us, event | category | flops | bytes accessed | tf_op | source)
XLA Modules:
  0.0 47.3 jit_solution(16513751496668118415)
XLA Ops:
  0.7 2.2 %first_strips.1 = (bf16[80,128]{1,0:T(8,128)(2,1)}, bf16[64,128]{1,0:T(8,128)(2,1)}, bf16[64,128]{1,0:T(8,128)(2,1)}, bf16[128,128]{1,0:T(8,128)(2,1)}) custom-call(bf16[1024,128]{1,0:T(8,128)(2,1)} %bitcast.38, bf16[1024,128]{1,0:T(8,128)(2,1)} %bitcast.41, s32[4,8]{1,0:T(4,128)} %bitcast.44, s32[4,8]{1,0:T(4,128)} %bitcast.47), custom_call_target="tpu_custom_call" | custom-call | flops 3019898880 | bytes 610560 | tf_op jit(solution)/shard_map/first_strips/pallas_call | solution.py:463
  2.9 3.0 %collective-permute-start = (bf16[80,128]{1,0:T(8,128)(2,1)}, bf16[80,128]{1,0:T(8,128)(2,1)S(1)}, u32[]{:S(2)}, u32[]{:S(2)}) collective-permute-start(bf16[80,128]{1,0:T(8,128)(2,1)} %get-tuple-element.49), channel_id=1, source_target_pairs={{0,4},{1,5},{2,6},{3,7},{4,0},{5,1},{6,2},{7,3},{8,12},{9,13},{10,... | collective-permute-start | bytes 61448 | tf_op jit(solution)/shard_map/ppermute | solution.py:486
  5.9 1.5 %collective-permute-start.1 = (bf16[64,128]{1,0:T(8,128)(2,1)}, bf16[64,128]{1,0:T(8,128)(2,1)S(1)}, u32[]{:S(2)}, u32[]{:S(2)}) collective-permute-start(bf16[64,128]{1,0:T(8,128)(2,1)} %get-tuple-element.50), channel_id=1, source_target_pairs={{0,12},{1,13},{2,14},{3,15},{4,8},{5,9},{6,10},{7,11},{8,4},{9,5},... | collective-permute-start | bytes 49160 | tf_op jit(solution)/shard_map/ppermute | solution.py:486
  7.4 3.4 %collective-permute-start.2 = (bf16[64,128]{1,0:T(8,128)(2,1)}, bf16[64,128]{1,0:T(8,128)(2,1)S(1)}, u32[]{:S(2)}, u32[]{:S(2)}) collective-permute-start(bf16[64,128]{1,0:T(8,128)(2,1)} %get-tuple-element.51), channel_id=1, source_target_pairs={{0,28},{1,29},{2,30},{3,31},{4,24},{5,25},{6,26},{7,27},{8,20},{9,... | collective-permute-start | bytes 49160 | tf_op jit(solution)/shard_map/ppermute | solution.py:486
  10.8 0.8 %pad_maximum_fusion.6 = bf16[144,128]{1,0:T(8,128)(2,1)S(1)} fusion(bf16[16,128]{1,0:T(8,128)(2,1)S(1)} %slice.53, bf16[128,128]{1,0:T(8,128)(2,1)} %get-tuple-element.52), kind=kLoop, calls=%fused_computation.18 | loop fusion | flops 73728 | bytes 73728 | tf_op jit(solution)/shard_map/concatenate | solution.py:551
  11.6 0.1 collective-permute-start.3
  11.8 3.2 %inner_products.1 = (bf16[1024,128]{1,0:T(8,128)(2,1)S(1)}, bf16[1024,128]{1,0:T(8,128)(2,1)S(1)}, f32[128,128]{1,0:T(8,128)S(1)}, f32[128,128]{1,0:T(8,128)S(1)...) custom-call(s32[4,8]{1,0:T(4,128)S(1)} %bitcast.45, ...), custom_call_target="tpu_custom_call" | custom-call | flops 1207959552 | bytes 3621120 | tf_op jit(solution)/shard_map/inner_products/pallas_call | solution.py:463
  15.0 1.9 %collective-permute-done.3 = bf16[144,128]{1,0:T(8,128)(2,1)S(1)} collective-permute-done((bf16[144,128]{1,0:T(8,128)(2,1)S(1)}, bf16[144,128]{1,0:T(8,128)(2,1)S(1)}, u32[]{:S(2)}, u32[]{:S(2)}) %collective-permute-start.3) | collective-permute-done | bytes 36896 | tf_op jit(solution)/shard_map/ppermute | solution.py:486
  16.9 1.2 %gradients.1 = (f32[1152,128]{1,0:T(8,128)S(1)}, bf16[1152,128]{1,0:T(8,128)(2,1)S(1)}, bf16[128,128]{1,0:T(8,128)(2,1)S(1)}, bf16[128,128]{1,0:T(8,128)(2,1)S(1...) custom-call(f32[128,128]{1,0:T(8,128)S(1)} %get-tuple-element.42.preb_ref, ...), custom_call_target="tpu_custom_call" | custom-call | flops 75497472 | bytes 3682304 | tf_op jit(solution)/shard_map/gradients/pallas_call | solution.py:463
  18.1 0.1 collective-permute-start.4
  18.2 1.5 %collective-permute-done.4 = bf16[1152,128]{1,0:T(8,128)(2,1)S(1)} collective-permute-done((bf16[1152,128]{1,0:T(8,128)(2,1)S(1)}, bf16[1152,128]{1,0:T(8,128)(2,1)S(1)}, u32[]{:S(2)}, u32[]{:S(2)}) %collective-permute-start.4) | collective-permute-done | bytes 294944 | tf_op jit(solution)/shard_map/ppermute | solution.py:486
  19.8 0.1 fusion.4
  19.8 0.6 %collective-permute-start.7 = (bf16[432,128]{1,0:T(8,128)(2,1)S(1)}, bf16[432,128]{1,0:T(8,128)(2,1)S(1)}, u32[]{:S(2)}, u32[]{:S(2)}) collective-permute-start(bf16[432,128]{1,0:T(8,128)(2,1)S(1)} %pad_maximum_fusion.2), channel_id=1, source_target_pairs={{0,4},{1,5},{2,6},{3,7},{4,0},{5,1},{6,2},{7,3},{8,12},{9,13},{10,... | collective-permute-start | bytes 331784 | tf_op jit(solution)/shard_map/ppermute | solution.py:486
  20.4 2.4 %collective-permute-start.5 = (bf16[288,128]{1,0:T(8,128)(2,1)S(1)}, bf16[288,128]{1,0:T(8,128)(2,1)S(1)}, u32[]{:S(2)}, u32[]{:S(2)}) collective-permute-start(bf16[288,128]{1,0:T(8,128)(2,1)S(1)} %get-tuple-element.82), channel_id=1, source_target_pairs={{0,6},{1,7},{2,4},{3,5},{4,2},{5,3},{6,0},{7,1},{8,14},{9,15},{10,... | collective-permute-start | bytes 221192 | tf_op jit(solution)/shard_map/ppermute | solution.py:486
  22.9 0.5 %collective-permute-start.6 = (bf16[288,128]{1,0:T(8,128)(2,1)S(1)}, bf16[288,128]{1,0:T(8,128)(2,1)S(1)}, u32[]{:S(2)}, u32[]{:S(2)}) collective-permute-start(bf16[288,128]{1,0:T(8,128)(2,1)S(1)} %get-tuple-element.81), channel_id=1, source_target_pairs={{0,2},{1,3},{2,0},{3,1},{4,6},{5,7},{6,4},{7,5},{8,10},{9,11},{10,... | collective-permute-start | bytes 221192 | tf_op jit(solution)/shard_map/ppermute | solution.py:486
  23.4 4.3 %collective-permute-done.5 = bf16[288,128]{1,0:T(8,128)(2,1)S(1)} collective-permute-done((bf16[288,128]{1,0:T(8,128)(2,1)S(1)}, bf16[288,128]{1,0:T(8,128)(2,1)S(1)}, u32[]{:S(2)}, u32[]{:S(2)}) %collective-permute-start.5) | collective-permute-done | bytes 73760 | tf_op jit(solution)/shard_map/ppermute | solution.py:486
  27.7 0.6 %collective-permute-done.6 = bf16[288,128]{1,0:T(8,128)(2,1)S(1)} collective-permute-done((bf16[288,128]{1,0:T(8,128)(2,1)S(1)}, bf16[288,128]{1,0:T(8,128)(2,1)S(1)}, u32[]{:S(2)}, u32[]{:S(2)}) %collective-permute-start.6) | collective-permute-done | bytes 73760 | tf_op jit(solution)/shard_map/ppermute | solution.py:486
  28.2 0.1 fusion.1
  28.3 1.0 %collective-permute-start.9 = (bf16[432,128]{1,0:T(8,128)(2,1)S(1)}, bf16[432,128]{1,0:T(8,128)(2,1)S(1)}, u32[]{:S(2)}, u32[]{:S(2)}) collective-permute-start(bf16[432,128]{1,0:T(8,128)(2,1)S(1)} %pad_maximum_fusion.3), channel_id=1, source_target_pairs={{0,16},{1,17},{2,18},{3,19},{4,20},{5,21},{6,22},{7,23},{8,24},{9,... | collective-permute-start | bytes 331784 | tf_op jit(solution)/shard_map/ppermute | solution.py:486
  29.4 1.9 %collective-permute-start.10 = (bf16[352,128]{1,0:T(8,128)(2,1)S(1)}, bf16[352,128]{1,0:T(8,128)(2,1)S(1)}, u32[]{:S(2)}, u32[]{:S(2)}) collective-permute-start(bf16[352,128]{1,0:T(8,128)(2,1)S(1)} %get-tuple-element.90), channel_id=1, source_target_pairs={{0,24},{1,25},{2,26},{3,27},{4,28},{5,29},{6,30},{7,31},{8,16},{9,... | collective-permute-start | bytes 270344 | tf_op jit(solution)/shard_map/ppermute | solution.py:486
  31.2 0.7 %collective-permute-start.8 = (bf16[352,128]{1,0:T(8,128)(2,1)S(1)}, bf16[352,128]{1,0:T(8,128)(2,1)S(1)}, u32[]{:S(2)}, u32[]{:S(2)}) collective-permute-start(bf16[352,128]{1,0:T(8,128)(2,1)S(1)} %get-tuple-element.89), channel_id=1, source_target_pairs={{0,8},{1,9},{2,10},{3,11},{4,12},{5,13},{6,14},{7,15},{8,0},{9,1},... | collective-permute-start | bytes 270344 | tf_op jit(solution)/shard_map/ppermute | solution.py:486
  32.0 2.2 %later_products.1 = (f32[1024,128]{1,0:T(8,128)S(1)}, f32[1024,128]{1,0:T(8,128)S(1)}, bf16[1024,160]{1,0:T(8,128)(2,1)S(1)}, bf16[1024,128]{1,0:T(8,128)(2,1)S(1)}) custom-call(s32[4,8]{1,0:T(4,128)S(1)} %bitcast.46, s32[4,8]{1,0:T(4,128)S(1)} %bitcast.49, bf16[1024,128]{1,0:T(8,128)(2,1)S(1)} %bitcast.40, bf16[1024,128]{1,0:T(8,128)(2,1)S(1)} %bitcast.43, ...), custom_call_target="tpu_custom_call" | custom-call | flops 603979776 | bytes 3342592 | tf_op jit(solution)/shard_map/later_products/pallas_call | solution.py:463
  34.2 1.9 %collective-permute-done.10 = bf16[352,128]{1,0:T(8,128)(2,1)S(1)} collective-permute-done((bf16[352,128]{1,0:T(8,128)(2,1)S(1)}, bf16[352,128]{1,0:T(8,128)(2,1)S(1)}, u32[]{:S(2)}, u32[]{:S(2)}) %collective-permute-start.10) | collective-permute-done | bytes 90144 | tf_op jit(solution)/shard_map/ppermute | solution.py:486
  36.1 1.5 %collective-permute-done.8 = bf16[352,128]{1,0:T(8,128)(2,1)S(1)} collective-permute-done((bf16[352,128]{1,0:T(8,128)(2,1)S(1)}, bf16[352,128]{1,0:T(8,128)(2,1)S(1)}, u32[]{:S(2)}, u32[]{:S(2)}) %collective-permute-start.8) | collective-permute-done | bytes 90144 | tf_op jit(solution)/shard_map/ppermute | solution.py:486
  37.6 0.9 %collective-permute-start.11 = (bf16[288,128]{1,0:T(8,128)(2,1)S(1)}, bf16[288,128]{1,0:T(8,128)(2,1)S(1)}, u32[]{:S(2)}, u32[]{:S(2)}) collective-permute-start(bf16[288,128]{1,0:T(8,128)(2,1)S(1)} %add_add_fusion), channel_id=1, source_target_pairs={{0,2},{1,3},{2,0},{3,1},{4,6},{5,7},{6,4},{7,5},{8,10},{9,11},{10,... | collective-permute-start | bytes 221192 | tf_op jit(solution)/shard_map/ppermute | solution.py:486
  38.5 0.6 %collective-permute-start.12 = (bf16[288,128]{1,0:T(8,128)(2,1)S(1)}, bf16[288,128]{1,0:T(8,128)(2,1)S(1)}, u32[]{:S(2)}, u32[]{:S(2)}) collective-permute-start(bf16[288,128]{1,0:T(8,128)(2,1)S(1)} %add_add_fusion), channel_id=1, source_target_pairs={{0,4},{1,5},{2,6},{3,7},{4,0},{5,1},{6,2},{7,3},{8,12},{9,13},{10,... | collective-permute-start | bytes 221192 | tf_op jit(solution)/shard_map/ppermute | solution.py:486
  39.1 2.0 %collective-permute-start.13 = (bf16[288,128]{1,0:T(8,128)(2,1)S(1)}, bf16[288,128]{1,0:T(8,128)(2,1)S(1)}, u32[]{:S(2)}, u32[]{:S(2)}) collective-permute-start(bf16[288,128]{1,0:T(8,128)(2,1)S(1)} %add_add_fusion), channel_id=1, source_target_pairs={{0,6},{1,7},{2,4},{3,5},{4,2},{5,3},{6,0},{7,1},{8,14},{9,15},{10,... | collective-permute-start | bytes 221192 | tf_op jit(solution)/shard_map/ppermute | solution.py:486
  41.2 1.6 %outputs.1 = (bf16[1024,128]{1,0:T(8,128)(2,1)}, bf16[1024,128]{1,0:T(8,128)(2,1)}) custom-call(f32[1024,128]{1,0:T(8,128)S(1)} %get-tuple-element.71.part_ref, f32[1024,128]{1,0:T(8,128)S(1)} %get-tuple-element.72.dpart_ref, bf16[1024,160]{1,0:T(8,128)(2,1)S(1)} %get-tuple-element.73.scatter_ref, bf16[1024,128]{1,0:T(8,128)(2,1)S(1)} %get-tuple-element.74.column_ref, ...), custom_call_target="tpu_custom_call" | custom-call | flops 75497472 | bytes 2838528 | tf_op jit(solution)/shard_map/outputs/pallas_call | solution.py:463
  42.8 1.5 %collective-permute-done.13 = bf16[288,128]{1,0:T(8,128)(2,1)S(1)} collective-permute-done((bf16[288,128]{1,0:T(8,128)(2,1)S(1)}, bf16[288,128]{1,0:T(8,128)(2,1)S(1)}, u32[]{:S(2)}, u32[]{:S(2)}) %collective-permute-start.13) | collective-permute-done | bytes 73760 | tf_op jit(solution)/shard_map/ppermute | solution.py:486
  44.5 0.1 collective-permute-start.14
  44.6 1.6 %collective-permute-done.14 = bf16[4,288,128]{2,1,0:T(8,128)(2,1)S(1)} collective-permute-done((bf16[4,288,128]{2,1,0:T(8,128)(2,1)S(1)}, bf16[4,288,128]{2,1,0:T(8,128)(2,1)S(1)}, u32[]{:S(2)}, u32[]{:S(2)}) %collective-permute-start.14) | collective-permute-done | bytes 294944 | tf_op jit(solution)/shard_map/ppermute | solution.py:486
  46.1 1.1 %convert_multiply_fusion = (f32[4,288,128]{2,1,0:T(8,128)}, f32[4,288,128]{2,1,0:T(8,128)}) fusion(bf16[4,288,128]{2,1,0:T(8,128)(2,1)S(1)} %collective-permute-done.14, bf16[4,288,128]{2,1,0:T(8,128)(2,1)S(1)} %pad_maximum_fusion.1, pred[]{:T(512)S(6)} %eq.16), kind=kLoop, calls=%fused_computation | loop fusion | flops 884736 | bytes 1769473 | tf_op jit(solution)/shard_map/mul | solution.py:826
  (36 shorter events, 0.3 us)
Async XLA Ops:
  0.6 11.1 %copy-start = (bf16[9,128,128]{2,1,0:T(8,128)(2,1)S(1)}, bf16[9,128,128]{2,1,0:T(8,128)(2,1)}, u32[]{:S(2)}) copy-start(bf16[9,128,128]{2,1,0:T(8,128)(2,1)} %param.7) | copy-start | bytes 884740
  0.6 11.1 %copy-start.1 = (bf16[9,128,128]{2,1,0:T(8,128)(2,1)S(1)}, bf16[9,128,128]{2,1,0:T(8,128)(2,1)}, u32[]{:S(2)}) copy-start(bf16[9,128,128]{2,1,0:T(8,128)(2,1)} %param.8) | copy-start | bytes 884740
  0.7 11.1 %copy-start.2 = (bf16[1,1,32,32,128]{4,3,2,1,0:T(8,128)(2,1)S(1)}, bf16[1,1,32,32,128]{4,3,2,1,0:T(8,128)(2,1)}, u32[]{:S(2)}) copy-start(bf16[1,1,32,32,128]{4,3,2,1,0:T(8,128)(2,1)} %param.6) | copy-start | bytes 786436
  0.7 11.1 %copy-start.3 = (bf16[1,1,32,32,128]{4,3,2,1,0:T(8,128)(2,1)S(1)}, bf16[1,1,32,32,128]{4,3,2,1,0:T(8,128)(2,1)}, u32[]{:S(2)}) copy-start(bf16[1,1,32,32,128]{4,3,2,1,0:T(8,128)(2,1)} %param.9) | copy-start | bytes 786436
  0.7 11.1 %copy-start.4 = (s32[8,4]{0,1:T(4,128)S(1)}, s32[8,4]{0,1:T(4,128)}, u32[]{:S(2)}) copy-start(s32[8,4]{0,1:T(4,128)} %param.10) | copy-start | bytes 388
  0.7 11.1 %copy-start.5 = (s32[8,4]{0,1:T(4,128)S(1)}, s32[8,4]{0,1:T(4,128)}, u32[]{:S(2)}) copy-start(s32[8,4]{0,1:T(4,128)} %param.11) | copy-start | bytes 388
  2.9 8.0 %collective-permute-start = (bf16[80,128]{1,0:T(8,128)(2,1)}, bf16[80,128]{1,0:T(8,128)(2,1)S(1)}, u32[]{:S(2)}, u32[]{:S(2)}) collective-permute-start(bf16[80,128]{1,0:T(8,128)(2,1)} %get-tuple-element.49), channel_id=1, source_target_pairs={{0,4},{1,5},{2,6},{3,7},{4,0},{5,1},{6,2},{7,3},{8,12},{9,13},{10,... | collective-permute-start | bytes 61448 | tf_op jit(solution)/shard_map/ppermute | solution.py:486
  5.9 11.0 %collective-permute-start.1 = (bf16[64,128]{1,0:T(8,128)(2,1)}, bf16[64,128]{1,0:T(8,128)(2,1)S(1)}, u32[]{:S(2)}, u32[]{:S(2)}) collective-permute-start(bf16[64,128]{1,0:T(8,128)(2,1)} %get-tuple-element.50), channel_id=1, source_target_pairs={{0,12},{1,13},{2,14},{3,15},{4,8},{5,9},{6,10},{7,11},{8,4},{9,5},... | collective-permute-start | bytes 49160 | tf_op jit(solution)/shard_map/ppermute | solution.py:486
  7.4 9.4 %collective-permute-start.2 = (bf16[64,128]{1,0:T(8,128)(2,1)}, bf16[64,128]{1,0:T(8,128)(2,1)S(1)}, u32[]{:S(2)}, u32[]{:S(2)}) collective-permute-start(bf16[64,128]{1,0:T(8,128)(2,1)} %get-tuple-element.51), channel_id=1, source_target_pairs={{0,28},{1,29},{2,30},{3,31},{4,24},{5,25},{6,26},{7,27},{8,20},{9,... | collective-permute-start | bytes 49160 | tf_op jit(solution)/shard_map/ppermute | solution.py:486
  11.6 5.3 %collective-permute-start.3 = (bf16[144,128]{1,0:T(8,128)(2,1)S(1)}, bf16[144,128]{1,0:T(8,128)(2,1)S(1)}, u32[]{:S(2)}, u32[]{:S(2)}) collective-permute-start(bf16[144,128]{1,0:T(8,128)(2,1)S(1)} %pad_maximum_fusion.6), channel_id=1, source_target_pairs={{0,16},{1,17},{2,18},{3,19},{4,20},{5,21},{6,22},{7,23},{8,24},{9,... | collective-permute-start | bytes 110600 | tf_op jit(solution)/shard_map/ppermute | solution.py:486
  18.1 1.6 %collective-permute-start.4 = (bf16[1152,128]{1,0:T(8,128)(2,1)S(1)}, bf16[1152,128]{1,0:T(8,128)(2,1)S(1)}, u32[]{:S(2)}, u32[]{:S(2)}) collective-permute-start(bf16[1152,128]{1,0:T(8,128)(2,1)S(1)} %get-tuple-element.54), channel_id=1, source_target_pairs={{0,1},{1,0},{2,3},{3,2},{4,5},{5,4},{6,7},{7,6},{8,9},{9,8},{10,11... | collective-permute-start | bytes 884744 | tf_op jit(solution)/shard_map/ppermute | solution.py:486
  19.8 8.4 %collective-permute-start.7 = (bf16[432,128]{1,0:T(8,128)(2,1)S(1)}, bf16[432,128]{1,0:T(8,128)(2,1)S(1)}, u32[]{:S(2)}, u32[]{:S(2)}) collective-permute-start(bf16[432,128]{1,0:T(8,128)(2,1)S(1)} %pad_maximum_fusion.2), channel_id=1, source_target_pairs={{0,4},{1,5},{2,6},{3,7},{4,0},{5,1},{6,2},{7,3},{8,12},{9,13},{10,... | collective-permute-start | bytes 331784 | tf_op jit(solution)/shard_map/ppermute | solution.py:486
  20.4 7.2 %collective-permute-start.5 = (bf16[288,128]{1,0:T(8,128)(2,1)S(1)}, bf16[288,128]{1,0:T(8,128)(2,1)S(1)}, u32[]{:S(2)}, u32[]{:S(2)}) collective-permute-start(bf16[288,128]{1,0:T(8,128)(2,1)S(1)} %get-tuple-element.82), channel_id=1, source_target_pairs={{0,6},{1,7},{2,4},{3,5},{4,2},{5,3},{6,0},{7,1},{8,14},{9,15},{10,... | collective-permute-start | bytes 221192 | tf_op jit(solution)/shard_map/ppermute | solution.py:486
  22.9 5.3 %collective-permute-start.6 = (bf16[288,128]{1,0:T(8,128)(2,1)S(1)}, bf16[288,128]{1,0:T(8,128)(2,1)S(1)}, u32[]{:S(2)}, u32[]{:S(2)}) collective-permute-start(bf16[288,128]{1,0:T(8,128)(2,1)S(1)} %get-tuple-element.81), channel_id=1, source_target_pairs={{0,2},{1,3},{2,0},{3,1},{4,6},{5,7},{6,4},{7,5},{8,10},{9,11},{10,... | collective-permute-start | bytes 221192 | tf_op jit(solution)/shard_map/ppermute | solution.py:486
  28.3 9.2 %collective-permute-start.9 = (bf16[432,128]{1,0:T(8,128)(2,1)S(1)}, bf16[432,128]{1,0:T(8,128)(2,1)S(1)}, u32[]{:S(2)}, u32[]{:S(2)}) collective-permute-start(bf16[432,128]{1,0:T(8,128)(2,1)S(1)} %pad_maximum_fusion.3), channel_id=1, source_target_pairs={{0,16},{1,17},{2,18},{3,19},{4,20},{5,21},{6,22},{7,23},{8,24},{9,... | collective-permute-start | bytes 331784 | tf_op jit(solution)/shard_map/ppermute | solution.py:486
  29.4 6.7 %collective-permute-start.10 = (bf16[352,128]{1,0:T(8,128)(2,1)S(1)}, bf16[352,128]{1,0:T(8,128)(2,1)S(1)}, u32[]{:S(2)}, u32[]{:S(2)}) collective-permute-start(bf16[352,128]{1,0:T(8,128)(2,1)S(1)} %get-tuple-element.90), channel_id=1, source_target_pairs={{0,24},{1,25},{2,26},{3,27},{4,28},{5,29},{6,30},{7,31},{8,16},{9,... | collective-permute-start | bytes 270344 | tf_op jit(solution)/shard_map/ppermute | solution.py:486
  31.2 6.3 %collective-permute-start.8 = (bf16[352,128]{1,0:T(8,128)(2,1)S(1)}, bf16[352,128]{1,0:T(8,128)(2,1)S(1)}, u32[]{:S(2)}, u32[]{:S(2)}) collective-permute-start(bf16[352,128]{1,0:T(8,128)(2,1)S(1)} %get-tuple-element.89), channel_id=1, source_target_pairs={{0,8},{1,9},{2,10},{3,11},{4,12},{5,13},{6,14},{7,15},{8,0},{9,1},... | collective-permute-start | bytes 270344 | tf_op jit(solution)/shard_map/ppermute | solution.py:486
  37.6 5.2 %collective-permute-start.11 = (bf16[288,128]{1,0:T(8,128)(2,1)S(1)}, bf16[288,128]{1,0:T(8,128)(2,1)S(1)}, u32[]{:S(2)}, u32[]{:S(2)}) collective-permute-start(bf16[288,128]{1,0:T(8,128)(2,1)S(1)} %add_add_fusion), channel_id=1, source_target_pairs={{0,2},{1,3},{2,0},{3,1},{4,6},{5,7},{6,4},{7,5},{8,10},{9,11},{10,... | collective-permute-start | bytes 221192 | tf_op jit(solution)/shard_map/ppermute | solution.py:486
  38.5 4.4 %collective-permute-start.12 = (bf16[288,128]{1,0:T(8,128)(2,1)S(1)}, bf16[288,128]{1,0:T(8,128)(2,1)S(1)}, u32[]{:S(2)}, u32[]{:S(2)}) collective-permute-start(bf16[288,128]{1,0:T(8,128)(2,1)S(1)} %add_add_fusion), channel_id=1, source_target_pairs={{0,4},{1,5},{2,6},{3,7},{4,0},{5,1},{6,2},{7,3},{8,12},{9,13},{10,... | collective-permute-start | bytes 221192 | tf_op jit(solution)/shard_map/ppermute | solution.py:486
  39.1 5.3 %collective-permute-start.13 = (bf16[288,128]{1,0:T(8,128)(2,1)S(1)}, bf16[288,128]{1,0:T(8,128)(2,1)S(1)}, u32[]{:S(2)}, u32[]{:S(2)}) collective-permute-start(bf16[288,128]{1,0:T(8,128)(2,1)S(1)} %add_add_fusion), channel_id=1, source_target_pairs={{0,6},{1,7},{2,4},{3,5},{4,2},{5,3},{6,0},{7,1},{8,14},{9,15},{10,... | collective-permute-start | bytes 221192 | tf_op jit(solution)/shard_map/ppermute | solution.py:486
  44.5 1.6 %collective-permute-start.14 = (bf16[4,288,128]{2,1,0:T(8,128)(2,1)S(1)}, bf16[4,288,128]{2,1,0:T(8,128)(2,1)S(1)}, u32[]{:S(2)}, u32[]{:S(2)}) collective-permute-start(bf16[4,288,128]{2,1,0:T(8,128)(2,1)S(1)} %pad_maximum_fusion.1), channel_id=1, source_target_pairs={{0,1},{1,0},{2,3},{3,2},{4,5},{5,4},{6,7},{7,6},{8,9},{9,8},{10,11... | collective-permute-start | bytes 884744 | tf_op jit(solution)/shard_map/ppermute | solution.py:486

commit v6 on v5

--- a/solution.py
+++ b/solution.py
@@ -547,9 +547,9 @@
 
 
 def reach_neighbours(across, one, three, far, total):
-    across, three, one = swap(across, 4, total), swap(three, 28, total), swap(one, 12, total)
-    two = swap(jnp.concatenate([far, across[-16:]], axis=0), 16, total)
-    return [across, one, three, two[:-16], two[-16:]]
+    two, three, one = swap(far, 16, total), swap(three, 28, total), swap(one, 12, total)
+    across = swap(jnp.concatenate([across, two[-16:]], axis=0), 4, total)
+    return [across, one, three, two[:-16], across[-16:]]
 
 
 def per_device(inputs, weight_one, weight_two, cotangent, edge_code, corner_code):
@@ -567,7 +567,7 @@
     near_b, far_b, corner_b = sds((4 * extent + 16, channels), BF16), sds((4 * extent, channels), BF16), sds((16, channels), BF16)
     pair_b = sds((2 * extent, channels), BF16)
     if hops:
-        first_routed, second_routed = [sds((2 * extent + 16, channels), BF16), pair_b, pair_b, far_b], [near_b, far_b]
+        first_routed, second_routed = [pair_b, pair_b, pair_b, sds((4 * extent + 16, channels), BF16)], [near_b, far_b]
         n_routes = 5
     else:
         first_routed = second_routed = [sds((route_rows(r, extent), channels), BF16) for r in plan]
@@ -579,8 +579,8 @@
             write_near(a, b, near_ref, extent)
             write_far(a, b, outs[3], extent)
             for start, out in zip(near_starts(lax.axis_index("tile"), extent), outs):
-                out[0 : 2 * extent, :] = near_ref[pl.ds(pl.multiple_of(start, 16), 2 * extent), :]
-            outs[0][2 * extent : 2 * extent + 16, :] = near_ref[4 * extent : 4 * extent + 16, :]
+                out[...] = near_ref[pl.ds(pl.multiple_of(start, 16), 2 * extent), :]
+            outs[3][4 * extent : 4 * extent + 16, :] = near_ref[4 * extent : 4 * extent + 16, :]
         else:
             write_routes(a, b, plan, outs, extent)
 

time: 47.5 us -> 47.1 us (level)
  waiting for transfers between devices: 14.8 us -> 14 us
    ppermute x15, waiting for transfers between devices: 14.8 us -> 14 us  [swap(): return lax.ppermute(value, AXES, [(i, i ^ mask) for i in range(total)])]
where the time goes in v6:
time: 47.1 us; the launch traced here: 46.8 us
  starting transfers between devices  19.3 us (41%)
  waiting for transfers between devices  14 us (30%)
  Pallas kernels  10.4 us (22%)
  other arithmetic  2.11 us (4%)
  between operations  0.89 us (2%)
    ppermute x15, starting transfers between devices, swap(): return lax.ppermute(value, AXES, [(i, i ^ mask) for i in range(total)])  19.3 us
    ppermute x15, waiting for transfers between devices, swap(): return lax.ppermute(value, AXES, [(i, i ^ mask) for i in range(total)])  14 us
    pallas_call x5, Pallas kernels, call(): pl.pallas_call(kernel, name=name, out_shape=outs, in_specs=specs, out_spe...  10.4 us
    mul x1, other arithmetic, per_device(): two.astype(F32) * factor  1.13 us
  transfers between devices with their start and end apart: 15, of which 8 were waited for; matrix products, arithmetic and copies ran while one was open for 2% of the time, Pallas kernels for 15%

profile of v6, /device:TPU:0, one launch (start us, length us, event | category | flops | bytes accessed | tf_op | source)
XLA Modules:
  0.0 46.8 jit_solution(15628726569979294191)
XLA Ops:
  0.7 2.2 %first_strips.1 = (bf16[64,128]{1,0:T(8,128)(2,1)}, bf16[64,128]{1,0:T(8,128)(2,1)}, bf16[64,128]{1,0:T(8,128)(2,1)}, bf16[144,128]{1,0:T(8,128)(2,1)}) custom-call(bf16[1024,128]{1,0:T(8,128)(2,1)} %bitcast.38, bf16[1024,128]{1,0:T(8,128)(2,1)} %bitcast.41, s32[4,8]{1,0:T(4,128)} %bitcast.44, s32[4,8]{1,0:T(4,128)} %bitcast.47), custom_call_target="tpu_custom_call" | custom-call | flops 3019898880 | bytes 610560 | tf_op jit(solution)/shard_map/first_strips/pallas_call | solution.py:463
  2.9 4.1 %collective-permute-start = (bf16[144,128]{1,0:T(8,128)(2,1)}, bf16[144,128]{1,0:T(8,128)(2,1)S(1)}, u32[]{:S(2)}, u32[]{:S(2)}) collective-permute-start(bf16[144,128]{1,0:T(8,128)(2,1)} %get-tuple-element.50), channel_id=1, source_target_pairs={{0,16},{1,17},{2,18},{3,19},{4,20},{5,21},{6,22},{7,23},{8,24},{9,... | collective-permute-start | bytes 110600 | tf_op jit(solution)/shard_map/ppermute | solution.py:486
  7.0 2.5 %collective-permute-start.2 = (bf16[64,128]{1,0:T(8,128)(2,1)}, bf16[64,128]{1,0:T(8,128)(2,1)S(1)}, u32[]{:S(2)}, u32[]{:S(2)}) collective-permute-start(bf16[64,128]{1,0:T(8,128)(2,1)} %get-tuple-element.51), channel_id=1, source_target_pairs={{0,12},{1,13},{2,14},{3,15},{4,8},{5,9},{6,10},{7,11},{8,4},{9,5},... | collective-permute-start | bytes 49160 | tf_op jit(solution)/shard_map/ppermute | solution.py:486
  9.5 0.0 collective-permute-done
  9.5 0.7 %pad_maximum_fusion.6 = bf16[80,128]{1,0:T(8,128)(2,1)S(1)} fusion(bf16[16,128]{1,0:T(8,128)(2,1)S(1)} %slice.53, bf16[64,128]{1,0:T(8,128)(2,1)} %get-tuple-element.49), kind=kLoop, calls=%fused_computation.18 | loop fusion | flops 40960 | bytes 40960 | tf_op jit(solution)/shard_map/concatenate | solution.py:551
  10.3 1.8 %collective-permute-start.1 = (bf16[80,128]{1,0:T(8,128)(2,1)S(1)}, bf16[80,128]{1,0:T(8,128)(2,1)S(1)}, u32[]{:S(2)}, u32[]{:S(2)}) collective-permute-start(bf16[80,128]{1,0:T(8,128)(2,1)S(1)} %pad_maximum_fusion.6), channel_id=1, source_target_pairs={{0,4},{1,5},{2,6},{3,7},{4,0},{5,1},{6,2},{7,3},{8,12},{9,13},{10,... | collective-permute-start | bytes 61448 | tf_op jit(solution)/shard_map/ppermute | solution.py:486
  12.1 3.2 %inner_products.1 = (bf16[1024,128]{1,0:T(8,128)(2,1)S(1)}, bf16[1024,128]{1,0:T(8,128)(2,1)S(1)}, f32[128,128]{1,0:T(8,128)S(1)}, f32[128,128]{1,0:T(8,128)S(1)...) custom-call(s32[4,8]{1,0:T(4,128)S(1)} %bitcast.45, ...), custom_call_target="tpu_custom_call" | custom-call | flops 1207959552 | bytes 3621120 | tf_op jit(solution)/shard_map/inner_products/pallas_call | solution.py:463
  15.3 0.8 %collective-permute-done.3.refs_2_ = bf16[64,128]{1,0:T(8,128)(2,1)S(1)} collective-permute-done((bf16[64,128]{1,0:T(8,128)(2,1)}, bf16[64,128]{1,0:T(8,128)(2,1)S(1)}, u32[]{:S(2)}, u32[]{:S(2)}) %collective-permute-start.3) | collective-permute-done | bytes 16416 | tf_op jit(solution)/shard_map/ppermute | solution.py:486
  16.1 1.2 %gradients.1 = (f32[1152,128]{1,0:T(8,128)S(1)}, bf16[1152,128]{1,0:T(8,128)(2,1)S(1)}, bf16[128,128]{1,0:T(8,128)(2,1)S(1)}, bf16[128,128]{1,0:T(8,128)(2,1)S(1...) custom-call(f32[128,128]{1,0:T(8,128)S(1)} %get-tuple-element.42.preb_ref, ...), custom_call_target="tpu_custom_call" | custom-call | flops 75497472 | bytes 3682304 | tf_op jit(solution)/shard_map/gradients/pallas_call | solution.py:463
  17.4 0.1 collective-permute-start.4
  17.5 1.5 %collective-permute-done.4 = bf16[1152,128]{1,0:T(8,128)(2,1)S(1)} collective-permute-done((bf16[1152,128]{1,0:T(8,128)(2,1)S(1)}, bf16[1152,128]{1,0:T(8,128)(2,1)S(1)}, u32[]{:S(2)}, u32[]{:S(2)}) %collective-permute-start.4) | collective-permute-done | bytes 294944 | tf_op jit(solution)/shard_map/ppermute | solution.py:486
  19.0 0.1 fusion.4
  19.1 0.6 %collective-permute-start.7 = (bf16[432,128]{1,0:T(8,128)(2,1)S(1)}, bf16[432,128]{1,0:T(8,128)(2,1)S(1)}, u32[]{:S(2)}, u32[]{:S(2)}) collective-permute-start(bf16[432,128]{1,0:T(8,128)(2,1)S(1)} %pad_maximum_fusion.2), channel_id=1, source_target_pairs={{0,4},{1,5},{2,6},{3,7},{4,0},{5,1},{6,2},{7,3},{8,12},{9,13},{10,... | collective-permute-start | bytes 331784 | tf_op jit(solution)/shard_map/ppermute | solution.py:486
  19.7 2.4 %collective-permute-start.5 = (bf16[288,128]{1,0:T(8,128)(2,1)S(1)}, bf16[288,128]{1,0:T(8,128)(2,1)S(1)}, u32[]{:S(2)}, u32[]{:S(2)}) collective-permute-start(bf16[288,128]{1,0:T(8,128)(2,1)S(1)} %get-tuple-element.82), channel_id=1, source_target_pairs={{0,6},{1,7},{2,4},{3,5},{4,2},{5,3},{6,0},{7,1},{8,14},{9,15},{10,... | collective-permute-start | bytes 221192 | tf_op jit(solution)/shard_map/ppermute | solution.py:486
  22.1 0.5 %collective-permute-start.6 = (bf16[288,128]{1,0:T(8,128)(2,1)S(1)}, bf16[288,128]{1,0:T(8,128)(2,1)S(1)}, u32[]{:S(2)}, u32[]{:S(2)}) collective-permute-start(bf16[288,128]{1,0:T(8,128)(2,1)S(1)} %get-tuple-element.81), channel_id=1, source_target_pairs={{0,2},{1,3},{2,0},{3,1},{4,6},{5,7},{6,4},{7,5},{8,10},{9,11},{10,... | collective-permute-start | bytes 221192 | tf_op jit(solution)/shard_map/ppermute | solution.py:486
  22.6 4.3 %collective-permute-done.5 = bf16[288,128]{1,0:T(8,128)(2,1)S(1)} collective-permute-done((bf16[288,128]{1,0:T(8,128)(2,1)S(1)}, bf16[288,128]{1,0:T(8,128)(2,1)S(1)}, u32[]{:S(2)}, u32[]{:S(2)}) %collective-permute-start.5) | collective-permute-done | bytes 73760 | tf_op jit(solution)/shard_map/ppermute | solution.py:486
  26.9 0.6 %collective-permute-done.6 = bf16[288,128]{1,0:T(8,128)(2,1)S(1)} collective-permute-done((bf16[288,128]{1,0:T(8,128)(2,1)S(1)}, bf16[288,128]{1,0:T(8,128)(2,1)S(1)}, u32[]{:S(2)}, u32[]{:S(2)}) %collective-permute-start.6) | collective-permute-done | bytes 73760 | tf_op jit(solution)/shard_map/ppermute | solution.py:486
  27.5 0.1 fusion.1
  27.6 1.7 %collective-permute-start.9 = (bf16[432,128]{1,0:T(8,128)(2,1)S(1)}, bf16[432,128]{1,0:T(8,128)(2,1)S(1)}, u32[]{:S(2)}, u32[]{:S(2)}) collective-permute-start(bf16[432,128]{1,0:T(8,128)(2,1)S(1)} %pad_maximum_fusion.3), channel_id=1, source_target_pairs={{0,16},{1,17},{2,18},{3,19},{4,20},{5,21},{6,22},{7,23},{8,24},{9,... | collective-permute-start | bytes 331784 | tf_op jit(solution)/shard_map/ppermute | solution.py:486
  29.3 1.4 %collective-permute-start.10 = (bf16[352,128]{1,0:T(8,128)(2,1)S(1)}, bf16[352,128]{1,0:T(8,128)(2,1)S(1)}, u32[]{:S(2)}, u32[]{:S(2)}) collective-permute-start(bf16[352,128]{1,0:T(8,128)(2,1)S(1)} %get-tuple-element.90), channel_id=1, source_target_pairs={{0,24},{1,25},{2,26},{3,27},{4,28},{5,29},{6,30},{7,31},{8,16},{9,... | collective-permute-start | bytes 270344 | tf_op jit(solution)/shard_map/ppermute | solution.py:486
  30.7 0.6 %collective-permute-start.8 = (bf16[352,128]{1,0:T(8,128)(2,1)S(1)}, bf16[352,128]{1,0:T(8,128)(2,1)S(1)}, u32[]{:S(2)}, u32[]{:S(2)}) collective-permute-start(bf16[352,128]{1,0:T(8,128)(2,1)S(1)} %get-tuple-element.89), channel_id=1, source_target_pairs={{0,8},{1,9},{2,10},{3,11},{4,12},{5,13},{6,14},{7,15},{8,0},{9,1},... | collective-permute-start | bytes 270344 | tf_op jit(solution)/shard_map/ppermute | solution.py:486
  31.3 2.2 %later_products.1 = (f32[1024,128]{1,0:T(8,128)S(1)}, f32[1024,128]{1,0:T(8,128)S(1)}, bf16[1024,160]{1,0:T(8,128)(2,1)S(1)}, bf16[1024,128]{1,0:T(8,128)(2,1)S(1)}) custom-call(s32[4,8]{1,0:T(4,128)S(1)} %bitcast.46, s32[4,8]{1,0:T(4,128)S(1)} %bitcast.49, bf16[1024,128]{1,0:T(8,128)(2,1)S(1)} %bitcast.40, bf16[1024,128]{1,0:T(8,128)(2,1)S(1)} %bitcast.43, ...), custom_call_target="tpu_custom_call" | custom-call | flops 603979776 | bytes 3342592 | tf_op jit(solution)/shard_map/later_products/pallas_call | solution.py:463
  33.5 2.5 %collective-permute-done.10 = bf16[352,128]{1,0:T(8,128)(2,1)S(1)} collective-permute-done((bf16[352,128]{1,0:T(8,128)(2,1)S(1)}, bf16[352,128]{1,0:T(8,128)(2,1)S(1)}, u32[]{:S(2)}, u32[]{:S(2)}) %collective-permute-start.10) | collective-permute-done | bytes 90144 | tf_op jit(solution)/shard_map/ppermute | solution.py:486
  36.0 1.2 %collective-permute-done.8 = bf16[352,128]{1,0:T(8,128)(2,1)S(1)} collective-permute-done((bf16[352,128]{1,0:T(8,128)(2,1)S(1)}, bf16[352,128]{1,0:T(8,128)(2,1)S(1)}, u32[]{:S(2)}, u32[]{:S(2)}) %collective-permute-start.8) | collective-permute-done | bytes 90144 | tf_op jit(solution)/shard_map/ppermute | solution.py:486
  37.3 0.6 %collective-permute-start.11 = (bf16[288,128]{1,0:T(8,128)(2,1)S(1)}, bf16[288,128]{1,0:T(8,128)(2,1)S(1)}, u32[]{:S(2)}, u32[]{:S(2)}) collective-permute-start(bf16[288,128]{1,0:T(8,128)(2,1)S(1)} %add_add_fusion), channel_id=1, source_target_pairs={{0,2},{1,3},{2,0},{3,1},{4,6},{5,7},{6,4},{7,5},{8,10},{9,11},{10,... | collective-permute-start | bytes 221192 | tf_op jit(solution)/shard_map/ppermute | solution.py:486
  37.9 0.6 %collective-permute-start.12 = (bf16[288,128]{1,0:T(8,128)(2,1)S(1)}, bf16[288,128]{1,0:T(8,128)(2,1)S(1)}, u32[]{:S(2)}, u32[]{:S(2)}) collective-permute-start(bf16[288,128]{1,0:T(8,128)(2,1)S(1)} %add_add_fusion), channel_id=1, source_target_pairs={{0,4},{1,5},{2,6},{3,7},{4,0},{5,1},{6,2},{7,3},{8,12},{9,13},{10,... | collective-permute-start | bytes 221192 | tf_op jit(solution)/shard_map/ppermute | solution.py:486
  38.5 2.3 %collective-permute-start.13 = (bf16[288,128]{1,0:T(8,128)(2,1)S(1)}, bf16[288,128]{1,0:T(8,128)(2,1)S(1)}, u32[]{:S(2)}, u32[]{:S(2)}) collective-permute-start(bf16[288,128]{1,0:T(8,128)(2,1)S(1)} %add_add_fusion), channel_id=1, source_target_pairs={{0,6},{1,7},{2,4},{3,5},{4,2},{5,3},{6,0},{7,1},{8,14},{9,15},{10,... | collective-permute-start | bytes 221192 | tf_op jit(solution)/shard_map/ppermute | solution.py:486
  40.8 1.6 %outputs.1 = (bf16[1024,128]{1,0:T(8,128)(2,1)}, bf16[1024,128]{1,0:T(8,128)(2,1)}) custom-call(f32[1024,128]{1,0:T(8,128)S(1)} %get-tuple-element.71.part_ref, f32[1024,128]{1,0:T(8,128)S(1)} %get-tuple-element.72.dpart_ref, bf16[1024,160]{1,0:T(8,128)(2,1)S(1)} %get-tuple-element.73.scatter_ref, bf16[1024,128]{1,0:T(8,128)(2,1)S(1)} %get-tuple-element.74.column_ref, ...), custom_call_target="tpu_custom_call" | custom-call | flops 75497472 | bytes 2838528 | tf_op jit(solution)/shard_map/outputs/pallas_call | solution.py:463
  42.5 1.5 %collective-permute-done.13 = bf16[288,128]{1,0:T(8,128)(2,1)S(1)} collective-permute-done((bf16[288,128]{1,0:T(8,128)(2,1)S(1)}, bf16[288,128]{1,0:T(8,128)(2,1)S(1)}, u32[]{:S(2)}, u32[]{:S(2)}) %collective-permute-start.13) | collective-permute-done | bytes 73760 | tf_op jit(solution)/shard_map/ppermute | solution.py:486
  44.1 0.1 collective-permute-start.14
  44.2 1.6 %collective-permute-done.14 = bf16[4,288,128]{2,1,0:T(8,128)(2,1)S(1)} collective-permute-done((bf16[4,288,128]{2,1,0:T(8,128)(2,1)S(1)}, bf16[4,288,128]{2,1,0:T(8,128)(2,1)S(1)}, u32[]{:S(2)}, u32[]{:S(2)}) %collective-permute-start.14) | collective-permute-done | bytes 294944 | tf_op jit(solution)/shard_map/ppermute | solution.py:486
  45.7 1.1 %convert_multiply_fusion = (f32[4,288,128]{2,1,0:T(8,128)}, f32[4,288,128]{2,1,0:T(8,128)}) fusion(bf16[4,288,128]{2,1,0:T(8,128)(2,1)S(1)} %collective-permute-done.14, bf16[4,288,128]{2,1,0:T(8,128)(2,1)S(1)} %pad_maximum_fusion.1, pred[]{:T(512)S(6)} %eq.16), kind=kLoop, calls=%fused_computation | loop fusion | flops 884736 | bytes 1769473 | tf_op jit(solution)/shard_map/mul | solution.py:826
  (36 shorter events, 0.3 us)
Async XLA Ops:
  0.6 11.4 %copy-start = (bf16[9,128,128]{2,1,0:T(8,128)(2,1)S(1)}, bf16[9,128,128]{2,1,0:T(8,128)(2,1)}, u32[]{:S(2)}) copy-start(bf16[9,128,128]{2,1,0:T(8,128)(2,1)} %param.7) | copy-start | bytes 884740
  0.6 11.4 %copy-start.1 = (bf16[9,128,128]{2,1,0:T(8,128)(2,1)S(1)}, bf16[9,128,128]{2,1,0:T(8,128)(2,1)}, u32[]{:S(2)}) copy-start(bf16[9,128,128]{2,1,0:T(8,128)(2,1)} %param.8) | copy-start | bytes 884740
  0.7 11.4 %copy-start.2 = (bf16[1,1,32,32,128]{4,3,2,1,0:T(8,128)(2,1)S(1)}, bf16[1,1,32,32,128]{4,3,2,1,0:T(8,128)(2,1)}, u32[]{:S(2)}) copy-start(bf16[1,1,32,32,128]{4,3,2,1,0:T(8,128)(2,1)} %param.6) | copy-start | bytes 786436
  0.7 11.4 %copy-start.3 = (bf16[1,1,32,32,128]{4,3,2,1,0:T(8,128)(2,1)S(1)}, bf16[1,1,32,32,128]{4,3,2,1,0:T(8,128)(2,1)}, u32[]{:S(2)}) copy-start(bf16[1,1,32,32,128]{4,3,2,1,0:T(8,128)(2,1)} %param.9) | copy-start | bytes 786436
  0.7 11.4 %copy-start.4 = (s32[8,4]{0,1:T(4,128)S(1)}, s32[8,4]{0,1:T(4,128)}, u32[]{:S(2)}) copy-start(s32[8,4]{0,1:T(4,128)} %param.10) | copy-start | bytes 388
  0.7 11.4 %copy-start.5 = (s32[8,4]{0,1:T(4,128)S(1)}, s32[8,4]{0,1:T(4,128)}, u32[]{:S(2)}) copy-start(s32[8,4]{0,1:T(4,128)} %param.11) | copy-start | bytes 388
  2.9 6.6 %collective-permute-start = (bf16[144,128]{1,0:T(8,128)(2,1)}, bf16[144,128]{1,0:T(8,128)(2,1)S(1)}, u32[]{:S(2)}, u32[]{:S(2)}) collective-permute-start(bf16[144,128]{1,0:T(8,128)(2,1)} %get-tuple-element.50), channel_id=1, source_target_pairs={{0,16},{1,17},{2,18},{3,19},{4,20},{5,21},{6,22},{7,23},{8,24},{9,... | collective-permute-start | bytes 110600 | tf_op jit(solution)/shard_map/ppermute | solution.py:486
  7.0 8.3 %collective-permute-start.2 = (bf16[64,128]{1,0:T(8,128)(2,1)}, bf16[64,128]{1,0:T(8,128)(2,1)S(1)}, u32[]{:S(2)}, u32[]{:S(2)}) collective-permute-start(bf16[64,128]{1,0:T(8,128)(2,1)} %get-tuple-element.51), channel_id=1, source_target_pairs={{0,12},{1,13},{2,14},{3,15},{4,8},{5,9},{6,10},{7,11},{8,4},{9,5},... | collective-permute-start | bytes 49160 | tf_op jit(solution)/shard_map/ppermute | solution.py:486
  9.5 6.6 %collective-permute-start.3 = (bf16[64,128]{1,0:T(8,128)(2,1)}, bf16[64,128]{1,0:T(8,128)(2,1)S(1)}, u32[]{:S(2)}, u32[]{:S(2)}) collective-permute-start(bf16[64,128]{1,0:T(8,128)(2,1)} %get-tuple-element.52), channel_id=1, source_target_pairs={{0,28},{1,29},{2,30},{3,31},{4,24},{5,25},{6,26},{7,27},{8,20},{9,... | collective-permute-start | bytes 49160 | tf_op jit(solution)/shard_map/ppermute | solution.py:486
  10.3 5.0 %collective-permute-start.1 = (bf16[80,128]{1,0:T(8,128)(2,1)S(1)}, bf16[80,128]{1,0:T(8,128)(2,1)S(1)}, u32[]{:S(2)}, u32[]{:S(2)}) collective-permute-start(bf16[80,128]{1,0:T(8,128)(2,1)S(1)} %pad_maximum_fusion.6), channel_id=1, source_target_pairs={{0,4},{1,5},{2,6},{3,7},{4,0},{5,1},{6,2},{7,3},{8,12},{9,13},{10,... | collective-permute-start | bytes 61448 | tf_op jit(solution)/shard_map/ppermute | solution.py:486
  17.4 1.6 %collective-permute-start.4 = (bf16[1152,128]{1,0:T(8,128)(2,1)S(1)}, bf16[1152,128]{1,0:T(8,128)(2,1)S(1)}, u32[]{:S(2)}, u32[]{:S(2)}) collective-permute-start(bf16[1152,128]{1,0:T(8,128)(2,1)S(1)} %get-tuple-element.54), channel_id=1, source_target_pairs={{0,1},{1,0},{2,3},{3,2},{4,5},{5,4},{6,7},{7,6},{8,9},{9,8},{10,11... | collective-permute-start | bytes 884744 | tf_op jit(solution)/shard_map/ppermute | solution.py:486
  19.1 8.4 %collective-permute-start.7 = (bf16[432,128]{1,0:T(8,128)(2,1)S(1)}, bf16[432,128]{1,0:T(8,128)(2,1)S(1)}, u32[]{:S(2)}, u32[]{:S(2)}) collective-permute-start(bf16[432,128]{1,0:T(8,128)(2,1)S(1)} %pad_maximum_fusion.2), channel_id=1, source_target_pairs={{0,4},{1,5},{2,6},{3,7},{4,0},{5,1},{6,2},{7,3},{8,12},{9,13},{10,... | collective-permute-start | bytes 331784 | tf_op jit(solution)/shard_map/ppermute | solution.py:486
  19.7 7.2 %collective-permute-start.5 = (bf16[288,128]{1,0:T(8,128)(2,1)S(1)}, bf16[288,128]{1,0:T(8,128)(2,1)S(1)}, u32[]{:S(2)}, u32[]{:S(2)}) collective-permute-start(bf16[288,128]{1,0:T(8,128)(2,1)S(1)} %get-tuple-element.82), channel_id=1, source_target_pairs={{0,6},{1,7},{2,4},{3,5},{4,2},{5,3},{6,0},{7,1},{8,14},{9,15},{10,... | collective-permute-start | bytes 221192 | tf_op jit(solution)/shard_map/ppermute | solution.py:486
  22.1 5.3 %collective-permute-start.6 = (bf16[288,128]{1,0:T(8,128)(2,1)S(1)}, bf16[288,128]{1,0:T(8,128)(2,1)S(1)}, u32[]{:S(2)}, u32[]{:S(2)}) collective-permute-start(bf16[288,128]{1,0:T(8,128)(2,1)S(1)} %get-tuple-element.81), channel_id=1, source_target_pairs={{0,2},{1,3},{2,0},{3,1},{4,6},{5,7},{6,4},{7,5},{8,10},{9,11},{10,... | collective-permute-start | bytes 221192 | tf_op jit(solution)/shard_map/ppermute | solution.py:486
  27.6 9.7 %collective-permute-start.9 = (bf16[432,128]{1,0:T(8,128)(2,1)S(1)}, bf16[432,128]{1,0:T(8,128)(2,1)S(1)}, u32[]{:S(2)}, u32[]{:S(2)}) collective-permute-start(bf16[432,128]{1,0:T(8,128)(2,1)S(1)} %pad_maximum_fusion.3), channel_id=1, source_target_pairs={{0,16},{1,17},{2,18},{3,19},{4,20},{5,21},{6,22},{7,23},{8,24},{9,... | collective-permute-start | bytes 331784 | tf_op jit(solution)/shard_map/ppermute | solution.py:486
  29.3 6.7 %collective-permute-start.10 = (bf16[352,128]{1,0:T(8,128)(2,1)S(1)}, bf16[352,128]{1,0:T(8,128)(2,1)S(1)}, u32[]{:S(2)}, u32[]{:S(2)}) collective-permute-start(bf16[352,128]{1,0:T(8,128)(2,1)S(1)} %get-tuple-element.90), channel_id=1, source_target_pairs={{0,24},{1,25},{2,26},{3,27},{4,28},{5,29},{6,30},{7,31},{8,16},{9,... | collective-permute-start | bytes 270344 | tf_op jit(solution)/shard_map/ppermute | solution.py:486
  30.7 6.6 %collective-permute-start.8 = (bf16[352,128]{1,0:T(8,128)(2,1)S(1)}, bf16[352,128]{1,0:T(8,128)(2,1)S(1)}, u32[]{:S(2)}, u32[]{:S(2)}) collective-permute-start(bf16[352,128]{1,0:T(8,128)(2,1)S(1)} %get-tuple-element.89), channel_id=1, source_target_pairs={{0,8},{1,9},{2,10},{3,11},{4,12},{5,13},{6,14},{7,15},{8,0},{9,1},... | collective-permute-start | bytes 270344 | tf_op jit(solution)/shard_map/ppermute | solution.py:486
  37.3 5.2 %collective-permute-start.11 = (bf16[288,128]{1,0:T(8,128)(2,1)S(1)}, bf16[288,128]{1,0:T(8,128)(2,1)S(1)}, u32[]{:S(2)}, u32[]{:S(2)}) collective-permute-start(bf16[288,128]{1,0:T(8,128)(2,1)S(1)} %add_add_fusion), channel_id=1, source_target_pairs={{0,2},{1,3},{2,0},{3,1},{4,6},{5,7},{6,4},{7,5},{8,10},{9,11},{10,... | collective-permute-start | bytes 221192 | tf_op jit(solution)/shard_map/ppermute | solution.py:486
  37.9 4.6 %collective-permute-start.12 = (bf16[288,128]{1,0:T(8,128)(2,1)S(1)}, bf16[288,128]{1,0:T(8,128)(2,1)S(1)}, u32[]{:S(2)}, u32[]{:S(2)}) collective-permute-start(bf16[288,128]{1,0:T(8,128)(2,1)S(1)} %add_add_fusion), channel_id=1, source_target_pairs={{0,4},{1,5},{2,6},{3,7},{4,0},{5,1},{6,2},{7,3},{8,12},{9,13},{10,... | collective-permute-start | bytes 221192 | tf_op jit(solution)/shard_map/ppermute | solution.py:486
  38.5 5.5 %collective-permute-start.13 = (bf16[288,128]{1,0:T(8,128)(2,1)S(1)}, bf16[288,128]{1,0:T(8,128)(2,1)S(1)}, u32[]{:S(2)}, u32[]{:S(2)}) collective-permute-start(bf16[288,128]{1,0:T(8,128)(2,1)S(1)} %add_add_fusion), channel_id=1, source_target_pairs={{0,6},{1,7},{2,4},{3,5},{4,2},{5,3},{6,0},{7,1},{8,14},{9,15},{10,... | collective-permute-start | bytes 221192 | tf_op jit(solution)/shard_map/ppermute | solution.py:486
  44.1 1.6 %collective-permute-start.14 = (bf16[4,288,128]{2,1,0:T(8,128)(2,1)S(1)}, bf16[4,288,128]{2,1,0:T(8,128)(2,1)S(1)}, u32[]{:S(2)}, u32[]{:S(2)}) collective-permute-start(bf16[4,288,128]{2,1,0:T(8,128)(2,1)S(1)} %pad_maximum_fusion.1), channel_id=1, source_target_pairs={{0,1},{1,0},{2,3},{3,2},{4,5},{5,4},{6,7},{7,6},{8,9},{9,8},{10,11... | collective-permute-start | bytes 884744 | tf_op jit(solution)/shard_map/ppermute | solution.py:486

commit v7 on v6

--- a/solution.py
+++ b/solution.py
@@ -1,3 +1,4 @@
+import functools
 import math
 
 import jax
@@ -540,10 +541,51 @@
     return whole, extras, done
 
 
-def join_cores(whole, total):
+def join_cores(whole, factor, total):
+    rows, channels = whole.shape
+    half = sds(whole.shape, F32)
+    pieces = 2
+    step = rows // pieces
+
+    def write(flip, value_ref, outs, scaled_ref, sems):
+        mine = (lax.axis_index("dp") + flip) % 2
+
+        def send(out_ref):
+            copies = []
+            for i in range(pieces):
+                span = pl.ds(i * step, step)
+                scaled_ref[span, :] = value_ref[span, :].astype(F32) * factor
+                copies.append(pltpu.make_async_copy(scaled_ref.at[span], out_ref.at[span], sems.at[i]))
+                copies[-1].start()
+            for copy in copies:
+                copy.wait()
+
+        for which in range(2):
+            pl.when(mine == which)(functools.partial(send, outs[which]))
+
+    def own_half(value_ref, one_ref, two_ref, scaled_ref, sems):
+        write(0, value_ref, (one_ref, two_ref), scaled_ref, sems)
+
+    def other_half(value_ref, one_in, two_in, one_ref, two_ref, scaled_ref, sems):
+        write(1, value_ref, (one_ref, two_ref), scaled_ref, sems)
+
+    def run(kernel, name, operands, aliases):
+        anywhere = pl.BlockSpec(memory_space=pl.ANY)
+        return pl.pallas_call(
+            kernel,
+            name=name,
+            out_shape=[half, half],
+            in_specs=[pl.BlockSpec(memory_space=pltpu.VMEM)] + [anywhere] * (len(operands) - 1),
+            out_specs=[anywhere, anywhere],
+            scratch_shapes=[pltpu.VMEM(half.shape, F32), pltpu.SemaphoreType.DMA((pieces,))],
+            input_output_aliases=aliases,
+            cost_estimate=pl.CostEstimate(flops=rows * channels, bytes_accessed=6 * rows * channels, transcendentals=0),
+            compiler_params=pltpu.CompilerParams(vmem_limit_bytes=LIMIT),
+        )(*operands)
+
     other = swap(whole, 1, total)
-    low = (lax.axis_index(AXES) & 1) == 0
-    return jnp.where(low, whole, other), jnp.where(low, other, whole)
+    begun = run(own_half, "own_half", (whole,), {})
+    return run(other_half, "other_half", (other, *begun), {1: 0, 2: 1})
 
 
 def reach_neighbours(across, one, three, far, total):
@@ -817,13 +859,13 @@
         flops=conv // 4,
     )
     whole, output, d_input = lax.optimization_barrier((whole, output, d_input))
-    one, two = join_cores(whole, total)
+    one, two = join_cores(whole.reshape(9 * channels, channels), factor, total)
     shape = (9, channels, channels)
     return (
         output.reshape(inputs.shape),
         d_input.reshape(inputs.shape),
-        (one.astype(F32) * factor).reshape(shape),
-        (two.astype(F32) * factor).reshape(shape),
+        one.reshape(shape),
+        two.reshape(shape),
     )
 
 

time: 47.1 us -> 46.8 us (level)
  Pallas kernels: 10.4 us -> 12.1 us
  other arithmetic: 2.11 us -> 0.99 us
  waiting for transfers between devices: 14 us -> 13.1 us
    pallas_call x0 -> x2, Pallas kernels: none -> 1.72 us  [run(): pl.pallas_call(kernel, name=name, out_shape=[half, half], in_specs=[pl.Bl...]
    mul x1 -> x0, other arithmetic: 1.13 us -> none  [per_device(): two.astype(F32) * factor]
    ppermute x15, waiting for transfers between devices: 14 us -> 13.1 us  [swap(): return lax.ppermute(value, AXES, [(i, i ^ mask) for i in range(total)])]
  transfers between devices with their start and end apart: 15 -> 15, of which waited for: 8 -> 8; matrix products, arithmetic and copies ran while one was open for 2% -> 2% of each run, Pallas kernels for 15% -> 17%
where the time goes in v7:
time: 46.8 us; the launch traced here: 46.6 us
  starting transfers between devices  19.3 us (41%)
  waiting for transfers between devices  13.1 us (28%)
  Pallas kernels  12.1 us (26%)
  other arithmetic  0.99 us (2%)
  between operations  0.89 us (2%)
    ppermute x15, starting transfers between devices, swap(): return lax.ppermute(value, AXES, [(i, i ^ mask) for i in range(total)])  19.3 us
    ppermute x15, waiting for transfers between devices, swap(): return lax.ppermute(value, AXES, [(i, i ^ mask) for i in range(total)])  13.1 us
    pallas_call x5, Pallas kernels, call(): pl.pallas_call(kernel, name=name, out_shape=outs, in_specs=specs, out_spe...  10.4 us
    pallas_call x2, Pallas kernels, run(): pl.pallas_call(kernel, name=name, out_shape=[half, half], in_specs=[pl.Bl...  1.72 us
  transfers between devices with their start and end apart: 15, of which 8 were waited for; matrix products, arithmetic and copies ran while one was open for 2% of the time, Pallas kernels for 17%

profile of v7, /device:TPU:0, one launch (start us, length us, event | category | flops | bytes accessed | tf_op | source)
XLA Modules:
  0.0 46.6 jit_solution(4571643871545597145)
XLA Ops:
  0.7 2.2 %first_strips.1 = (bf16[64,128]{1,0:T(8,128)(2,1)}, bf16[64,128]{1,0:T(8,128)(2,1)}, bf16[64,128]{1,0:T(8,128)(2,1)}, bf16[144,128]{1,0:T(8,128)(2,1)}) custom-call(bf16[1024,128]{1,0:T(8,128)(2,1)} %bitcast.41, bf16[1024,128]{1,0:T(8,128)(2,1)} %bitcast.44, s32[4,8]{1,0:T(4,128)} %bitcast.47, s32[4,8]{1,0:T(4,128)} %bitcast.50), custom_call_target="tpu_custom_call" | custom-call | flops 3019898880 | bytes 610560 | tf_op jit(solution)/shard_map/first_strips/pallas_call | solution.py:464
  2.9 4.1 %collective-permute-start = (bf16[144,128]{1,0:T(8,128)(2,1)}, bf16[144,128]{1,0:T(8,128)(2,1)S(1)}, u32[]{:S(2)}, u32[]{:S(2)}) collective-permute-start(bf16[144,128]{1,0:T(8,128)(2,1)} %get-tuple-element.54), channel_id=1, source_target_pairs={{0,16},{1,17},{2,18},{3,19},{4,20},{5,21},{6,22},{7,23},{8,24},{9,... | collective-permute-start | bytes 110600 | tf_op jit(solution)/shard_map/ppermute | solution.py:487
  7.0 2.5 %collective-permute-start.2 = (bf16[64,128]{1,0:T(8,128)(2,1)}, bf16[64,128]{1,0:T(8,128)(2,1)S(1)}, u32[]{:S(2)}, u32[]{:S(2)}) collective-permute-start(bf16[64,128]{1,0:T(8,128)(2,1)} %get-tuple-element.55), channel_id=1, source_target_pairs={{0,12},{1,13},{2,14},{3,15},{4,8},{5,9},{6,10},{7,11},{8,4},{9,5},... | collective-permute-start | bytes 49160 | tf_op jit(solution)/shard_map/ppermute | solution.py:487
  9.5 0.7 %pad_maximum_fusion.6 = bf16[80,128]{1,0:T(8,128)(2,1)S(1)} fusion(bf16[16,128]{1,0:T(8,128)(2,1)S(1)} %slice.53, bf16[64,128]{1,0:T(8,128)(2,1)} %get-tuple-element.53), kind=kLoop, calls=%fused_computation.16 | loop fusion | flops 40960 | bytes 40960 | tf_op jit(solution)/shard_map/concatenate | solution.py:593
  10.3 1.8 %collective-permute-start.1 = (bf16[80,128]{1,0:T(8,128)(2,1)S(1)}, bf16[80,128]{1,0:T(8,128)(2,1)S(1)}, u32[]{:S(2)}, u32[]{:S(2)}) collective-permute-start(bf16[80,128]{1,0:T(8,128)(2,1)S(1)} %pad_maximum_fusion.6), channel_id=1, source_target_pairs={{0,4},{1,5},{2,6},{3,7},{4,0},{5,1},{6,2},{7,3},{8,12},{9,13},{10,... | collective-permute-start | bytes 61448 | tf_op jit(solution)/shard_map/ppermute | solution.py:487
  12.1 3.2 %inner_products.1 = (bf16[1024,128]{1,0:T(8,128)(2,1)S(1)}, bf16[1024,128]{1,0:T(8,128)(2,1)S(1)}, f32[128,128]{1,0:T(8,128)S(1)}, f32[128,128]{1,0:T(8,128)S(1)...) custom-call(s32[4,8]{1,0:T(4,128)S(1)} %bitcast.48, ...), custom_call_target="tpu_custom_call" | custom-call | flops 1207959552 | bytes 3621120 | tf_op jit(solution)/shard_map/inner_products/pallas_call | solution.py:464
  15.3 0.8 %collective-permute-done.3.refs_2_ = bf16[64,128]{1,0:T(8,128)(2,1)S(1)} collective-permute-done((bf16[64,128]{1,0:T(8,128)(2,1)}, bf16[64,128]{1,0:T(8,128)(2,1)S(1)}, u32[]{:S(2)}, u32[]{:S(2)}) %collective-permute-start.3) | collective-permute-done | bytes 16416 | tf_op jit(solution)/shard_map/ppermute | solution.py:487
  16.1 1.2 %gradients.1 = (f32[1152,128]{1,0:T(8,128)S(1)}, bf16[1152,128]{1,0:T(8,128)(2,1)S(1)}, bf16[128,128]{1,0:T(8,128)(2,1)S(1)}, bf16[128,128]{1,0:T(8,128)(2,1)S(1...) custom-call(f32[128,128]{1,0:T(8,128)S(1)} %get-tuple-element.46.preb_ref, ...), custom_call_target="tpu_custom_call" | custom-call | flops 75497472 | bytes 3682304 | tf_op jit(solution)/shard_map/gradients/pallas_call | solution.py:464
  17.4 0.1 collective-permute-start.4
  17.5 1.5 %collective-permute-done.4 = bf16[1152,128]{1,0:T(8,128)(2,1)S(1)} collective-permute-done((bf16[1152,128]{1,0:T(8,128)(2,1)S(1)}, bf16[1152,128]{1,0:T(8,128)(2,1)S(1)}, u32[]{:S(2)}, u32[]{:S(2)}) %collective-permute-start.4) | collective-permute-done | bytes 294944 | tf_op jit(solution)/shard_map/ppermute | solution.py:487
  19.0 0.1 fusion.4
  19.1 0.6 %collective-permute-start.7 = (bf16[432,128]{1,0:T(8,128)(2,1)S(1)}, bf16[432,128]{1,0:T(8,128)(2,1)S(1)}, u32[]{:S(2)}, u32[]{:S(2)}) collective-permute-start(bf16[432,128]{1,0:T(8,128)(2,1)S(1)} %pad_maximum_fusion.2), channel_id=1, source_target_pairs={{0,4},{1,5},{2,6},{3,7},{4,0},{5,1},{6,2},{7,3},{8,12},{9,13},{10,... | collective-permute-start | bytes 331784 | tf_op jit(solution)/shard_map/ppermute | solution.py:487
  19.7 2.4 %collective-permute-start.5 = (bf16[288,128]{1,0:T(8,128)(2,1)S(1)}, bf16[288,128]{1,0:T(8,128)(2,1)S(1)}, u32[]{:S(2)}, u32[]{:S(2)}) collective-permute-start(bf16[288,128]{1,0:T(8,128)(2,1)S(1)} %get-tuple-element.90), channel_id=1, source_target_pairs={{0,6},{1,7},{2,4},{3,5},{4,2},{5,3},{6,0},{7,1},{8,14},{9,15},{10,... | collective-permute-start | bytes 221192 | tf_op jit(solution)/shard_map/ppermute | solution.py:487
  22.1 0.5 %collective-permute-start.6 = (bf16[288,128]{1,0:T(8,128)(2,1)S(1)}, bf16[288,128]{1,0:T(8,128)(2,1)S(1)}, u32[]{:S(2)}, u32[]{:S(2)}) collective-permute-start(bf16[288,128]{1,0:T(8,128)(2,1)S(1)} %get-tuple-element.89), channel_id=1, source_target_pairs={{0,2},{1,3},{2,0},{3,1},{4,6},{5,7},{6,4},{7,5},{8,10},{9,11},{10,... | collective-permute-start | bytes 221192 | tf_op jit(solution)/shard_map/ppermute | solution.py:487
  22.6 4.3 %collective-permute-done.5 = bf16[288,128]{1,0:T(8,128)(2,1)S(1)} collective-permute-done((bf16[288,128]{1,0:T(8,128)(2,1)S(1)}, bf16[288,128]{1,0:T(8,128)(2,1)S(1)}, u32[]{:S(2)}, u32[]{:S(2)}) %collective-permute-start.5) | collective-permute-done | bytes 73760 | tf_op jit(solution)/shard_map/ppermute | solution.py:487
  26.9 0.6 %collective-permute-done.6 = bf16[288,128]{1,0:T(8,128)(2,1)S(1)} collective-permute-done((bf16[288,128]{1,0:T(8,128)(2,1)S(1)}, bf16[288,128]{1,0:T(8,128)(2,1)S(1)}, u32[]{:S(2)}, u32[]{:S(2)}) %collective-permute-start.6) | collective-permute-done | bytes 73760 | tf_op jit(solution)/shard_map/ppermute | solution.py:487
  27.5 0.1 fusion.1
  27.6 1.7 %collective-permute-start.9 = (bf16[432,128]{1,0:T(8,128)(2,1)S(1)}, bf16[432,128]{1,0:T(8,128)(2,1)S(1)}, u32[]{:S(2)}, u32[]{:S(2)}) collective-permute-start(bf16[432,128]{1,0:T(8,128)(2,1)S(1)} %pad_maximum_fusion.3), channel_id=1, source_target_pairs={{0,16},{1,17},{2,18},{3,19},{4,20},{5,21},{6,22},{7,23},{8,24},{9,... | collective-permute-start | bytes 331784 | tf_op jit(solution)/shard_map/ppermute | solution.py:487
  29.3 1.4 %collective-permute-start.10 = (bf16[352,128]{1,0:T(8,128)(2,1)S(1)}, bf16[352,128]{1,0:T(8,128)(2,1)S(1)}, u32[]{:S(2)}, u32[]{:S(2)}) collective-permute-start(bf16[352,128]{1,0:T(8,128)(2,1)S(1)} %get-tuple-element.96), channel_id=1, source_target_pairs={{0,24},{1,25},{2,26},{3,27},{4,28},{5,29},{6,30},{7,31},{8,16},{9,... | collective-permute-start | bytes 270344 | tf_op jit(solution)/shard_map/ppermute | solution.py:487
  30.7 0.6 %collective-permute-start.8 = (bf16[352,128]{1,0:T(8,128)(2,1)S(1)}, bf16[352,128]{1,0:T(8,128)(2,1)S(1)}, u32[]{:S(2)}, u32[]{:S(2)}) collective-permute-start(bf16[352,128]{1,0:T(8,128)(2,1)S(1)} %get-tuple-element.95), channel_id=1, source_target_pairs={{0,8},{1,9},{2,10},{3,11},{4,12},{5,13},{6,14},{7,15},{8,0},{9,1},... | collective-permute-start | bytes 270344 | tf_op jit(solution)/shard_map/ppermute | solution.py:487
  31.3 2.2 %later_products.1 = (f32[1024,128]{1,0:T(8,128)S(1)}, f32[1024,128]{1,0:T(8,128)S(1)}, bf16[1024,160]{1,0:T(8,128)(2,1)S(1)}, bf16[1024,128]{1,0:T(8,128)(2,1)S(1)}) custom-call(s32[4,8]{1,0:T(4,128)S(1)} %bitcast.49, s32[4,8]{1,0:T(4,128)S(1)} %bitcast.52, bf16[1024,128]{1,0:T(8,128)(2,1)S(1)} %bitcast.43, bf16[1024,128]{1,0:T(8,128)(2,1)S(1)} %bitcast.46, ...), custom_call_target="tpu_custom_call" | custom-call | flops 603979776 | bytes 3342592 | tf_op jit(solution)/shard_map/later_products/pallas_call | solution.py:464
  33.5 2.5 %collective-permute-done.10 = bf16[352,128]{1,0:T(8,128)(2,1)S(1)} collective-permute-done((bf16[352,128]{1,0:T(8,128)(2,1)S(1)}, bf16[352,128]{1,0:T(8,128)(2,1)S(1)}, u32[]{:S(2)}, u32[]{:S(2)}) %collective-permute-start.10) | collective-permute-done | bytes 90144 | tf_op jit(solution)/shard_map/ppermute | solution.py:487
  36.0 1.2 %collective-permute-done.8 = bf16[352,128]{1,0:T(8,128)(2,1)S(1)} collective-permute-done((bf16[352,128]{1,0:T(8,128)(2,1)S(1)}, bf16[352,128]{1,0:T(8,128)(2,1)S(1)}, u32[]{:S(2)}, u32[]{:S(2)}) %collective-permute-start.8) | collective-permute-done | bytes 90144 | tf_op jit(solution)/shard_map/ppermute | solution.py:487
  37.3 0.6 %collective-permute-start.11 = (bf16[288,128]{1,0:T(8,128)(2,1)S(1)}, bf16[288,128]{1,0:T(8,128)(2,1)S(1)}, u32[]{:S(2)}, u32[]{:S(2)}) collective-permute-start(bf16[288,128]{1,0:T(8,128)(2,1)S(1)} %add_add_fusion), channel_id=1, source_target_pairs={{0,2},{1,3},{2,0},{3,1},{4,6},{5,7},{6,4},{7,5},{8,10},{9,11},{10,... | collective-permute-start | bytes 221192 | tf_op jit(solution)/shard_map/ppermute | solution.py:487
  37.9 0.6 %collective-permute-start.12 = (bf16[288,128]{1,0:T(8,128)(2,1)S(1)}, bf16[288,128]{1,0:T(8,128)(2,1)S(1)}, u32[]{:S(2)}, u32[]{:S(2)}) collective-permute-start(bf16[288,128]{1,0:T(8,128)(2,1)S(1)} %add_add_fusion), channel_id=1, source_target_pairs={{0,4},{1,5},{2,6},{3,7},{4,0},{5,1},{6,2},{7,3},{8,12},{9,13},{10,... | collective-permute-start | bytes 221192 | tf_op jit(solution)/shard_map/ppermute | solution.py:487
  38.5 2.3 %collective-permute-start.13 = (bf16[288,128]{1,0:T(8,128)(2,1)S(1)}, bf16[288,128]{1,0:T(8,128)(2,1)S(1)}, u32[]{:S(2)}, u32[]{:S(2)}) collective-permute-start(bf16[288,128]{1,0:T(8,128)(2,1)S(1)} %add_add_fusion), channel_id=1, source_target_pairs={{0,6},{1,7},{2,4},{3,5},{4,2},{5,3},{6,0},{7,1},{8,14},{9,15},{10,... | collective-permute-start | bytes 221192 | tf_op jit(solution)/shard_map/ppermute | solution.py:487
  40.8 1.6 %outputs.1 = (bf16[1024,128]{1,0:T(8,128)(2,1)}, bf16[1024,128]{1,0:T(8,128)(2,1)}) custom-call(f32[1024,128]{1,0:T(8,128)S(1)} %get-tuple-element.75.part_ref, f32[1024,128]{1,0:T(8,128)S(1)} %get-tuple-element.76.dpart_ref, bf16[1024,160]{1,0:T(8,128)(2,1)S(1)} %get-tuple-element.77.scatter_ref, bf16[1024,128]{1,0:T(8,128)(2,1)S(1)} %get-tuple-element.78.column_ref, ...), custom_call_target="tpu_custom_call" | custom-call | flops 75497472 | bytes 2838528 | tf_op jit(solution)/shard_map/outputs/pallas_call | solution.py:464
  42.5 1.5 %collective-permute-done.13 = bf16[288,128]{1,0:T(8,128)(2,1)S(1)} collective-permute-done((bf16[288,128]{1,0:T(8,128)(2,1)S(1)}, bf16[288,128]{1,0:T(8,128)(2,1)S(1)}, u32[]{:S(2)}, u32[]{:S(2)}) %collective-permute-start.13) | collective-permute-done | bytes 73760 | tf_op jit(solution)/shard_map/ppermute | solution.py:487
  44.1 0.1 collective-permute-start.14
  44.2 0.9 %own_half.1 = (f32[1152,128]{1,0:T(8,128)}, f32[1152,128]{1,0:T(8,128)}) custom-call(bf16[1152,128]{1,0:T(8,128)(2,1)S(1)} %bitcast.38), custom_call_target="tpu_custom_call" | custom-call | flops 147456 | bytes 884736 | tf_op jit(solution)/shard_map/own_half/pallas_call | solution.py:574
  45.0 0.7 %collective-permute-done.14.value_ref = bf16[1152,128]{1,0:T(8,128)(2,1)S(1)} collective-permute-done((bf16[1152,128]{1,0:T(8,128)(2,1)S(1)}, bf16[1152,128]{1,0:T(8,128)(2,1)S(1)}, u32[]{:S(2)}, u32[]{:S(2)}) %collective-permute-start.14) | collective-permute-done | bytes 294944 | tf_op jit(solution)/shard_map/ppermute | solution.py:487
  45.7 0.9 %other_half.1 = (f32[1152,128]{1,0:T(8,128)}, f32[1152,128]{1,0:T(8,128)}) custom-call(bf16[1152,128]{1,0:T(8,128)(2,1)S(1)} %collective-permute-done.14.value_ref, f32[1152,128]{1,0:T(8,128)} %get-tuple-element.84.one_in, f32[1152,128]{1,0:T(8,128)} %get-tuple-element.85.two_in), custom_call_target="tpu_custom_call", output_to_operand_aliasing={{0}: (1, {}), {1}: (2, {})} | custom-call | flops 147456 | bytes 884736 | tf_op jit(solution)/shard_map/other_half/pallas_call | solution.py:574
  (37 shorter events, 0.3 us)
Async XLA Ops:
  0.6 11.4 %copy-start = (bf16[9,128,128]{2,1,0:T(8,128)(2,1)S(1)}, bf16[9,128,128]{2,1,0:T(8,128)(2,1)}, u32[]{:S(2)}) copy-start(bf16[9,128,128]{2,1,0:T(8,128)(2,1)} %param.7) | copy-start | bytes 884740
  0.6 11.4 %copy-start.1 = (bf16[9,128,128]{2,1,0:T(8,128)(2,1)S(1)}, bf16[9,128,128]{2,1,0:T(8,128)(2,1)}, u32[]{:S(2)}) copy-start(bf16[9,128,128]{2,1,0:T(8,128)(2,1)} %param.8) | copy-start | bytes 884740
  0.7 11.4 %copy-start.2 = (bf16[1,1,32,32,128]{4,3,2,1,0:T(8,128)(2,1)S(1)}, bf16[1,1,32,32,128]{4,3,2,1,0:T(8,128)(2,1)}, u32[]{:S(2)}) copy-start(bf16[1,1,32,32,128]{4,3,2,1,0:T(8,128)(2,1)} %param.6) | copy-start | bytes 786436
  0.7 11.4 %copy-start.3 = (bf16[1,1,32,32,128]{4,3,2,1,0:T(8,128)(2,1)S(1)}, bf16[1,1,32,32,128]{4,3,2,1,0:T(8,128)(2,1)}, u32[]{:S(2)}) copy-start(bf16[1,1,32,32,128]{4,3,2,1,0:T(8,128)(2,1)} %param.9) | copy-start | bytes 786436
  0.7 11.4 %copy-start.4 = (s32[8,4]{0,1:T(4,128)S(1)}, s32[8,4]{0,1:T(4,128)}, u32[]{:S(2)}) copy-start(s32[8,4]{0,1:T(4,128)} %param.10) | copy-start | bytes 388
  0.7 11.4 %copy-start.5 = (s32[8,4]{0,1:T(4,128)S(1)}, s32[8,4]{0,1:T(4,128)}, u32[]{:S(2)}) copy-start(s32[8,4]{0,1:T(4,128)} %param.11) | copy-start | bytes 388
  2.9 6.6 %collective-permute-start = (bf16[144,128]{1,0:T(8,128)(2,1)}, bf16[144,128]{1,0:T(8,128)(2,1)S(1)}, u32[]{:S(2)}, u32[]{:S(2)}) collective-permute-start(bf16[144,128]{1,0:T(8,128)(2,1)} %get-tuple-element.54), channel_id=1, source_target_pairs={{0,16},{1,17},{2,18},{3,19},{4,20},{5,21},{6,22},{7,23},{8,24},{9,... | collective-permute-start | bytes 110600 | tf_op jit(solution)/shard_map/ppermute | solution.py:487
  7.0 8.3 %collective-permute-start.2 = (bf16[64,128]{1,0:T(8,128)(2,1)}, bf16[64,128]{1,0:T(8,128)(2,1)S(1)}, u32[]{:S(2)}, u32[]{:S(2)}) collective-permute-start(bf16[64,128]{1,0:T(8,128)(2,1)} %get-tuple-element.55), channel_id=1, source_target_pairs={{0,12},{1,13},{2,14},{3,15},{4,8},{5,9},{6,10},{7,11},{8,4},{9,5},... | collective-permute-start | bytes 49160 | tf_op jit(solution)/shard_map/ppermute | solution.py:487
  9.5 6.6 %collective-permute-start.3 = (bf16[64,128]{1,0:T(8,128)(2,1)}, bf16[64,128]{1,0:T(8,128)(2,1)S(1)}, u32[]{:S(2)}, u32[]{:S(2)}) collective-permute-start(bf16[64,128]{1,0:T(8,128)(2,1)} %get-tuple-element.56), channel_id=1, source_target_pairs={{0,28},{1,29},{2,30},{3,31},{4,24},{5,25},{6,26},{7,27},{8,20},{9,... | collective-permute-start | bytes 49160 | tf_op jit(solution)/shard_map/ppermute | solution.py:487
  10.3 5.0 %collective-permute-start.1 = (bf16[80,128]{1,0:T(8,128)(2,1)S(1)}, bf16[80,128]{1,0:T(8,128)(2,1)S(1)}, u32[]{:S(2)}, u32[]{:S(2)}) collective-permute-start(bf16[80,128]{1,0:T(8,128)(2,1)S(1)} %pad_maximum_fusion.6), channel_id=1, source_target_pairs={{0,4},{1,5},{2,6},{3,7},{4,0},{5,1},{6,2},{7,3},{8,12},{9,13},{10,... | collective-permute-start | bytes 61448 | tf_op jit(solution)/shard_map/ppermute | solution.py:487
  17.4 1.6 %collective-permute-start.4 = (bf16[1152,128]{1,0:T(8,128)(2,1)S(1)}, bf16[1152,128]{1,0:T(8,128)(2,1)S(1)}, u32[]{:S(2)}, u32[]{:S(2)}) collective-permute-start(bf16[1152,128]{1,0:T(8,128)(2,1)S(1)} %get-tuple-element.58), channel_id=1, source_target_pairs={{0,1},{1,0},{2,3},{3,2},{4,5},{5,4},{6,7},{7,6},{8,9},{9,8},{10,11... | collective-permute-start | bytes 884744 | tf_op jit(solution)/shard_map/ppermute | solution.py:487
  19.1 8.4 %collective-permute-start.7 = (bf16[432,128]{1,0:T(8,128)(2,1)S(1)}, bf16[432,128]{1,0:T(8,128)(2,1)S(1)}, u32[]{:S(2)}, u32[]{:S(2)}) collective-permute-start(bf16[432,128]{1,0:T(8,128)(2,1)S(1)} %pad_maximum_fusion.2), channel_id=1, source_target_pairs={{0,4},{1,5},{2,6},{3,7},{4,0},{5,1},{6,2},{7,3},{8,12},{9,13},{10,... | collective-permute-start | bytes 331784 | tf_op jit(solution)/shard_map/ppermute | solution.py:487
  19.7 7.2 %collective-permute-start.5 = (bf16[288,128]{1,0:T(8,128)(2,1)S(1)}, bf16[288,128]{1,0:T(8,128)(2,1)S(1)}, u32[]{:S(2)}, u32[]{:S(2)}) collective-permute-start(bf16[288,128]{1,0:T(8,128)(2,1)S(1)} %get-tuple-element.90), channel_id=1, source_target_pairs={{0,6},{1,7},{2,4},{3,5},{4,2},{5,3},{6,0},{7,1},{8,14},{9,15},{10,... | collective-permute-start | bytes 221192 | tf_op jit(solution)/shard_map/ppermute | solution.py:487
  22.1 5.3 %collective-permute-start.6 = (bf16[288,128]{1,0:T(8,128)(2,1)S(1)}, bf16[288,128]{1,0:T(8,128)(2,1)S(1)}, u32[]{:S(2)}, u32[]{:S(2)}) collective-permute-start(bf16[288,128]{1,0:T(8,128)(2,1)S(1)} %get-tuple-element.89), channel_id=1, source_target_pairs={{0,2},{1,3},{2,0},{3,1},{4,6},{5,7},{6,4},{7,5},{8,10},{9,11},{10,... | collective-permute-start | bytes 221192 | tf_op jit(solution)/shard_map/ppermute | solution.py:487
  27.6 9.7 %collective-permute-start.9 = (bf16[432,128]{1,0:T(8,128)(2,1)S(1)}, bf16[432,128]{1,0:T(8,128)(2,1)S(1)}, u32[]{:S(2)}, u32[]{:S(2)}) collective-permute-start(bf16[432,128]{1,0:T(8,128)(2,1)S(1)} %pad_maximum_fusion.3), channel_id=1, source_target_pairs={{0,16},{1,17},{2,18},{3,19},{4,20},{5,21},{6,22},{7,23},{8,24},{9,... | collective-permute-start | bytes 331784 | tf_op jit(solution)/shard_map/ppermute | solution.py:487
  29.3 6.7 %collective-permute-start.10 = (bf16[352,128]{1,0:T(8,128)(2,1)S(1)}, bf16[352,128]{1,0:T(8,128)(2,1)S(1)}, u32[]{:S(2)}, u32[]{:S(2)}) collective-permute-start(bf16[352,128]{1,0:T(8,128)(2,1)S(1)} %get-tuple-element.96), channel_id=1, source_target_pairs={{0,24},{1,25},{2,26},{3,27},{4,28},{5,29},{6,30},{7,31},{8,16},{9,... | collective-permute-start | bytes 270344 | tf_op jit(solution)/shard_map/ppermute | solution.py:487
  30.7 6.6 %collective-permute-start.8 = (bf16[352,128]{1,0:T(8,128)(2,1)S(1)}, bf16[352,128]{1,0:T(8,128)(2,1)S(1)}, u32[]{:S(2)}, u32[]{:S(2)}) collective-permute-start(bf16[352,128]{1,0:T(8,128)(2,1)S(1)} %get-tuple-element.95), channel_id=1, source_target_pairs={{0,8},{1,9},{2,10},{3,11},{4,12},{5,13},{6,14},{7,15},{8,0},{9,1},... | collective-permute-start | bytes 270344 | tf_op jit(solution)/shard_map/ppermute | solution.py:487
  37.3 5.2 %collective-permute-start.11 = (bf16[288,128]{1,0:T(8,128)(2,1)S(1)}, bf16[288,128]{1,0:T(8,128)(2,1)S(1)}, u32[]{:S(2)}, u32[]{:S(2)}) collective-permute-start(bf16[288,128]{1,0:T(8,128)(2,1)S(1)} %add_add_fusion), channel_id=1, source_target_pairs={{0,2},{1,3},{2,0},{3,1},{4,6},{5,7},{6,4},{7,5},{8,10},{9,11},{10,... | collective-permute-start | bytes 221192 | tf_op jit(solution)/shard_map/ppermute | solution.py:487
  37.9 4.6 %collective-permute-start.12 = (bf16[288,128]{1,0:T(8,128)(2,1)S(1)}, bf16[288,128]{1,0:T(8,128)(2,1)S(1)}, u32[]{:S(2)}, u32[]{:S(2)}) collective-permute-start(bf16[288,128]{1,0:T(8,128)(2,1)S(1)} %add_add_fusion), channel_id=1, source_target_pairs={{0,4},{1,5},{2,6},{3,7},{4,0},{5,1},{6,2},{7,3},{8,12},{9,13},{10,... | collective-permute-start | bytes 221192 | tf_op jit(solution)/shard_map/ppermute | solution.py:487
  38.5 5.5 %collective-permute-start.13 = (bf16[288,128]{1,0:T(8,128)(2,1)S(1)}, bf16[288,128]{1,0:T(8,128)(2,1)S(1)}, u32[]{:S(2)}, u32[]{:S(2)}) collective-permute-start(bf16[288,128]{1,0:T(8,128)(2,1)S(1)} %add_add_fusion), channel_id=1, source_target_pairs={{0,6},{1,7},{2,4},{3,5},{4,2},{5,3},{6,0},{7,1},{8,14},{9,15},{10,... | collective-permute-start | bytes 221192 | tf_op jit(solution)/shard_map/ppermute | solution.py:487
  44.1 1.6 %collective-permute-start.14 = (bf16[1152,128]{1,0:T(8,128)(2,1)S(1)}, bf16[1152,128]{1,0:T(8,128)(2,1)S(1)}, u32[]{:S(2)}, u32[]{:S(2)}) collective-permute-start(bf16[1152,128]{1,0:T(8,128)(2,1)S(1)} %bitcast.37), channel_id=1, source_target_pairs={{0,1},{1,0},{2,3},{3,2},{4,5},{5,4},{6,7},{7,6},{8,9},{9,8},{10,11... | collective-permute-start | bytes 884744 | tf_op jit(solution)/shard_map/ppermute | solution.py:487

commit v8 on v7

--- a/solution.py
+++ b/solution.py
@@ -650,20 +650,26 @@
         x_ref, g_ref, near_ref, edge_ref, corner_ref, sems = refs[n_first:]
         pairs = [(edge_hbm, edge_ref), (corner_hbm, corner_ref)]
         step = count // pieces
-        for source_ref, target_ref in ((x_hbm, x_ref), (g_hbm, g_ref)):
+        for source_ref, target_ref in ((g_hbm, g_ref), (x_hbm, x_ref)):
             for i in range(pieces):
                 pairs.append((source_ref.at[pl.ds(i * step, step)], target_ref.at[pl.ds(i * step, step)]))
         copies = [pltpu.make_async_copy(a, b, sems.at[i]) for i, (a, b) in enumerate(pairs)]
         for copy in copies:
             copy.start()
-        fixed = block_choice(*fixed_lines(extent), extent)
+
+        def gather_pieces(choice, image_ref, arriving):
+            strips = 0.0
+            for i, copy in enumerate(arriving):
+                copy.wait()
+                span = slice(i * step, (i + 1) * step)
+                strips = strips + dot(choice[:, span], image_ref[span, :])
+            strips = strips.astype(BF16)
+            return [strips[start : start + rows] for start, rows in zip(block_starts(extent), block_rows(extent))]
+
+        b = gather_pieces(block_choice(*fixed_lines(extent), extent), g_ref, copies[2 : 2 + pieces])
         for copy in copies[:2]:
             copy.wait()
-        seam = block_choice(*seam_lines(edge_ref, corner_ref, extent), extent)
-        for copy in copies[2:]:
-            copy.wait()
-        a = gather_blocks(seam, x_ref[...], extent)
-        b = gather_blocks(fixed, g_ref[...], extent)
+        a = gather_pieces(block_choice(*seam_lines(edge_ref, corner_ref, extent), extent), x_ref, copies[2 + pieces :])
         write_first(a, b, outs, near_ref)
 
     first = call(

time: 46.8 us -> 47 us (level)
  no operation moved by 1% of the time
where the time goes in v8:
time: 47 us; the launch traced here: 46.7 us
  starting transfers between devices  19.3 us (41%)
  waiting for transfers between devices  13.1 us (28%)
  Pallas kernels  12.3 us (26%)
  other arithmetic  0.99 us (2%)
  between operations  0.89 us (2%)
    ppermute x15, starting transfers between devices, swap(): return lax.ppermute(value, AXES, [(i, i ^ mask) for i in range(total)])  19.3 us
    ppermute x15, waiting for transfers between devices, swap(): return lax.ppermute(value, AXES, [(i, i ^ mask) for i in range(total)])  13.1 us
    pallas_call x5, Pallas kernels, call(): pl.pallas_call(kernel, name=name, out_shape=outs, in_specs=specs, out_spe...  10.6 us
    pallas_call x2, Pallas kernels, run(): pl.pallas_call(kernel, name=name, out_shape=[half, half], in_specs=[pl.Bl...  1.72 us
  transfers between devices with their start and end apart: 15, of which 8 were waited for; matrix products, arithmetic and copies ran while one was open for 2% of the time, Pallas kernels for 17%

profile of v8, /device:TPU:0, one launch (start us, length us, event | category | flops | bytes accessed | tf_op | source)
XLA Modules:
  0.0 46.7 jit_solution(16542320798127338952)
XLA Ops:
  0.7 2.3 %first_strips.1 = (bf16[64,128]{1,0:T(8,128)(2,1)}, bf16[64,128]{1,0:T(8,128)(2,1)}, bf16[64,128]{1,0:T(8,128)(2,1)}, bf16[144,128]{1,0:T(8,128)(2,1)}) custom-call(bf16[1024,128]{1,0:T(8,128)(2,1)} %bitcast.41, bf16[1024,128]{1,0:T(8,128)(2,1)} %bitcast.44, s32[4,8]{1,0:T(4,128)} %bitcast.47, s32[4,8]{1,0:T(4,128)} %bitcast.50), custom_call_target="tpu_custom_call" | custom-call | flops 3019898880 | bytes 610560 | tf_op jit(solution)/shard_map/first_strips/pallas_call | solution.py:464
  3.0 4.1 %collective-permute-start = (bf16[144,128]{1,0:T(8,128)(2,1)}, bf16[144,128]{1,0:T(8,128)(2,1)S(1)}, u32[]{:S(2)}, u32[]{:S(2)}) collective-permute-start(bf16[144,128]{1,0:T(8,128)(2,1)} %get-tuple-element.54), channel_id=1, source_target_pairs={{0,16},{1,17},{2,18},{3,19},{4,20},{5,21},{6,22},{7,23},{8,24},{9,... | collective-permute-start | bytes 110600 | tf_op jit(solution)/shard_map/ppermute | solution.py:487
  7.1 2.5 %collective-permute-start.2 = (bf16[64,128]{1,0:T(8,128)(2,1)}, bf16[64,128]{1,0:T(8,128)(2,1)S(1)}, u32[]{:S(2)}, u32[]{:S(2)}) collective-permute-start(bf16[64,128]{1,0:T(8,128)(2,1)} %get-tuple-element.55), channel_id=1, source_target_pairs={{0,12},{1,13},{2,14},{3,15},{4,8},{5,9},{6,10},{7,11},{8,4},{9,5},... | collective-permute-start | bytes 49160 | tf_op jit(solution)/shard_map/ppermute | solution.py:487
  9.7 0.7 %pad_maximum_fusion.6 = bf16[80,128]{1,0:T(8,128)(2,1)S(1)} fusion(bf16[16,128]{1,0:T(8,128)(2,1)S(1)} %slice.53, bf16[64,128]{1,0:T(8,128)(2,1)} %get-tuple-element.53), kind=kLoop, calls=%fused_computation.16 | loop fusion | flops 40960 | bytes 40960 | tf_op jit(solution)/shard_map/concatenate | solution.py:593
  10.4 1.8 %collective-permute-start.1 = (bf16[80,128]{1,0:T(8,128)(2,1)S(1)}, bf16[80,128]{1,0:T(8,128)(2,1)S(1)}, u32[]{:S(2)}, u32[]{:S(2)}) collective-permute-start(bf16[80,128]{1,0:T(8,128)(2,1)S(1)} %pad_maximum_fusion.6), channel_id=1, source_target_pairs={{0,4},{1,5},{2,6},{3,7},{4,0},{5,1},{6,2},{7,3},{8,12},{9,13},{10,... | collective-permute-start | bytes 61448 | tf_op jit(solution)/shard_map/ppermute | solution.py:487
  12.2 3.2 %inner_products.1 = (bf16[1024,128]{1,0:T(8,128)(2,1)S(1)}, bf16[1024,128]{1,0:T(8,128)(2,1)S(1)}, f32[128,128]{1,0:T(8,128)S(1)}, f32[128,128]{1,0:T(8,128)S(1)...) custom-call(s32[4,8]{1,0:T(4,128)S(1)} %bitcast.48, ...), custom_call_target="tpu_custom_call" | custom-call | flops 1207959552 | bytes 3621120 | tf_op jit(solution)/shard_map/inner_products/pallas_call | solution.py:464
  15.5 0.8 %collective-permute-done.3.refs_2_ = bf16[64,128]{1,0:T(8,128)(2,1)S(1)} collective-permute-done((bf16[64,128]{1,0:T(8,128)(2,1)}, bf16[64,128]{1,0:T(8,128)(2,1)S(1)}, u32[]{:S(2)}, u32[]{:S(2)}) %collective-permute-start.3) | collective-permute-done | bytes 16416 | tf_op jit(solution)/shard_map/ppermute | solution.py:487
  16.3 1.2 %gradients.1 = (f32[1152,128]{1,0:T(8,128)S(1)}, bf16[1152,128]{1,0:T(8,128)(2,1)S(1)}, bf16[128,128]{1,0:T(8,128)(2,1)S(1)}, bf16[128,128]{1,0:T(8,128)(2,1)S(1...) custom-call(f32[128,128]{1,0:T(8,128)S(1)} %get-tuple-element.46.preb_ref, ...), custom_call_target="tpu_custom_call" | custom-call | flops 75497472 | bytes 3682304 | tf_op jit(solution)/shard_map/gradients/pallas_call | solution.py:464
  17.5 0.1 collective-permute-start.4
  17.6 1.5 %collective-permute-done.4 = bf16[1152,128]{1,0:T(8,128)(2,1)S(1)} collective-permute-done((bf16[1152,128]{1,0:T(8,128)(2,1)S(1)}, bf16[1152,128]{1,0:T(8,128)(2,1)S(1)}, u32[]{:S(2)}, u32[]{:S(2)}) %collective-permute-start.4) | collective-permute-done | bytes 294944 | tf_op jit(solution)/shard_map/ppermute | solution.py:487
  19.2 0.1 fusion.4
  19.3 0.6 %collective-permute-start.7 = (bf16[432,128]{1,0:T(8,128)(2,1)S(1)}, bf16[432,128]{1,0:T(8,128)(2,1)S(1)}, u32[]{:S(2)}, u32[]{:S(2)}) collective-permute-start(bf16[432,128]{1,0:T(8,128)(2,1)S(1)} %pad_maximum_fusion.2), channel_id=1, source_target_pairs={{0,4},{1,5},{2,6},{3,7},{4,0},{5,1},{6,2},{7,3},{8,12},{9,13},{10,... | collective-permute-start | bytes 331784 | tf_op jit(solution)/shard_map/ppermute | solution.py:487
  19.8 2.5 %collective-permute-start.5 = (bf16[288,128]{1,0:T(8,128)(2,1)S(1)}, bf16[288,128]{1,0:T(8,128)(2,1)S(1)}, u32[]{:S(2)}, u32[]{:S(2)}) collective-permute-start(bf16[288,128]{1,0:T(8,128)(2,1)S(1)} %get-tuple-element.90), channel_id=1, source_target_pairs={{0,6},{1,7},{2,4},{3,5},{4,2},{5,3},{6,0},{7,1},{8,14},{9,15},{10,... | collective-permute-start | bytes 221192 | tf_op jit(solution)/shard_map/ppermute | solution.py:487
  22.3 0.5 %collective-permute-start.6 = (bf16[288,128]{1,0:T(8,128)(2,1)S(1)}, bf16[288,128]{1,0:T(8,128)(2,1)S(1)}, u32[]{:S(2)}, u32[]{:S(2)}) collective-permute-start(bf16[288,128]{1,0:T(8,128)(2,1)S(1)} %get-tuple-element.89), channel_id=1, source_target_pairs={{0,2},{1,3},{2,0},{3,1},{4,6},{5,7},{6,4},{7,5},{8,10},{9,11},{10,... | collective-permute-start | bytes 221192 | tf_op jit(solution)/shard_map/ppermute | solution.py:487
  22.8 4.3 %collective-permute-done.5 = bf16[288,128]{1,0:T(8,128)(2,1)S(1)} collective-permute-done((bf16[288,128]{1,0:T(8,128)(2,1)S(1)}, bf16[288,128]{1,0:T(8,128)(2,1)S(1)}, u32[]{:S(2)}, u32[]{:S(2)}) %collective-permute-start.5) | collective-permute-done | bytes 73760 | tf_op jit(solution)/shard_map/ppermute | solution.py:487
  27.1 0.6 %collective-permute-done.6 = bf16[288,128]{1,0:T(8,128)(2,1)S(1)} collective-permute-done((bf16[288,128]{1,0:T(8,128)(2,1)S(1)}, bf16[288,128]{1,0:T(8,128)(2,1)S(1)}, u32[]{:S(2)}, u32[]{:S(2)}) %collective-permute-start.6) | collective-permute-done | bytes 73760 | tf_op jit(solution)/shard_map/ppermute | solution.py:487
  27.6 0.1 fusion.1
  27.7 1.7 %collective-permute-start.9 = (bf16[432,128]{1,0:T(8,128)(2,1)S(1)}, bf16[432,128]{1,0:T(8,128)(2,1)S(1)}, u32[]{:S(2)}, u32[]{:S(2)}) collective-permute-start(bf16[432,128]{1,0:T(8,128)(2,1)S(1)} %pad_maximum_fusion.3), channel_id=1, source_target_pairs={{0,16},{1,17},{2,18},{3,19},{4,20},{5,21},{6,22},{7,23},{8,24},{9,... | collective-permute-start | bytes 331784 | tf_op jit(solution)/shard_map/ppermute | solution.py:487
  29.4 1.4 %collective-permute-start.10 = (bf16[352,128]{1,0:T(8,128)(2,1)S(1)}, bf16[352,128]{1,0:T(8,128)(2,1)S(1)}, u32[]{:S(2)}, u32[]{:S(2)}) collective-permute-start(bf16[352,128]{1,0:T(8,128)(2,1)S(1)} %get-tuple-element.96), channel_id=1, source_target_pairs={{0,24},{1,25},{2,26},{3,27},{4,28},{5,29},{6,30},{7,31},{8,16},{9,... | collective-permute-start | bytes 270344 | tf_op jit(solution)/shard_map/ppermute | solution.py:487
  30.8 0.6 %collective-permute-start.8 = (bf16[352,128]{1,0:T(8,128)(2,1)S(1)}, bf16[352,128]{1,0:T(8,128)(2,1)S(1)}, u32[]{:S(2)}, u32[]{:S(2)}) collective-permute-start(bf16[352,128]{1,0:T(8,128)(2,1)S(1)} %get-tuple-element.95), channel_id=1, source_target_pairs={{0,8},{1,9},{2,10},{3,11},{4,12},{5,13},{6,14},{7,15},{8,0},{9,1},... | collective-permute-start | bytes 270344 | tf_op jit(solution)/shard_map/ppermute | solution.py:487
  31.4 2.2 %later_products.1 = (f32[1024,128]{1,0:T(8,128)S(1)}, f32[1024,128]{1,0:T(8,128)S(1)}, bf16[1024,160]{1,0:T(8,128)(2,1)S(1)}, bf16[1024,128]{1,0:T(8,128)(2,1)S(1)}) custom-call(s32[4,8]{1,0:T(4,128)S(1)} %bitcast.49, s32[4,8]{1,0:T(4,128)S(1)} %bitcast.52, bf16[1024,128]{1,0:T(8,128)(2,1)S(1)} %bitcast.43, bf16[1024,128]{1,0:T(8,128)(2,1)S(1)} %bitcast.46, ...), custom_call_target="tpu_custom_call" | custom-call | flops 603979776 | bytes 3342592 | tf_op jit(solution)/shard_map/later_products/pallas_call | solution.py:464
  33.6 2.5 %collective-permute-done.10 = bf16[352,128]{1,0:T(8,128)(2,1)S(1)} collective-permute-done((bf16[352,128]{1,0:T(8,128)(2,1)S(1)}, bf16[352,128]{1,0:T(8,128)(2,1)S(1)}, u32[]{:S(2)}, u32[]{:S(2)}) %collective-permute-start.10) | collective-permute-done | bytes 90144 | tf_op jit(solution)/shard_map/ppermute | solution.py:487
  36.1 1.2 %collective-permute-done.8 = bf16[352,128]{1,0:T(8,128)(2,1)S(1)} collective-permute-done((bf16[352,128]{1,0:T(8,128)(2,1)S(1)}, bf16[352,128]{1,0:T(8,128)(2,1)S(1)}, u32[]{:S(2)}, u32[]{:S(2)}) %collective-permute-start.8) | collective-permute-done | bytes 90144 | tf_op jit(solution)/shard_map/ppermute | solution.py:487
  37.4 0.6 %collective-permute-start.11 = (bf16[288,128]{1,0:T(8,128)(2,1)S(1)}, bf16[288,128]{1,0:T(8,128)(2,1)S(1)}, u32[]{:S(2)}, u32[]{:S(2)}) collective-permute-start(bf16[288,128]{1,0:T(8,128)(2,1)S(1)} %add_add_fusion), channel_id=1, source_target_pairs={{0,2},{1,3},{2,0},{3,1},{4,6},{5,7},{6,4},{7,5},{8,10},{9,11},{10,... | collective-permute-start | bytes 221192 | tf_op jit(solution)/shard_map/ppermute | solution.py:487
  38.0 0.6 %collective-permute-start.12 = (bf16[288,128]{1,0:T(8,128)(2,1)S(1)}, bf16[288,128]{1,0:T(8,128)(2,1)S(1)}, u32[]{:S(2)}, u32[]{:S(2)}) collective-permute-start(bf16[288,128]{1,0:T(8,128)(2,1)S(1)} %add_add_fusion), channel_id=1, source_target_pairs={{0,4},{1,5},{2,6},{3,7},{4,0},{5,1},{6,2},{7,3},{8,12},{9,13},{10,... | collective-permute-start | bytes 221192 | tf_op jit(solution)/shard_map/ppermute | solution.py:487
  38.6 2.3 %collective-permute-start.13 = (bf16[288,128]{1,0:T(8,128)(2,1)S(1)}, bf16[288,128]{1,0:T(8,128)(2,1)S(1)}, u32[]{:S(2)}, u32[]{:S(2)}) collective-permute-start(bf16[288,128]{1,0:T(8,128)(2,1)S(1)} %add_add_fusion), channel_id=1, source_target_pairs={{0,6},{1,7},{2,4},{3,5},{4,2},{5,3},{6,0},{7,1},{8,14},{9,15},{10,... | collective-permute-start | bytes 221192 | tf_op jit(solution)/shard_map/ppermute | solution.py:487
  41.0 1.6 %outputs.1 = (bf16[1024,128]{1,0:T(8,128)(2,1)}, bf16[1024,128]{1,0:T(8,128)(2,1)}) custom-call(f32[1024,128]{1,0:T(8,128)S(1)} %get-tuple-element.75.part_ref, f32[1024,128]{1,0:T(8,128)S(1)} %get-tuple-element.76.dpart_ref, bf16[1024,160]{1,0:T(8,128)(2,1)S(1)} %get-tuple-element.77.scatter_ref, bf16[1024,128]{1,0:T(8,128)(2,1)S(1)} %get-tuple-element.78.column_ref, ...), custom_call_target="tpu_custom_call" | custom-call | flops 75497472 | bytes 2838528 | tf_op jit(solution)/shard_map/outputs/pallas_call | solution.py:464
  42.6 1.5 %collective-permute-done.13 = bf16[288,128]{1,0:T(8,128)(2,1)S(1)} collective-permute-done((bf16[288,128]{1,0:T(8,128)(2,1)S(1)}, bf16[288,128]{1,0:T(8,128)(2,1)S(1)}, u32[]{:S(2)}, u32[]{:S(2)}) %collective-permute-start.13) | collective-permute-done | bytes 73760 | tf_op jit(solution)/shard_map/ppermute | solution.py:487
  44.2 0.1 collective-permute-start.14
  44.3 0.9 %own_half.1 = (f32[1152,128]{1,0:T(8,128)}, f32[1152,128]{1,0:T(8,128)}) custom-call(bf16[1152,128]{1,0:T(8,128)(2,1)S(1)} %bitcast.38), custom_call_target="tpu_custom_call" | custom-call | flops 147456 | bytes 884736 | tf_op jit(solution)/shard_map/own_half/pallas_call | solution.py:574
  45.2 0.7 %collective-permute-done.14.value_ref = bf16[1152,128]{1,0:T(8,128)(2,1)S(1)} collective-permute-done((bf16[1152,128]{1,0:T(8,128)(2,1)S(1)}, bf16[1152,128]{1,0:T(8,128)(2,1)S(1)}, u32[]{:S(2)}, u32[]{:S(2)}) %collective-permute-start.14) | collective-permute-done | bytes 294944 | tf_op jit(solution)/shard_map/ppermute | solution.py:487
  45.9 0.9 %other_half.1 = (f32[1152,128]{1,0:T(8,128)}, f32[1152,128]{1,0:T(8,128)}) custom-call(bf16[1152,128]{1,0:T(8,128)(2,1)S(1)} %collective-permute-done.14.value_ref, f32[1152,128]{1,0:T(8,128)} %get-tuple-element.84.one_in, f32[1152,128]{1,0:T(8,128)} %get-tuple-element.85.two_in), custom_call_target="tpu_custom_call", output_to_operand_aliasing={{0}: (1, {}), {1}: (2, {})} | custom-call | flops 147456 | bytes 884736 | tf_op jit(solution)/shard_map/other_half/pallas_call | solution.py:574
  (37 shorter events, 0.3 us)
Async XLA Ops:
  0.6 11.6 %copy-start = (bf16[9,128,128]{2,1,0:T(8,128)(2,1)S(1)}, bf16[9,128,128]{2,1,0:T(8,128)(2,1)}, u32[]{:S(2)}) copy-start(bf16[9,128,128]{2,1,0:T(8,128)(2,1)} %param.7) | copy-start | bytes 884740
  0.6 11.6 %copy-start.1 = (bf16[9,128,128]{2,1,0:T(8,128)(2,1)S(1)}, bf16[9,128,128]{2,1,0:T(8,128)(2,1)}, u32[]{:S(2)}) copy-start(bf16[9,128,128]{2,1,0:T(8,128)(2,1)} %param.8) | copy-start | bytes 884740
  0.7 11.6 %copy-start.2 = (bf16[1,1,32,32,128]{4,3,2,1,0:T(8,128)(2,1)S(1)}, bf16[1,1,32,32,128]{4,3,2,1,0:T(8,128)(2,1)}, u32[]{:S(2)}) copy-start(bf16[1,1,32,32,128]{4,3,2,1,0:T(8,128)(2,1)} %param.6) | copy-start | bytes 786436
  0.7 11.6 %copy-start.3 = (bf16[1,1,32,32,128]{4,3,2,1,0:T(8,128)(2,1)S(1)}, bf16[1,1,32,32,128]{4,3,2,1,0:T(8,128)(2,1)}, u32[]{:S(2)}) copy-start(bf16[1,1,32,32,128]{4,3,2,1,0:T(8,128)(2,1)} %param.9) | copy-start | bytes 786436
  0.7 11.6 %copy-start.4 = (s32[8,4]{0,1:T(4,128)S(1)}, s32[8,4]{0,1:T(4,128)}, u32[]{:S(2)}) copy-start(s32[8,4]{0,1:T(4,128)} %param.10) | copy-start | bytes 388
  0.7 11.6 %copy-start.5 = (s32[8,4]{0,1:T(4,128)S(1)}, s32[8,4]{0,1:T(4,128)}, u32[]{:S(2)}) copy-start(s32[8,4]{0,1:T(4,128)} %param.11) | copy-start | bytes 388
  3.0 6.6 %collective-permute-start = (bf16[144,128]{1,0:T(8,128)(2,1)}, bf16[144,128]{1,0:T(8,128)(2,1)S(1)}, u32[]{:S(2)}, u32[]{:S(2)}) collective-permute-start(bf16[144,128]{1,0:T(8,128)(2,1)} %get-tuple-element.54), channel_id=1, source_target_pairs={{0,16},{1,17},{2,18},{3,19},{4,20},{5,21},{6,22},{7,23},{8,24},{9,... | collective-permute-start | bytes 110600 | tf_op jit(solution)/shard_map/ppermute | solution.py:487
  7.1 8.3 %collective-permute-start.2 = (bf16[64,128]{1,0:T(8,128)(2,1)}, bf16[64,128]{1,0:T(8,128)(2,1)S(1)}, u32[]{:S(2)}, u32[]{:S(2)}) collective-permute-start(bf16[64,128]{1,0:T(8,128)(2,1)} %get-tuple-element.55), channel_id=1, source_target_pairs={{0,12},{1,13},{2,14},{3,15},{4,8},{5,9},{6,10},{7,11},{8,4},{9,5},... | collective-permute-start | bytes 49160 | tf_op jit(solution)/shard_map/ppermute | solution.py:487
  9.6 6.6 %collective-permute-start.3 = (bf16[64,128]{1,0:T(8,128)(2,1)}, bf16[64,128]{1,0:T(8,128)(2,1)S(1)}, u32[]{:S(2)}, u32[]{:S(2)}) collective-permute-start(bf16[64,128]{1,0:T(8,128)(2,1)} %get-tuple-element.56), channel_id=1, source_target_pairs={{0,28},{1,29},{2,30},{3,31},{4,24},{5,25},{6,26},{7,27},{8,20},{9,... | collective-permute-start | bytes 49160 | tf_op jit(solution)/shard_map/ppermute | solution.py:487
  10.4 5.0 %collective-permute-start.1 = (bf16[80,128]{1,0:T(8,128)(2,1)S(1)}, bf16[80,128]{1,0:T(8,128)(2,1)S(1)}, u32[]{:S(2)}, u32[]{:S(2)}) collective-permute-start(bf16[80,128]{1,0:T(8,128)(2,1)S(1)} %pad_maximum_fusion.6), channel_id=1, source_target_pairs={{0,4},{1,5},{2,6},{3,7},{4,0},{5,1},{6,2},{7,3},{8,12},{9,13},{10,... | collective-permute-start | bytes 61448 | tf_op jit(solution)/shard_map/ppermute | solution.py:487
  17.5 1.6 %collective-permute-start.4 = (bf16[1152,128]{1,0:T(8,128)(2,1)S(1)}, bf16[1152,128]{1,0:T(8,128)(2,1)S(1)}, u32[]{:S(2)}, u32[]{:S(2)}) collective-permute-start(bf16[1152,128]{1,0:T(8,128)(2,1)S(1)} %get-tuple-element.58), channel_id=1, source_target_pairs={{0,1},{1,0},{2,3},{3,2},{4,5},{5,4},{6,7},{7,6},{8,9},{9,8},{10,11... | collective-permute-start | bytes 884744 | tf_op jit(solution)/shard_map/ppermute | solution.py:487
  19.3 8.4 %collective-permute-start.7 = (bf16[432,128]{1,0:T(8,128)(2,1)S(1)}, bf16[432,128]{1,0:T(8,128)(2,1)S(1)}, u32[]{:S(2)}, u32[]{:S(2)}) collective-permute-start(bf16[432,128]{1,0:T(8,128)(2,1)S(1)} %pad_maximum_fusion.2), channel_id=1, source_target_pairs={{0,4},{1,5},{2,6},{3,7},{4,0},{5,1},{6,2},{7,3},{8,12},{9,13},{10,... | collective-permute-start | bytes 331784 | tf_op jit(solution)/shard_map/ppermute | solution.py:487
  19.8 7.2 %collective-permute-start.5 = (bf16[288,128]{1,0:T(8,128)(2,1)S(1)}, bf16[288,128]{1,0:T(8,128)(2,1)S(1)}, u32[]{:S(2)}, u32[]{:S(2)}) collective-permute-start(bf16[288,128]{1,0:T(8,128)(2,1)S(1)} %get-tuple-element.90), channel_id=1, source_target_pairs={{0,6},{1,7},{2,4},{3,5},{4,2},{5,3},{6,0},{7,1},{8,14},{9,15},{10,... | collective-permute-start | bytes 221192 | tf_op jit(solution)/shard_map/ppermute | solution.py:487
  22.3 5.3 %collective-permute-start.6 = (bf16[288,128]{1,0:T(8,128)(2,1)S(1)}, bf16[288,128]{1,0:T(8,128)(2,1)S(1)}, u32[]{:S(2)}, u32[]{:S(2)}) collective-permute-start(bf16[288,128]{1,0:T(8,128)(2,1)S(1)} %get-tuple-element.89), channel_id=1, source_target_pairs={{0,2},{1,3},{2,0},{3,1},{4,6},{5,7},{6,4},{7,5},{8,10},{9,11},{10,... | collective-permute-start | bytes 221192 | tf_op jit(solution)/shard_map/ppermute | solution.py:487
  27.7 9.6 %collective-permute-start.9 = (bf16[432,128]{1,0:T(8,128)(2,1)S(1)}, bf16[432,128]{1,0:T(8,128)(2,1)S(1)}, u32[]{:S(2)}, u32[]{:S(2)}) collective-permute-start(bf16[432,128]{1,0:T(8,128)(2,1)S(1)} %pad_maximum_fusion.3), channel_id=1, source_target_pairs={{0,16},{1,17},{2,18},{3,19},{4,20},{5,21},{6,22},{7,23},{8,24},{9,... | collective-permute-start | bytes 331784 | tf_op jit(solution)/shard_map/ppermute | solution.py:487
  29.4 6.7 %collective-permute-start.10 = (bf16[352,128]{1,0:T(8,128)(2,1)S(1)}, bf16[352,128]{1,0:T(8,128)(2,1)S(1)}, u32[]{:S(2)}, u32[]{:S(2)}) collective-permute-start(bf16[352,128]{1,0:T(8,128)(2,1)S(1)} %get-tuple-element.96), channel_id=1, source_target_pairs={{0,24},{1,25},{2,26},{3,27},{4,28},{5,29},{6,30},{7,31},{8,16},{9,... | collective-permute-start | bytes 270344 | tf_op jit(solution)/shard_map/ppermute | solution.py:487
  30.8 6.6 %collective-permute-start.8 = (bf16[352,128]{1,0:T(8,128)(2,1)S(1)}, bf16[352,128]{1,0:T(8,128)(2,1)S(1)}, u32[]{:S(2)}, u32[]{:S(2)}) collective-permute-start(bf16[352,128]{1,0:T(8,128)(2,1)S(1)} %get-tuple-element.95), channel_id=1, source_target_pairs={{0,8},{1,9},{2,10},{3,11},{4,12},{5,13},{6,14},{7,15},{8,0},{9,1},... | collective-permute-start | bytes 270344 | tf_op jit(solution)/shard_map/ppermute | solution.py:487
  37.4 5.2 %collective-permute-start.11 = (bf16[288,128]{1,0:T(8,128)(2,1)S(1)}, bf16[288,128]{1,0:T(8,128)(2,1)S(1)}, u32[]{:S(2)}, u32[]{:S(2)}) collective-permute-start(bf16[288,128]{1,0:T(8,128)(2,1)S(1)} %add_add_fusion), channel_id=1, source_target_pairs={{0,2},{1,3},{2,0},{3,1},{4,6},{5,7},{6,4},{7,5},{8,10},{9,11},{10,... | collective-permute-start | bytes 221192 | tf_op jit(solution)/shard_map/ppermute | solution.py:487
  38.0 4.6 %collective-permute-start.12 = (bf16[288,128]{1,0:T(8,128)(2,1)S(1)}, bf16[288,128]{1,0:T(8,128)(2,1)S(1)}, u32[]{:S(2)}, u32[]{:S(2)}) collective-permute-start(bf16[288,128]{1,0:T(8,128)(2,1)S(1)} %add_add_fusion), channel_id=1, source_target_pairs={{0,4},{1,5},{2,6},{3,7},{4,0},{5,1},{6,2},{7,3},{8,12},{9,13},{10,... | collective-permute-start | bytes 221192 | tf_op jit(solution)/shard_map/ppermute | solution.py:487
  38.6 5.5 %collective-permute-start.13 = (bf16[288,128]{1,0:T(8,128)(2,1)S(1)}, bf16[288,128]{1,0:T(8,128)(2,1)S(1)}, u32[]{:S(2)}, u32[]{:S(2)}) collective-permute-start(bf16[288,128]{1,0:T(8,128)(2,1)S(1)} %add_add_fusion), channel_id=1, source_target_pairs={{0,6},{1,7},{2,4},{3,5},{4,2},{5,3},{6,0},{7,1},{8,14},{9,15},{10,... | collective-permute-start | bytes 221192 | tf_op jit(solution)/shard_map/ppermute | solution.py:487
  44.2 1.6 %collective-permute-start.14 = (bf16[1152,128]{1,0:T(8,128)(2,1)S(1)}, bf16[1152,128]{1,0:T(8,128)(2,1)S(1)}, u32[]{:S(2)}, u32[]{:S(2)}) collective-permute-start(bf16[1152,128]{1,0:T(8,128)(2,1)S(1)} %bitcast.37), channel_id=1, source_target_pairs={{0,1},{1,0},{2,3},{3,2},{4,5},{5,4},{6,7},{7,6},{8,9},{9,8},{10,11... | collective-permute-start | bytes 884744 | tf_op jit(solution)/shard_map/ppermute | solution.py:487
